TPU v7x, 32 devices: a whole 2x2x4 slice. The times are simulated.
32 devices in a mesh: dp: 16 (over z, y, x), fsdp: 2 (over core).
Axes of the slice: x: 2, y: 2, z: 4, core: 2. Of those that a mesh axis runs over, the one named last changes fastest.
Arguments:
- block_input: bfloat16 [32, 576, 1024], P(('dp', 'fsdp')), may hold values from -6 to 6
- cotangent: bfloat16 [32, 576, 1024], P(('dp', 'fsdp')), may hold values from -6 to 6
- seg_ids: int32 [32, 576], P(('dp', 'fsdp')), may hold values from 0 to 3, never falling along the last dimension, each value on 1 to 288 neighbouring positions
- slot_valid: int32 [32, 576], P(('dp', 'fsdp')), may hold values from 0 to 1, as said below
- rel_buckets: int32 [32, 3, 576, 576], P(('dp', 'fsdp')), may hold values from 0 to 127
- w_qkv: bfloat16 [1024, 3072], P(('dp', 'fsdp')), may hold values from -0.1875 to 0.1875
- w_out: bfloat16 [1024, 1024], P(('dp', 'fsdp')), may hold values from -1.5 to 1.5
- w_in: bfloat16 [1024, 4096], P(('dp', 'fsdp')), may hold values from -0.1875 to 0.1875
- w_down: bfloat16 [4096, 1024], P(('dp', 'fsdp')), may hold values from -0.09375 to 0.09375
- vec_bias: bfloat16 [6, 1024], P(None, ('dp', 'fsdp')), may hold values from -3 to 3
- norm_gain: bfloat16 [2, 1024], P(None, ('dp', 'fsdp')), may hold values from 0.25 to 1.75
- bias_hidden: bfloat16 [4096], P(('dp', 'fsdp')), may hold values from -3 to 3
- rel_tables: bfloat16 [6144], P(('dp', 'fsdp')), may hold values from -3 to 3
Outputs:
- block_output: bfloat16 [32, 576, 1024], P(('dp', 'fsdp'))
- grad_input: float32 [32, 576, 1024], P(('dp', 'fsdp'))
- grad_w_qkv: float32 [1024, 3072], P(('dp', 'fsdp'))
- grad_w_out: float32 [1024, 1024], P(('dp', 'fsdp'))
- grad_w_in: float32 [1024, 4096], P(('dp', 'fsdp'))
- grad_w_down: float32 [4096, 1024], P(('dp', 'fsdp'))
- grad_vec_bias: float32 [6, 1024], P(None, ('dp', 'fsdp'))
- grad_norm_gain: float32 [2, 1024], P(None, ('dp', 'fsdp'))
- grad_bias_hidden: float32 [4096], P(('dp', 'fsdp'))
- grad_rel_tables: float32 [6144], P(('dp', 'fsdp'))
Inputs may be any that keep to these rules, and one draw needn't show every extreme that they name: `seg_ids`: document numbers never fall along a row; a document holds 1 to 288 slots. `slot_valid`: in each row the used slots come first and number at least 432; row 0 is full.
All inputs are finite; a program needn't handle non-finite values.
Results may differ from a plain program's by a relative error of at most 0.013.
The roundings to bfloat16 on the way count: a program that leaves them out, or rounds other values in their place, can miss the bound.
Values may be sent and summed in bfloat16 or wider, within the bound.
A program may use at most 192 MiB of HBM per device.

v0:
```python
import jax
import jax.numpy as jnp
from jax import lax
from jax.sharding import PartitionSpec as P

H = 16
NB = 128


EPSILON = 1e-05
MASK_FILL = -1e30


def layer_norm(inputs, gain_row, shift_row):
    average = jnp.mean(inputs, axis=-1, keepdims=True)
    centered = inputs - average
    variance = jnp.mean(centered * centered, axis=-1, keepdims=True)
    return centered * lax.rsqrt(variance + EPSILON) * gain_row + shift_row


def gelu_exact(inputs):
    return jax.nn.gelu(inputs, approximate=False)


def dot_first(left, right):
    return lax.dot_general(
        left, right, (((0,), (0,)), ((), ())), preferred_element_type=jnp.float32
    )


def dot_last(left, right):
    return lax.dot_general(
        left, right, (((1,), (1,)), ((), ())), preferred_element_type=jnp.float32
    )


def query_blocks(length):
    return (length // 3, 3)


def spatial_bias(buckets, tables):
    length = buckets.shape[1]
    block_rows, block_count = query_blocks(length)
    levels = jnp.arange(tables.shape[1], dtype=jnp.int32)
    blocked = jnp.moveaxis(buckets.reshape(3, block_count, block_rows, length), 1, 0)

    def spatial_one_block(bucket_block):
        running = jnp.zeros((tables.shape[2], block_rows, length), jnp.float32)
        for table_index in range(3):
            onehot = (bucket_block[table_index][:, :, None] == levels).astype(jnp.bfloat16)
            running = running + jnp.einsum(
                "qkb,bh->hqk", onehot, tables[table_index], preferred_element_type=jnp.float32
            )
        return running

    pieces = lax.map(spatial_one_block, blocked)
    return jnp.moveaxis(pieces, 0, 1).reshape(tables.shape[2], length, length)


def table_grads(buckets, score_grad, bucket_total):
    length = buckets.shape[1]
    head_count = score_grad.shape[0]
    block_rows, block_count = query_blocks(length)
    levels = jnp.arange(bucket_total, dtype=jnp.int32)
    blocked = jnp.moveaxis(buckets.reshape(3, block_count, block_rows, length), 1, 0)
    grad_blocks = jnp.moveaxis(
        score_grad.reshape(head_count, block_count, block_rows, length), 1, 0
    )

    def table_one_block(running, inputs):
        bucket_block, grad_block = inputs
        per_table = []
        for table_index in range(3):
            onehot = (bucket_block[table_index][:, :, None] == levels).astype(jnp.bfloat16)
            per_table.append(
                jnp.einsum("qkb,hqk->bh", onehot, grad_block, preferred_element_type=jnp.float32)
            )
        return (running + jnp.stack(per_table), None)

    initial = jnp.zeros((3, bucket_total, head_count), jnp.float32)
    result, unused = lax.scan(table_one_block, initial, (blocked, grad_blocks))
    return result


def attention_forward(row_in, segments, validity, buckets, attn_full):
    full_qkv, full_out, vectors, gains, flat_tables = attn_full
    tables = flat_tables.reshape(3, NB, H)
    length, model_width = row_in.shape
    head_count = tables.shape[2]
    head_size = model_width // head_count
    scale = head_size ** (-0.5)
    mixed = jnp.dot(row_in, full_qkv, preferred_element_type=jnp.float32)
    queries = (
        (mixed[:, :model_width] + vectors[0])
        .astype(jnp.bfloat16)
        .reshape(length, head_count, head_size)
    )
    key_rows = (
        mixed[:, model_width : 2 * model_width]
        .astype(jnp.bfloat16)
        .reshape(length, head_count, head_size)
    )
    value_rows = (
        (mixed[:, 2 * model_width :] + vectors[1])
        .astype(jnp.bfloat16)
        .reshape(length, head_count, head_size)
    )
    spatial = spatial_bias(buckets, tables)
    position = jnp.arange(length)
    allowed = (segments[:, None] == segments[None, :]) & (
        (validity[None, :] > 0) | (position[:, None] == position[None, :])
    )
    raw_scores = (
        jnp.einsum("qhd,khd->hqk", queries, key_rows, preferred_element_type=jnp.float32) * scale
        + spatial
    )
    masked = jnp.where(allowed[None], raw_scores, MASK_FILL)
    top_score = jnp.max(masked, axis=-1, keepdims=True)
    exponent = jnp.exp(masked - top_score)
    row_total = jnp.sum(exponent, axis=-1, keepdims=True)
    probability = exponent / row_total
    log_total = top_score + jnp.log(row_total)
    context = (
        jnp.einsum(
            "hqk,khd->qhd",
            probability.astype(jnp.bfloat16),
            value_rows,
            preferred_element_type=jnp.float32,
        )
        .reshape(length, model_width)
        .astype(jnp.bfloat16)
    )
    branch = jnp.dot(context, full_out, preferred_element_type=jnp.float32) + vectors[2]
    first_sum = row_in.astype(jnp.float32) + branch
    normed_first = layer_norm(
        first_sum, gains[0].astype(jnp.float32), vectors[4].astype(jnp.float32)
    )
    return (
        (queries, key_rows, value_rows, spatial, allowed, log_total, context, first_sum),
        normed_first,
    )


def ffn_forward(normed_first, ffn_full, vectors, gains):
    full_in, full_down, hidden_bias = ffn_full
    first_low = normed_first.astype(jnp.bfloat16)
    hidden = jnp.dot(first_low, full_in, preferred_element_type=jnp.float32) + hidden_bias
    active = gelu_exact(hidden).astype(jnp.bfloat16)
    down_out = jnp.dot(active, full_down, preferred_element_type=jnp.float32) + vectors[3]
    second_sum = normed_first + down_out
    output = layer_norm(second_sum, gains[1].astype(jnp.float32), vectors[5].astype(jnp.float32))
    return ((first_low, hidden, active, second_sum), output.astype(jnp.bfloat16))


def ffn_backward(kept, row_cot, ffn_full, vectors, gains):
    first_low, hidden, active, second_sum = kept
    full_in, full_down, hidden_bias = ffn_full
    unused, norm_back = jax.vjp(
        layer_norm, second_sum, gains[1].astype(jnp.float32), vectors[5].astype(jnp.float32)
    )
    grad_second, grad_gain, grad_shift = norm_back(row_cot.astype(jnp.float32))
    down_grad = grad_second.astype(jnp.bfloat16)
    grad_w_down = dot_first(active, down_grad)
    grad_active = dot_last(down_grad, full_down)
    unused_gelu, gelu_back = jax.vjp(gelu_exact, hidden)
    hidden_grad = gelu_back(grad_active)[0].astype(jnp.bfloat16)
    grad_w_in = dot_first(first_low, hidden_grad)
    grad_first = dot_last(hidden_grad, full_in) + grad_second
    grads = (
        grad_w_in,
        grad_w_down,
        jnp.sum(hidden_grad.astype(jnp.float32), axis=0),
        jnp.sum(down_grad.astype(jnp.float32), axis=0),
        grad_gain,
        grad_shift,
    )
    return (grads, grad_first)


def attention_backward(kept, grad_first, row_in, buckets, attn_full):
    queries, key_rows, value_rows, spatial, allowed, log_total, context, first_sum = kept
    full_qkv, full_out, vectors, gains, flat_tables = attn_full
    length, model_width = row_in.shape
    head_count = queries.shape[1]
    head_size = queries.shape[2]
    scale = head_size ** (-0.5)
    unused, norm_back = jax.vjp(
        layer_norm, first_sum, gains[0].astype(jnp.float32), vectors[4].astype(jnp.float32)
    )
    grad_first_sum, grad_gain, grad_shift = norm_back(grad_first)
    branch_grad = grad_first_sum.astype(jnp.bfloat16)
    grad_w_out = dot_first(context, branch_grad)
    context_grad = (
        dot_last(branch_grad, full_out).astype(jnp.bfloat16).reshape(length, head_count, head_size)
    )
    raw_scores = (
        jnp.einsum("qhd,khd->hqk", queries, key_rows, preferred_element_type=jnp.float32) * scale
        + spatial
    )
    masked = jnp.where(allowed[None], raw_scores, MASK_FILL)
    probability = jnp.exp(masked - log_total)
    grad_probs = jnp.einsum(
        "qhd,khd->hqk", context_grad, value_rows, preferred_element_type=jnp.float32
    )
    grad_values = jnp.einsum(
        "hqk,qhd->khd",
        probability.astype(jnp.bfloat16),
        context_grad,
        preferred_element_type=jnp.float32,
    ).astype(jnp.bfloat16)
    inner = jnp.sum(grad_probs * probability, axis=-1, keepdims=True)
    score_grad = (probability * (grad_probs - inner)).astype(jnp.bfloat16)
    grad_queries = (
        jnp.einsum("hqk,khd->qhd", score_grad, key_rows, preferred_element_type=jnp.float32) * scale
    ).astype(jnp.bfloat16)
    grad_keys = (
        jnp.einsum("hqk,qhd->khd", score_grad, queries, preferred_element_type=jnp.float32) * scale
    ).astype(jnp.bfloat16)
    grad_mixed = jnp.concatenate(
        [
            grad_queries.reshape(length, model_width),
            grad_keys.reshape(length, model_width),
            grad_values.reshape(length, model_width),
        ],
        axis=1,
    )
    grad_w_qkv = dot_first(row_in, grad_mixed)
    grad_row_input = grad_first_sum + dot_last(grad_mixed, full_qkv)
    grad_tables = table_grads(buckets, score_grad, NB)
    grads = (
        grad_w_qkv,
        grad_w_out,
        jnp.sum(grad_mixed[:, :model_width].astype(jnp.float32), axis=0),
        jnp.sum(grad_mixed[:, 2 * model_width :].astype(jnp.float32), axis=0),
        jnp.sum(branch_grad.astype(jnp.float32), axis=0),
        grad_gain,
        grad_shift,
        grad_tables,
    )
    return (grads, grad_row_input)


def body(
    block_input,
    cotangent,
    seg_ids,
    slot_valid,
    rel_buckets,
    w_qkv,
    w_out,
    w_in,
    w_down,
    vec_bias,
    norm_gain,
    bias_hidden,
    rel_tables,
):
    attn_full = (
        lax.all_gather(w_qkv, ("dp", "fsdp"), axis=0, tiled=True),
        lax.all_gather(w_out, ("dp", "fsdp"), axis=0, tiled=True),
        lax.all_gather(vec_bias, ("dp", "fsdp"), axis=1, tiled=True),
        lax.all_gather(norm_gain, ("dp", "fsdp"), axis=1, tiled=True),
        lax.all_gather(rel_tables, ("dp", "fsdp"), axis=0, tiled=True),
    )
    ffn_full = (
        lax.all_gather(w_in, ("dp", "fsdp"), axis=0, tiled=True),
        lax.all_gather(w_down, ("dp", "fsdp"), axis=0, tiled=True),
        lax.all_gather(bias_hidden, ("dp", "fsdp"), axis=0, tiled=True),
    )
    vectors = attn_full[2]
    gains = attn_full[3]
    row_index = 0
    kept_row, normed_first = attention_forward(
        block_input[row_index],
        seg_ids[row_index],
        slot_valid[row_index],
        rel_buckets[row_index],
        attn_full,
    )
    ffn_row, output = ffn_forward(normed_first, ffn_full, vectors, gains)
    attn_kept = [kept_row]
    ffn_kept = [ffn_row]
    output_rows = [output]
    ffn_back = (
        lax.all_gather(w_in, ("dp", "fsdp"), axis=0, tiled=True),
        lax.all_gather(w_down, ("dp", "fsdp"), axis=0, tiled=True),
        lax.all_gather(bias_hidden, ("dp", "fsdp"), axis=0, tiled=True),
    )
    ffn_totals = None
    row_index = 0
    row_grads, grad_first = ffn_backward(
        ffn_kept[row_index], cotangent[row_index], ffn_back, vectors, gains
    )
    ffn_totals = row_grads
    first_grads = [grad_first]
    grad_w_in, grad_w_down, grad_hidden_bias, grad_down_bias, grad_gain_two, grad_shift_two = (
        ffn_totals
    )
    attn_back = (
        lax.all_gather(w_qkv, ("dp", "fsdp"), axis=0, tiled=True),
        lax.all_gather(w_out, ("dp", "fsdp"), axis=0, tiled=True),
        lax.all_gather(vec_bias, ("dp", "fsdp"), axis=1, tiled=True),
        lax.all_gather(norm_gain, ("dp", "fsdp"), axis=1, tiled=True),
        lax.all_gather(rel_tables, ("dp", "fsdp"), axis=0, tiled=True),
    )
    row_index = 0
    row_grads, grad_row_input = attention_backward(
        attn_kept[row_index],
        first_grads[row_index],
        block_input[row_index],
        rel_buckets[row_index],
        attn_back,
    )
    input_grads = [grad_row_input]
    (
        grad_w_qkv,
        grad_w_out,
        grad_query_bias,
        grad_value_bias,
        grad_out_bias,
        grad_gain_one,
        grad_shift_one,
        grad_tables,
    ) = row_grads
    grad_vectors = jnp.stack(
        [
            grad_query_bias,
            grad_value_bias,
            grad_out_bias,
            grad_down_bias,
            grad_shift_one,
            grad_shift_two,
        ]
    )
    grad_gains = jnp.stack([grad_gain_one, grad_gain_two])
    flat_table_grads = grad_tables.reshape(-1)
    all_shards = (
        lax.psum_scatter(grad_w_qkv, ("dp", "fsdp"), scatter_dimension=0, tiled=True),
        lax.psum_scatter(grad_w_out, ("dp", "fsdp"), scatter_dimension=0, tiled=True),
        lax.psum_scatter(grad_vectors, ("dp", "fsdp"), scatter_dimension=1, tiled=True),
        lax.psum_scatter(grad_gains, ("dp", "fsdp"), scatter_dimension=1, tiled=True),
        lax.psum_scatter(flat_table_grads, ("dp", "fsdp"), scatter_dimension=0, tiled=True),
        lax.psum_scatter(grad_w_in, ("dp", "fsdp"), scatter_dimension=0, tiled=True),
        lax.psum_scatter(grad_w_down, ("dp", "fsdp"), scatter_dimension=0, tiled=True),
        lax.psum_scatter(grad_hidden_bias, ("dp", "fsdp"), scatter_dimension=0, tiled=True),
    )
    (
        shard_w_qkv,
        shard_w_out,
        shard_vectors,
        shard_gains,
        shard_tables,
        shard_w_in,
        shard_w_down,
        shard_hidden_bias,
    ) = all_shards
    return (
        jnp.stack(output_rows),
        jnp.stack(input_grads),
        shard_w_qkv,
        shard_w_out,
        shard_w_in,
        shard_w_down,
        shard_vectors,
        shard_gains,
        shard_hidden_bias,
        shard_tables,
    )


def solution(mesh):
    in_specs = (
        P(("dp", "fsdp"), None, None),
        P(("dp", "fsdp"), None, None),
        P(("dp", "fsdp"), None),
        P(("dp", "fsdp"), None),
        P(("dp", "fsdp"), None, None, None),
        P(("dp", "fsdp"), None),
        P(("dp", "fsdp"), None),
        P(("dp", "fsdp"), None),
        P(("dp", "fsdp"), None),
        P(None, ("dp", "fsdp")),
        P(None, ("dp", "fsdp")),
        P(("dp", "fsdp")),
        P(("dp", "fsdp")),
    )
    out_specs = (
        P(("dp", "fsdp"), None, None),
        P(("dp", "fsdp"), None, None),
        P(("dp", "fsdp"), None),
        P(("dp", "fsdp"), None),
        P(("dp", "fsdp"), None),
        P(("dp", "fsdp"), None),
        P(None, ("dp", "fsdp")),
        P(None, ("dp", "fsdp")),
        P(("dp", "fsdp")),
        P(("dp", "fsdp")),
    )
    return jax.shard_map(body, mesh=mesh, in_specs=in_specs, out_specs=out_specs, check_vma=False)
```

profile of v0, /device:TPU:0, one launch (start us, length us, event | category | flops | bytes accessed | tf_op | source)
XLA Modules:
  0.0 1566.3 jit_solution(10269172568966203389)
XLA Ops:
  10.0 44.0 %all-gather = bf16[32,32,6]{1,2,0:T(8,128)(2,1)S(1)} all-gather(bf16[1,32,6]{1,2,0:T(8,128)(2,1)} %bitcast.267), channel_id=1, replica_groups=mesh['dp'=16,'fsdp'=2] {'dp','fsdp'}, dimensions={0}, use_global_device_ids=true | all-gather | bytes 12672 | tf_op jit(solution)/shard_map/all_gather | solution.py:261
  54.8 37.0 %all-gather.2 = bf16[32,1,128]{2,1,0:T(2,128)(2,1)S(1)} all-gather(bf16[1,1,128]{2,1,0:T(2,128)(2,1)} %bitcast.268), channel_id=1, replica_groups=mesh['dp'=16,'fsdp'=2] {'dp','fsdp'}, dimensions={0}, use_global_device_ids=true | all-gather | bytes 8448 | tf_op jit(solution)/shard_map/all_gather | solution.py:268
  97.2 37.2 %all-reduce = bf16[6144]{0:T(1024)(128)(2,1)S(1)} all-reduce(bf16[6144]{0:T(1024)(128)(2,1)S(1)} %dynamic-update-slice), channel_id=1, replica_groups=mesh['dp'=16,'fsdp'=2] {'dp','fsdp'}, use_global_device_ids=true, to_apply=%add | all-reduce | flops 6144 | bytes 24576
  134.7 249.3 %while.24 = (s32[]{:T(128)}, f32[3,16,192,576]{3,1,2,0:T(8,128)}, s32[3,3,192,576]{3,2,1,0:T(8,128)}, bf16[3,128,16]{1,2,0:T(8,128)(2,1)S(1)}, s32[]{:T(128)}, /*index=5*/s32[]{:T(128)}, s32[]{}, s32[]{}) while((s32[]{:T(128)}, f32[3,16,192,576]{3,1,2,0:T(8,128)}, s32[3,3,192,576]{3,2,1,0:T(8,128)}, ...), condition=%wide.region_1.2_spmd.clone.clone, body=%wide.region_0.1_spmd.clone.clone.sunk | while | flops 1404960768 | bytes 41889924 | solution.py:56
  190.0 27.8 %bitcast_dynamic-update-slice_fusion.2 = f32[3,16,192,576]{3,1,2,0:T(8,128)} fusion(f32[3,16,192,576]{3,1,2,0:T(8,128)} %get-tuple-element.316, s32[]{:T(128)S(6)} %copy.72, f32[192,576,16]{1,2,0:T(8,128)S(1)} %fusion.154, f32[192,576,16]{1,2,0:T(8,128)S(1)} %fusion.155, s32[192,576]{1,0:T(8,128)S(1)} %get-tuple-element.299, ...), kind=kOutput, calls=%fused_computation.11.clone.3 | convolution fusion | flops 470679552 | bytes 24088580 | tf_op jit(solution)/shard_map/while/body/eval_jaxpr/qkb,bh->hqk/dot_general | solution.py:51
  219.2 26.9 %fusion.154 = f32[192,576,16]{1,2,0:T(8,128)S(1)} fusion(s32[192,576]{1,0:T(8,128)S(1)} %get-tuple-element.297, bf16[3,128,16]{1,2,0:T(8,128)(2,1)S(1)} %get-tuple-element.326), kind=kOutput, calls=%fused_computation.5.clone.3 | convolution fusion | flops 467140608 | bytes 7573504 | tf_op jit(solution)/shard_map/while/body/eval_jaxpr/qkb,bh->hqk/dot_general | solution.py:51
  273.1 27.8 %bitcast_dynamic-update-slice_fusion.2 = f32[3,16,192,576]{3,1,2,0:T(8,128)} fusion(f32[3,16,192,576]{3,1,2,0:T(8,128)} %get-tuple-element.316, s32[]{:T(128)S(6)} %copy.72, f32[192,576,16]{1,2,0:T(8,128)S(1)} %fusion.154, f32[192,576,16]{1,2,0:T(8,128)S(1)} %fusion.155, s32[192,576]{1,0:T(8,128)S(1)} %get-tuple-element.299, ...), kind=kOutput, calls=%fused_computation.11.clone.3 | convolution fusion | flops 470679552 | bytes 24088580 | tf_op jit(solution)/shard_map/while/body/eval_jaxpr/qkb,bh->hqk/dot_general | solution.py:51
  356.1 27.8 %bitcast_dynamic-update-slice_fusion.2 = f32[3,16,192,576]{3,1,2,0:T(8,128)} fusion(f32[3,16,192,576]{3,1,2,0:T(8,128)} %get-tuple-element.316, s32[]{:T(128)S(6)} %copy.72, f32[192,576,16]{1,2,0:T(8,128)S(1)} %fusion.154, f32[192,576,16]{1,2,0:T(8,128)S(1)} %fusion.155, s32[192,576]{1,0:T(8,128)S(1)} %get-tuple-element.299, ...), kind=kOutput, calls=%fused_computation.11.clone.3 | convolution fusion | flops 470679552 | bytes 24088580 | tf_op jit(solution)/shard_map/while/body/eval_jaxpr/qkb,bh->hqk/dot_general | solution.py:51
  404.2 41.1 %all-gather.1 = bf16[32,32,2]{1,2,0:T(2,128)(2,1)S(1)} all-gather(bf16[1,32,2]{1,2,0:T(2,128)(2,1)S(1)} %bitcast.269), channel_id=1, replica_groups=mesh['dp'=16,'fsdp'=2] {'dp','fsdp'}, dimensions={0}, use_global_device_ids=true | all-gather | bytes 4224 | tf_op jit(solution)/shard_map/all_gather | solution.py:262
  514.3 30.5 %multiply_convert_fusion.1 = (bf16[576,4096]{1,0:T(8,128)(2,1)}, f32[576,4096]{1,0:T(8,128)}, f32[576,4096]{1,0:T(8,128)}) fusion(f32[4096]{0:T(1024)S(1)} %bitcast.260, bf16[1024,4096]{1,0:T(8,128)(2,1)} %all-gather.12.cloned.1.call-done, f32[576,1024]{1,0:T(8,128)S(1)} %get-tuple-element.234, f32[1024]{0:T(1024)S(1)} %bitcast.245, ...), kind=kOutput, calls=%fused_computation.65 | convolution fusion | flops 4990500864 | bytes 34370048 | tf_op jit(solution)/shard_map/dot_general | solution.py:147
  746.8 313.4 %while.25 = (s32[]{:T(128)}, f32[3,128,16]{1,2,0:T(8,128)S(1)}, s32[3,3,192,576]{3,2,1,0:T(8,128)}, bf16[3,16,192,576]{3,1,2,0:T(8,128)(2,1)}, s32[]{:T(128)}, /*index=5*/s32[]{:T(128)}, s32[]{}, s32[]{}) while((s32[]{:T(128)}, f32[3,128,16]{1,2,0:T(8,128)S(1)}, s32[3,3,192,576]{3,2,1,0:T(8,128)}, ...), condition=%wide.region_30.31_spmd.clone.clone, body=%wide.region_29.30_spmd.clone.clone.sunk | while | flops 1401446400 | bytes 71319776 | solution.py:81
  751.1 33.2 %fusion.160 = f32[1,128,16]{1,2,0:T(8,128)S(1)} fusion(s32[192,576]{1,0:T(8,128)S(1)} %get-tuple-element.304, bf16[16,192,576]{2,0,1:T(8,128)(2,1)S(1)} %fusion.159), kind=kOutput, calls=%fused_computation.36.clone.3 | convolution fusion | flops 467140608 | bytes 3989504 | tf_op jit(solution)/shard_map/while/body/eval_jaxpr/qkb,hqk->bh/dot_general | solution.py:76
  784.7 33.2 %fusion.162 = f32[1,128,16]{1,2,0:T(8,128)S(1)} fusion(s32[192,576]{1,0:T(8,128)S(1)} %get-tuple-element.305, bf16[16,192,576]{2,0,1:T(8,128)(2,1)S(1)} %fusion.161), kind=kOutput, calls=%fused_computation.37.clone.1 | convolution fusion | flops 467140608 | bytes 3989504 | tf_op jit(solution)/shard_map/while/body/eval_jaxpr/qkb,hqk->bh/dot_general | solution.py:76
  818.2 33.2 %fusion.164 = f32[1,128,16]{1,2,0:T(8,128)S(1)} fusion(s32[192,576]{1,0:T(8,128)S(1)} %get-tuple-element.306, bf16[16,192,576]{2,0,1:T(8,128)(2,1)S(1)} %fusion.163), kind=kOutput, calls=%fused_computation.38.clone.1 | convolution fusion | flops 467140608 | bytes 3989504 | tf_op jit(solution)/shard_map/while/body/eval_jaxpr/qkb,hqk->bh/dot_general | solution.py:76
  855.5 33.2 %fusion.160 = f32[1,128,16]{1,2,0:T(8,128)S(1)} fusion(s32[192,576]{1,0:T(8,128)S(1)} %get-tuple-element.304, bf16[16,192,576]{2,0,1:T(8,128)(2,1)S(1)} %fusion.159), kind=kOutput, calls=%fused_computation.36.clone.3 | convolution fusion | flops 467140608 | bytes 3989504 | tf_op jit(solution)/shard_map/while/body/eval_jaxpr/qkb,hqk->bh/dot_general | solution.py:76
  889.1 33.2 %fusion.162 = f32[1,128,16]{1,2,0:T(8,128)S(1)} fusion(s32[192,576]{1,0:T(8,128)S(1)} %get-tuple-element.305, bf16[16,192,576]{2,0,1:T(8,128)(2,1)S(1)} %fusion.161), kind=kOutput, calls=%fused_computation.37.clone.1 | convolution fusion | flops 467140608 | bytes 3989504 | tf_op jit(solution)/shard_map/while/body/eval_jaxpr/qkb,hqk->bh/dot_general | solution.py:76
  922.6 33.2 %fusion.164 = f32[1,128,16]{1,2,0:T(8,128)S(1)} fusion(s32[192,576]{1,0:T(8,128)S(1)} %get-tuple-element.306, bf16[16,192,576]{2,0,1:T(8,128)(2,1)S(1)} %fusion.163), kind=kOutput, calls=%fused_computation.38.clone.1 | convolution fusion | flops 467140608 | bytes 3989504 | tf_op jit(solution)/shard_map/while/body/eval_jaxpr/qkb,hqk->bh/dot_general | solution.py:76
  959.9 33.2 %fusion.160 = f32[1,128,16]{1,2,0:T(8,128)S(1)} fusion(s32[192,576]{1,0:T(8,128)S(1)} %get-tuple-element.304, bf16[16,192,576]{2,0,1:T(8,128)(2,1)S(1)} %fusion.159), kind=kOutput, calls=%fused_computation.36.clone.3 | convolution fusion | flops 467140608 | bytes 3989504 | tf_op jit(solution)/shard_map/while/body/eval_jaxpr/qkb,hqk->bh/dot_general | solution.py:76
  993.5 33.2 %fusion.162 = f32[1,128,16]{1,2,0:T(8,128)S(1)} fusion(s32[192,576]{1,0:T(8,128)S(1)} %get-tuple-element.305, bf16[16,192,576]{2,0,1:T(8,128)(2,1)S(1)} %fusion.161), kind=kOutput, calls=%fused_computation.37.clone.1 | convolution fusion | flops 467140608 | bytes 3989504 | tf_op jit(solution)/shard_map/while/body/eval_jaxpr/qkb,hqk->bh/dot_general | solution.py:76
  1027.0 33.2 %fusion.164 = f32[1,128,16]{1,2,0:T(8,128)S(1)} fusion(s32[192,576]{1,0:T(8,128)S(1)} %get-tuple-element.306, bf16[16,192,576]{2,0,1:T(8,128)(2,1)S(1)} %fusion.163), kind=kOutput, calls=%fused_computation.38.clone.1 | convolution fusion | flops 467140608 | bytes 3989504 | tf_op jit(solution)/shard_map/while/body/eval_jaxpr/qkb,hqk->bh/dot_general | solution.py:76
  1060.5 37.9 %all-reduce.3 = (f32[4096]{0:T(1024)S(1)}, f32[6144]{0:T(1024)S(1)}) all-reduce(f32[4096]{0:T(1024)S(1)} %copy-done.20, f32[6144]{0:T(1024)S(1)} %reshape.234), channel_id=8, replica_groups=mesh['dp'=16,'fsdp'=2] {'dp','fsdp'}, use_global_device_ids=true, to_apply=%region_28.29.clone | all-reduce | flops 10240 | bytes 81920
  1112.3 74.5 %reduce-scatter.19.cloned.1.call-done = f32[32,3072]{1,0:T(8,128)} async-done(((f32[1024,3072]{1,0:T(8,128)}), f32[32,3072]{1,0:T(8,128)}) %reduce-scatter.19.cloned.1.call-update) | async-done | bytes 393232
  1186.8 184.8 %reduce-scatter.15.cloned.1.call-done = f32[32,4096]{1,0:T(8,128)} async-done(((f32[1024,4096]{1,0:T(8,128)}), f32[32,4096]{1,0:T(8,128)}) %reduce-scatter.15.cloned.1.call-update) | async-done | bytes 524304 | tf_op jit(solution)/shard_map/reduce_scatter | solution.py:343
  1371.6 187.3 %reduce-scatter.17.cloned.1.call-done = f32[128,1024]{1,0:T(8,128)} async-done(((f32[4096,1024]{1,0:T(8,128)}), f32[128,1024]{1,0:T(8,128)}) %reduce-scatter.17.cloned.1.call-update) | async-done | bytes 524304 | tf_op jit(solution)/shard_map/reduce_scatter | solution.py:344
  (210 shorter events, 467.3 us)
Async XLA Ops:
  7.2 440.0 %all-gather.8.cloned.1.call-start = ((), (), s32[]{:S(2)}) async-start(), calls=%async_computation.6 | async-start | bytes 6488064 | tf_op jit(solution)/shard_map/all_gather | solution.py:259
  7.9 502.0 %all-gather.10.cloned.1.call-start = ((), (), s32[]{:S(2)}) async-start(), calls=%async_computation.7 | async-start | bytes 2162688 | tf_op jit(solution)/shard_map/all_gather | solution.py:260
  8.7 505.6 %all-gather.12.cloned.1.call-start = ((), (), s32[]{:S(2)}) async-start(), calls=%async_computation.8 | async-start | bytes 8650752 | tf_op jit(solution)/shard_map/all_gather | solution.py:266
  9.4 87.6 %copy-start.30 = (bf16[192]{0:T(256)(128)(2,1)S(1)}, bf16[192]{0:T(256)(128)(2,1)}, u32[]{:S(2)}) copy-start(bf16[192]{0:T(256)(128)(2,1)} %param.29) | copy-start | bytes 1156
  9.4 535.4 %all-gather.14.cloned.1.call-start = ((), (), s32[]{:S(2)}) async-start(), calls=%async_computation.9 | async-start | bytes 8650752 | tf_op jit(solution)/shard_map/all_gather | solution.py:267
  10.0 1099.6 %reduce-scatter.23.cloned.1.call-start = ((), (), s32[]{:S(2)}) async-start(), calls=%async_computation.15 | async-start | bytes 540672
  384.0 62.1 %copy-start.4 = (bf16[1,576,1024]{2,1,0:T(8,128)(2,1)S(1)}, bf16[1,576,1024]{2,1,0:T(8,128)(2,1)}, u32[]{:S(2)}) copy-start(bf16[1,576,1024]{2,1,0:T(8,128)(2,1)} %param.18) | copy-start | bytes 3538948
  384.0 63.3 %copy-start.28 = (bf16[1,576,1024]{2,1,0:T(8,128)(2,1)S(1)}, bf16[1,576,1024]{2,1,0:T(8,128)(2,1)}, u32[]{:S(2)}) copy-start(bf16[1,576,1024]{2,1,0:T(8,128)(2,1)} %param.17) | copy-start | bytes 3538948
  626.2 484.7 %reduce-scatter.21.cloned.1.call-start = ((), (), s32[]{:S(2)}) async-start(), calls=%async_computation.14 | async-start | bytes 540672
  662.1 450.2 %reduce-scatter.13.cloned.1.call-start = ((), (), s32[]{:S(2)}) async-start(), calls=%async_computation.10 | async-start | bytes 4325376 | tf_op jit(solution)/shard_map/reduce_scatter | solution.py:339
  667.4 519.4 %reduce-scatter.19.cloned.1.call-start = ((), (), s32[]{:S(2)}) async-start(), calls=%async_computation.13 | async-start | bytes 12976128
  700.1 671.5 %reduce-scatter.15.cloned.1.call-start = ((), (), s32[]{:S(2)}) async-start(), calls=%async_computation.11 | async-start | bytes 17301504 | tf_op jit(solution)/shard_map/reduce_scatter | solution.py:343
  713.0 845.9 %reduce-scatter.17.cloned.1.call-start = ((), (), s32[]{:S(2)}) async-start(), calls=%async_computation.12 | async-start | bytes 17301504 | tf_op jit(solution)/shard_map/reduce_scatter | solution.py:344
  746.8 313.7 %copy-start.20 = (f32[4096]{0:T(1024)S(1)}, f32[4096]{0:T(1024)}, u32[]{:S(2)}) copy-start(f32[4096]{0:T(1024)} %get-tuple-element.204) | copy-start | bytes 49156
  746.8 352.9 %copy-start.7 = (f32[576,1024]{1,0:T(8,128)S(1)}, f32[576,1024]{1,0:T(8,128)}, u32[]{:S(2)}) copy-start(f32[576,1024]{1,0:T(8,128)} %copy-done.6) | copy-start | bytes 7077892
  746.8 352.9 %copy-start.19 = (f32[576]{0:T(1024)S(1)}, f32[576]{0:T(1024)}, u32[]{:S(2)}) copy-start(f32[576]{0:T(1024)} %copy-done.18) | copy-start | bytes 6916
  748.4 35.8 %slice-start = ((s8[11796480]{0:T(1024)(128)(4,1)}), s8[4194304]{0:T(1024)(128)(4,1)S(1)}, s32[]{:S(2)}) async-start(s8[11796480]{0:T(1024)(128)(4,1)} %bitcast.221), calls=%async_computation.16 | async-start | bytes 8388608 | tf_op jit(solution)/shard_map/while
  751.1 33.2 %slice-start.1 = ((s8[11796480]{0:T(1024)(128)(4,1)}), s8[4194304]{0:T(1024)(128)(4,1)S(1)}, s32[]{:S(2)}) async-start(s8[11796480]{0:T(1024)(128)(4,1)} %bitcast.221), calls=%async_computation.17 | async-start | bytes 8388608 | tf_op jit(solution)/shard_map/while
  751.1 33.2 %slice-start.2 = ((s8[11796480]{0:T(1024)(128)(4,1)}), s8[3407872]{0:T(1024)(128)(4,1)S(1)}, s32[]{:S(2)}) async-start(s8[11796480]{0:T(1024)(128)(4,1)} %bitcast.221), calls=%async_computation.18 | async-start | bytes 6815744 | tf_op jit(solution)/shard_map/while
  852.9 35.8 %slice-start = ((s8[11796480]{0:T(1024)(128)(4,1)}), s8[4194304]{0:T(1024)(128)(4,1)S(1)}, s32[]{:S(2)}) async-start(s8[11796480]{0:T(1024)(128)(4,1)} %bitcast.221), calls=%async_computation.16 | async-start | bytes 8388608 | tf_op jit(solution)/shard_map/while
  855.5 33.2 %slice-start.1 = ((s8[11796480]{0:T(1024)(128)(4,1)}), s8[4194304]{0:T(1024)(128)(4,1)S(1)}, s32[]{:S(2)}) async-start(s8[11796480]{0:T(1024)(128)(4,1)} %bitcast.221), calls=%async_computation.17 | async-start | bytes 8388608 | tf_op jit(solution)/shard_map/while
  855.5 33.2 %slice-start.2 = ((s8[11796480]{0:T(1024)(128)(4,1)}), s8[3407872]{0:T(1024)(128)(4,1)S(1)}, s32[]{:S(2)}) async-start(s8[11796480]{0:T(1024)(128)(4,1)} %bitcast.221), calls=%async_computation.18 | async-start | bytes 6815744 | tf_op jit(solution)/shard_map/while
  957.3 35.8 %slice-start = ((s8[11796480]{0:T(1024)(128)(4,1)}), s8[4194304]{0:T(1024)(128)(4,1)S(1)}, s32[]{:S(2)}) async-start(s8[11796480]{0:T(1024)(128)(4,1)} %bitcast.221), calls=%async_computation.16 | async-start | bytes 8388608 | tf_op jit(solution)/shard_map/while
  959.9 33.2 %slice-start.1 = ((s8[11796480]{0:T(1024)(128)(4,1)}), s8[4194304]{0:T(1024)(128)(4,1)S(1)}, s32[]{:S(2)}) async-start(s8[11796480]{0:T(1024)(128)(4,1)} %bitcast.221), calls=%async_computation.17 | async-start | bytes 8388608 | tf_op jit(solution)/shard_map/while
  (27 other events, 329.0 us)
Sparse Core Ops, SparseCore 0:
  10.9 72.1 all-gather.7
  85.9 54.8 all-gather.9
  143.7 76.7 all-gather.11
  223.1 76.2 all-gather.13
  626.3 129.7 reduce-scatter.22
  758.3 130.3 reduce-scatter.20
  891.5 137.1 reduce-scatter.12
  1035.3 151.4 reduce-scatter.18
  1189.7 181.8 reduce-scatter.14
  1374.4 184.4 reduce-scatter.16
where the time goes:
time: 1570 us
  matrix products  750 us (48%)
  waiting for transfers between devices  449 us (29%)
  blocking collectives  197 us (13%)
  local copies, waits for them, and re-layouts  103 us (7%)
  other arithmetic  50.7 us (3%)
    dot_general x9, matrix products, table_one_block(): jnp.einsum('qkb,hqk->bh', onehot, grad_block, preferred_element_type=jnp....  299 us
    dot_general x9, matrix products, spatial_one_block(): jnp.einsum('qkb,bh->hqk', onehot, tables[table_index], preferred_element_...  245 us
    reduce_scatter x1, waiting for transfers between devices, body(): lax.psum_scatter(grad_w_down, ('dp', 'fsdp'), scatter_dimension=0, tiled=...  187 us
    reduce_scatter x1, waiting for transfers between devices, body(): lax.psum_scatter(grad_w_in, ('dp', 'fsdp'), scatter_dimension=0, tiled=True)  185 us
    unnamed x13, waiting for transfers between devices  77.1 us
    unnamed x2, blocking collectives  75.2 us
    all_gather x1, blocking collectives, body(): lax.all_gather(vec_bias, ('dp', 'fsdp'), axis=1, tiled=True)  44 us
    dot_general x4, matrix products, dot_first(): lax.dot_general(left, right, (((0,), (0,)), ((), ())), preferred_element_...  42.7 us
  transfers between devices with their start and end apart: 10, of which 3 were waited for; matrix products, arithmetic and copies ran while one was open for 52% of the time, Pallas kernels for 0%

commit v1 on v0

v1 whole, which is shorter than its diff:
```python
import functools
import itertools

import jax
import jax.numpy as jnp
from jax import lax
from jax.experimental import pallas as pl
from jax.experimental.pallas import tpu as pltpu
from jax.sharding import PartitionSpec as P

H = 16
NB = 128
LANES = 128
EPSILON = 1e-05
MASK_FILL = -1e30
TABLE_STEP = 8192.0
VMEM_BYTES = 60 << 20
BOTH = ("dp", "fsdp")
MESH = pl.DeviceIdType.MESH
DIMS = (4, 2, 2)
GATHER_ORDERS = ((0, 2, 1), (0, 1, 2), (2, 1, 0))
STEPS = 5
LAG = 2
SMALL_ROWS = 16
SMALL_GRAD_ROWS = 8
GRAD_TILE = 64
HIGH_PARTS = 4
LOW_PARTS = NB // HIGH_PARTS


def dot_plain(left, right):
    return jnp.dot(left, right, preferred_element_type=jnp.float32)


def dot_first(left, right):
    return lax.dot_general(
        left, right, (((0,), (0,)), ((), ())), preferred_element_type=jnp.float32
    )


def dot_last(left, right):
    return lax.dot_general(
        left, right, (((1,), (1,)), ((), ())), preferred_element_type=jnp.float32
    )


def layer_norm(inputs, gain_row, shift_row):
    average = jnp.mean(inputs, axis=-1, keepdims=True)
    centered = inputs - average
    variance = jnp.mean(centered * centered, axis=-1, keepdims=True)
    return centered * lax.rsqrt(variance + EPSILON) * gain_row + shift_row


def gelu_exact(inputs):
    return jax.nn.gelu(inputs, approximate=False)


def coordinates():
    chip = lax.axis_index("dp")
    core = lax.axis_index("fsdp")
    planes, rows, columns = DIMS
    place = (
        chip // (rows * columns),
        lax.rem(chip // columns, rows),
        lax.rem(chip, columns),
    )
    return place, core


def device_at(place, core):
    return ((place[0] * DIMS[1] + place[1]) * DIMS[2] + place[2], core)


def shifted(place, axis, distance):
    moved = list(place)
    moved[axis] = lax.rem(moved[axis] + distance, DIMS[axis])
    return tuple(moved)


def greet(place, core):
    barrier = pltpu.get_barrier_semaphore()
    peers = [
        device_at(shifted(place, axis, distance), core)
        for axis in range(3)
        for distance in range(1, DIMS[axis])
    ]
    peers.append(device_at(place, 1 - core))
    for peer in peers:
        pl.semaphore_signal(barrier, inc=1, device_id=peer, device_id_type=MESH)
    pl.semaphore_wait(barrier, len(peers))


def schedule(waves, lag):
    events = []
    for wave in range(waves):
        for step in range(STEPS):
            events.append((wave + lag * step, wave, step))
    return [(wave, step) for slot, wave, step in sorted(events)]


def wave_of(array, row, rows, column, *tiles):
    bounds = [column]
    for count in tiles:
        bounds.append(bounds[-1] + count * LANES)
    return (array, row, rows, tuple(bounds))


def hops_before(order, phase):
    return sum(DIMS[axis] - 1 for axis in order[:phase])


def gather_steps(wave, number, full, send, recv, place, core):
    array, row, rows, bounds = wave
    whole = full[array]
    routes = [r for r in range(len(GATHER_ORDERS)) if bounds[r + 1] > bounds[r]]
    total_hops = hops_before(GATHER_ORDERS[0], 3)
    started = []
    arriving = {}
    from_core = []

    def copy(route, slot, index, target):
        part = whole.at[
            index[0], index[1], index[2], core,
            pl.ds(row, rows), pl.ds(bounds[route], bounds[route + 1] - bounds[route]),
        ]
        made = pltpu.make_async_remote_copy(
            part, part, send.at[number, route, slot], recv.at[number, route, slot],
            device_id=target, device_id_type=MESH,
        )
        made.start()
        started.append(made)
        return made

    def to_core(route, slot, index):
        from_core.append(copy(route, total_hops + slot, index, device_at(place, 1 - core)))

    def launch(phase):
        for route in routes:
            order = GATHER_ORDERS[route]
            index = list(place)
            for axis in order[:phase]:
                index[axis] = slice(None)
            for distance in range(1, DIMS[order[phase]]):
                arriving[route, phase, distance] = copy(
                    route, hops_before(order, phase) + distance - 1, index,
                    device_at(shifted(place, order[phase], distance), core),
                )

    def land(phase):
        for route in routes:
            order = GATHER_ORDERS[route]
            axis = order[phase]
            for distance in range(1, DIMS[axis]):
                arriving[route, phase, distance].wait_recv()
                index = list(place)
                for done in order[:phase]:
                    index[done] = slice(None)
                index[axis] = lax.rem(place[axis] + DIMS[axis] - distance, DIMS[axis])
                to_core(route, 1 + hops_before(order, phase) + distance - 1, index)

    def first():
        for route in routes:
            to_core(route, 0, list(place))
        launch(0)

    def second():
        land(0)
        launch(1)

    def third():
        land(1)
        launch(2)

    def fourth():
        land(2)

    def fifth():
        for made in from_core:
            made.wait_recv()
        for made in started:
            made.wait_send()

    return [first, second, third, fourth, fifth]


def gather_kernel(waves, arrays, *refs):
    shards = refs[:arrays]
    outs = refs[arrays : 2 * arrays]
    local_sem, send, recv, out_sem = refs[2 * arrays : 2 * arrays + 4]
    full = refs[2 * arrays + 4 :]
    place, core = coordinates()
    own = [
        pltpu.make_async_copy(
            shards[i], full[i].at[place[0], place[1], place[2], core], local_sem.at[i]
        )
        for i in range(arrays)
    ]
    for copy in own:
        copy.start()
    greet(place, core)
    steps = [
        gather_steps(wave, number, full, send, recv, place, core)
        for number, wave in enumerate(waves)
    ]
    for copy in own:
        copy.wait()
    leaving = []
    for number, step in schedule(len(waves), LAG):
        steps[number][step]()
        if step == STEPS - 1:
            array, row, rows, bounds = waves[number]
            part = (slice(None),) * 4 + (
                pl.ds(row, rows), pl.ds(bounds[0], bounds[-1] - bounds[0]),
            )
            out = pltpu.make_async_copy(
                full[array].at[part], outs[array].at[part], out_sem.at[number]
            )
            out.start()
            leaving.append(out)
    for out in leaving:
        out.wait()


def gather_all(shards, waves, collective):
    arrays = len(shards)
    routes = len(GATHER_ORDERS)
    hops = 2 * hops_before(GATHER_ORDERS[0], 3) + 1
    return pl.pallas_call(
        functools.partial(gather_kernel, waves, arrays),
        in_specs=[pl.BlockSpec(memory_space=pl.ANY)] * arrays,
        out_specs=[pl.BlockSpec(memory_space=pl.ANY)] * arrays,
        out_shape=[
            jax.ShapeDtypeStruct(DIMS + (2,) + shard.shape, shard.dtype) for shard in shards
        ],
        scratch_shapes=[
            pltpu.SemaphoreType.DMA((arrays,)),
            pltpu.SemaphoreType.DMA((len(waves), routes, hops)),
            pltpu.SemaphoreType.DMA((len(waves), routes, hops)),
            pltpu.SemaphoreType.DMA((len(waves),)),
        ]
        + [pltpu.VMEM(DIMS + (2,) + shard.shape, shard.dtype) for shard in shards],
        compiler_params=pltpu.CompilerParams(
            collective_id=collective, has_side_effects=True, vmem_limit_bytes=VMEM_BYTES
        ),
    )(*shards)


def reduce_orders():
    return [tuple(reversed(order)) for order in GATHER_ORDERS]


def axes_left(order, phase):
    return [axis for axis in range(3) if axis not in order[: phase + 1]]


def scatter_scratch(waves, dtypes):
    shapes = []
    for array, row, rows, bounds in waves:
        dtype = dtypes[array]
        block = DIMS + (rows, bounds[-1] - bounds[0])
        shapes += [pltpu.VMEM(block, dtype), pltpu.VMEM(block, dtype)]
        for route, order in enumerate(reduce_orders()):
            width = bounds[route + 1] - bounds[route]
            for phase in range(3 if width else 0):
                left = tuple(DIMS[axis] for axis in axes_left(order, phase))
                shapes.append(
                    pltpu.VMEM((DIMS[order[phase]] - 1,) + left + (rows, width), dtype)
                )
    return shapes


def scatter_steps(wave, number, grads, outs, scratch, local_sem, send, recv, place, core):
    array, row, rows, bounds = wave
    grad = grads[array]
    base = bounds[0]
    width = bounds[-1] - base
    total = next(scratch)
    other = next(scratch)
    orders = reduce_orders()
    routes = [r for r in range(len(orders)) if bounds[r + 1] > bounds[r]]
    landing = {}
    for route in routes:
        for phase in range(3):
            landing[route, phase] = next(scratch)
    core_slot = hops_before(orders[0], 3)
    started = []
    arriving = {}
    every = slice(None)

    def half(which):
        return grad.at[:, :, :, which, pl.ds(row, rows), pl.ds(base, width)]

    def first():
        arriving["own"] = pltpu.make_async_copy(half(core), total, local_sem.at[number])
        arriving["own"].start()
        made = pltpu.make_async_remote_copy(
            half(1 - core), other, send.at[number, 0, core_slot], recv.at[number, 0, core_slot],
            device_id=device_at(place, 1 - core), device_id_type=MESH,
        )
        made.start()
        started.append(made)
        arriving["core"] = made

    def launch(phase):
        for route in routes:
            order = orders[route]
            axis = order[phase]
            for distance in range(1, DIMS[axis]):
                index = [every] * 3
                for done in order[:phase]:
                    index[done] = place[done]
                index[axis] = lax.rem(place[axis] + distance, DIMS[axis])
                slot = hops_before(order, phase) + distance - 1
                made = pltpu.make_async_remote_copy(
                    total.at[
                        index[0], index[1], index[2], :,
                        pl.ds(bounds[route] - base, bounds[route + 1] - bounds[route]),
                    ],
                    landing[route, phase].at[distance - 1],
                    send.at[number, route, slot], recv.at[number, route, slot],
                    device_id=device_at(shifted(place, axis, distance), core),
                    device_id_type=MESH,
                )
                made.start()
                started.append(made)
                arriving[route, phase, distance] = made

    def land(phase):
        for route in routes:
            order = orders[route]
            axis = order[phase]
            for distance in range(1, DIMS[axis]):
                arriving[route, phase, distance].wait_recv()
            left = axes_left(order, phase)
            columns = slice(bounds[route] - base, bounds[route + 1] - base)
            for spot in itertools.product(*[range(DIMS[a]) for a in left]):
                index = list(place)
                for a, value in zip(left, spot):
                    index[a] = value
                at = (index[0], index[1], index[2], every, columns)
                added = total[at].astype(jnp.float32)
                for distance in range(1, DIMS[axis]):
                    added += landing[route, phase][(distance - 1,) + spot].astype(jnp.float32)
                if phase == 2:
                    outs[array][pl.ds(row, rows), bounds[route] : bounds[route + 1]] = added
                else:
                    total[at] = added.astype(total.dtype)

    def second():
        arriving["own"].wait()
        arriving["core"].wait_recv()

        def one_plane(plane, carry):
            for y, x in itertools.product(range(DIMS[1]), range(DIMS[2])):
                total[plane, y, x] = total[plane, y, x] + other[plane, y, x]
            return carry

        lax.fori_loop(0, DIMS[0], one_plane, 0)
        launch(0)

    def third():
        land(0)
        launch(1)

    def fourth():
        land(1)
        launch(2)

    def fifth():
        land(2)
        for made in started:
            made.wait_send()

    return [first, second, third, fourth, fifth]


def scatter_kernel(waves, arrays, *refs):
    grads = refs[:arrays]
    outs = refs[arrays : 2 * arrays]
    local_sem, send, recv = refs[2 * arrays : 2 * arrays + 3]
    scratch = iter(refs[2 * arrays + 3 :])
    place, core = coordinates()
    greet(place, core)
    steps = [
        scatter_steps(wave, number, grads, outs, scratch, local_sem, send, recv, place, core)
        for number, wave in enumerate(waves)
    ]
    for number, step in schedule(len(waves), LAG):
        steps[number][step]()


def scatter_all(grads, waves, collective):
    arrays = len(grads)
    sems = (len(waves), len(GATHER_ORDERS), hops_before(GATHER_ORDERS[0], 3) + 1)
    return pl.pallas_call(
        functools.partial(scatter_kernel, waves, arrays),
        in_specs=[pl.BlockSpec(memory_space=pl.ANY)] * arrays,
        out_specs=[pl.BlockSpec(memory_space=pltpu.VMEM)] * arrays,
        out_shape=[jax.ShapeDtypeStruct(grad.shape[4:], jnp.float32) for grad in grads],
        scratch_shapes=[
            pltpu.SemaphoreType.DMA((len(waves),)),
            pltpu.SemaphoreType.DMA(sems),
            pltpu.SemaphoreType.DMA(sems),
        ]
        + scatter_scratch(waves, [grad.dtype for grad in grads]),
        compiler_params=pltpu.CompilerParams(
            collective_id=collective, has_side_effects=True, vmem_limit_bytes=VMEM_BYTES
        ),
    )(*grads)


def split_wave(array, row, rows, column, tiles, turn):
    edge = tiles // 8
    one = (tiles - edge + turn) // 2
    return wave_of(array, row, rows, column, one, tiles - edge - one, edge)


def weight_waves(array, rows, columns, row_step, tile_step):
    waves = []
    tiles = columns // LANES
    for row in range(0, rows, row_step):
        for tile in range(0, tiles, tile_step):
            size = min(tile_step, tiles - tile)
            waves.append(
                split_wave(array, row, row_step, tile * LANES, size, (len(waves) + array) % 2)
            )
    return waves


def attention_forward_kernel(
    key_ref, query_ref, value_ref, packed_ref, table_ref, mask_ref, probs_ref, context_ref,
    score_ref,
):
    length = key_ref.shape[0]
    padded = packed_ref.shape[1]
    pair = query_ref.shape[0]
    half = pair // 2
    feature = lax.broadcasted_iota(jnp.int32, (pair, padded), 0)
    queries = query_ref[...]
    zero = jnp.zeros_like(queries)
    score_ref[0] = dot_plain(key_ref[...], jnp.where(feature < half, queries, zero))
    score_ref[1] = dot_plain(key_ref[...], jnp.where(feature < half, zero, queries))
    for column in range(0, padded, LANES):
        lanes = slice(column, column + LANES)
        rows = [jnp.broadcast_to(table_ref[t, 0], (8, LANES)) for t in range(3)]
        tops = [jnp.full((8, LANES), 3.0 * MASK_FILL, jnp.float32) for side in range(2)]
        for start in range(0, length, 8):
            here = slice(start, start + 8)
            packed = packed_ref[here, lanes]
            sums = [None, None]
            for table in range(3):
                index = (packed >> (7 * table)) & (NB - 1)
                word = jnp.take_along_axis(rows[table], index, axis=1)
                for side, term in ((0, word >> 16), (1, (word << 16) >> 16)):
                    sums[side] = term if table == 0 else sums[side] + term
            mask = mask_ref[here, lanes]
            for side in range(2):
                scores = score_ref[side, here, lanes] + (
                    sums[side].astype(jnp.float32) * (1.0 / TABLE_STEP) + mask
                )
                score_ref[side, here, lanes] = scores
                tops[side] = jnp.maximum(tops[side], scores)
        for side in range(2):
            top = jnp.max(tops[side], axis=0, keepdims=True)
            exponent = jnp.exp(score_ref[side, :, lanes] - top)
            total = jnp.sum(exponent, axis=0, keepdims=True)
            probs_ref[side, :, lanes] = (exponent * (1.0 / total)).astype(jnp.bfloat16)
    for side in range(2):
        mine = slice(side * half, (side + 1) * half)
        context_ref[mine, :] = dot_plain(value_ref[mine, :], probs_ref[side]).astype(jnp.bfloat16)


def attention_forward(keys, queries_t, values_t, packed, tables, mask):
    length, width = keys.shape
    padded = packed.shape[1]
    pairs = H // 2
    pair = width // pairs
    whole = pl.BlockSpec((length, padded), lambda p: (0, 0))
    return pl.pallas_call(
        attention_forward_kernel,
        grid=(pairs,),
        in_specs=[
            pl.BlockSpec((length, pair), lambda p: (0, p)),
            pl.BlockSpec((pair, padded), lambda p: (p, 0)),
            pl.BlockSpec((pair, length), lambda p: (p, 0)),
            whole,
            pl.BlockSpec((3, 1, 1, NB), lambda p: (0, p, 0, 0)),
            whole,
        ],
        out_specs=[
            pl.BlockSpec((2, length, padded), lambda p: (p, 0, 0)),
            pl.BlockSpec((pair, padded), lambda p: (p, 0)),
        ],
        out_shape=[
            jax.ShapeDtypeStruct((H, length, padded), jnp.bfloat16),
            jax.ShapeDtypeStruct((width, padded), jnp.bfloat16),
        ],
        scratch_shapes=[pltpu.VMEM((2, length, padded), jnp.float32)],
        compiler_params=pltpu.CompilerParams(vmem_limit_bytes=VMEM_BYTES),
    )(keys, queries_t, values_t, packed, tables, mask)


def attention_backward_kernel(
    value_ref, context_grad_t_ref, context_grad_ref, query_ref, key_t_ref, probs_ref,
    grad_query_ref, grad_key_ref, grad_value_ref, score_grad_ref, prob_grad_ref, low_ref,
):
    length = value_ref.shape[0]
    pair, padded = context_grad_t_ref.shape
    half = pair // 2
    scale = half ** (-0.5)
    feature = lax.broadcasted_iota(jnp.int32, (pair, padded), 0)
    upstream = context_grad_t_ref[...]
    zero = jnp.zeros_like(upstream)
    prob_grad_ref[0] = dot_plain(value_ref[...], jnp.where(feature < half, upstream, zero))
    prob_grad_ref[1] = dot_plain(value_ref[...], jnp.where(feature < half, zero, upstream))
    for part in range(padded // LANES):
        lanes = slice(part * LANES, (part + 1) * LANES)
        for side in range(2):
            probs = probs_ref[side, :, lanes].astype(jnp.float32)
            prob_grad = prob_grad_ref[side, :, lanes]
            inner = jnp.sum(probs * prob_grad, axis=0, keepdims=True)
            score_grad = probs * (prob_grad - inner)
            score_grad_ref[part, side] = score_grad
            low_ref[side, :, lanes] = score_grad.astype(jnp.bfloat16)
    for side in range(2):
        mine = slice(side * half, (side + 1) * half)
        grad_query_ref[mine, :] = (dot_plain(key_t_ref[mine, :], low_ref[side]) * scale).astype(
            jnp.bfloat16
        )
    first_half = lax.broadcasted_iota(jnp.int32, (length, pair), 1) < half
    grad_key = [dot_plain(low_ref[side], query_ref[...]) for side in range(2)]
    grad_key_ref[...] = jnp.where(first_half, grad_key[0], grad_key[1]).astype(jnp.bfloat16)
    grad_value = [dot_plain(probs_ref[side], context_grad_ref[...]) for side in range(2)]
    grad_value_ref[...] = jnp.where(first_half, grad_value[0], grad_value[1]).astype(jnp.bfloat16)


def attention_backward(values, context_grad_t, context_grad, queries, keys_t, probs):
    length, width = values.shape
    padded = probs.shape[2]
    pairs = H // 2
    pair = width // pairs
    natural = pl.BlockSpec((length, pair), lambda p: (0, p))
    longer = pl.BlockSpec((padded, pair), lambda p: (0, p))
    flipped = pl.BlockSpec((pair, padded), lambda p: (p, 0))
    return pl.pallas_call(
        attention_backward_kernel,
        grid=(pairs,),
        in_specs=[
            natural,
            flipped,
            longer,
            longer,
            pl.BlockSpec((pair, length), lambda p: (p, 0)),
            pl.BlockSpec((2, length, padded), lambda p: (p, 0, 0)),
        ],
        out_specs=[
            flipped,
            natural,
            natural,
            pl.BlockSpec((padded // LANES, 2, length, LANES), lambda p: (0, p, 0, 0)),
        ],
        out_shape=[
            jax.ShapeDtypeStruct((width, padded), jnp.bfloat16),
            jax.ShapeDtypeStruct((length, width), jnp.bfloat16),
            jax.ShapeDtypeStruct((length, width), jnp.bfloat16),
            jax.ShapeDtypeStruct((padded // LANES, H, length, LANES), jnp.float32),
        ],
        scratch_shapes=[
            pltpu.VMEM((2, length, padded), jnp.float32),
            pltpu.VMEM((2, length, padded), jnp.bfloat16),
        ],
        compiler_params=pltpu.CompilerParams(vmem_limit_bytes=VMEM_BYTES),
    )(values, context_grad_t, context_grad, queries, keys_t, probs)


def table_grad_kernel(digit_ref, score_grad_ref, out_ref):
    padded = score_grad_ref.shape[0] * LANES

    @pl.when(pl.program_id(0) == 0)
    def start():
        out_ref[...] = jnp.zeros_like(out_ref)

    levels = lax.broadcasted_iota(jnp.int32, (LOW_PARTS, padded), 0).astype(jnp.bfloat16)
    one = jnp.ones((LOW_PARTS, padded), jnp.bfloat16)
    no_one = jnp.zeros((LOW_PARTS, padded), jnp.bfloat16)
    nothing = jnp.zeros((H, padded), jnp.bfloat16)
    flat_ref = score_grad_ref.reshape(padded // LANES * H * GRAD_TILE, LANES)

    def one_group(group, total):
        for offset in range(4):
            row = group * 4 + offset
            grads = jnp.concatenate(
                [
                    flat_ref[pl.ds(part * H * GRAD_TILE + row, H, stride=GRAD_TILE), :]
                    for part in range(padded // LANES)
                ],
                axis=1,
            ).astype(jnp.bfloat16)
            masked = []
            onehot = []
            for table in range(3):
                high = jnp.broadcast_to(digit_ref[row, table : table + 1, :], (H, padded))
                for part in range(HIGH_PARTS):
                    masked.append(jnp.where(high == jnp.bfloat16(part), grads, nothing))
                low = jnp.broadcast_to(digit_ref[row, 3 + table : 4 + table, :], (LOW_PARTS, padded))
                onehot.append(jnp.where(low == levels, one, no_one))
            total = total + dot_last(jnp.concatenate(masked, axis=0), jnp.concatenate(onehot, axis=0))
        return total

    out_ref[...] += lax.fori_loop(
        0, GRAD_TILE // 4, one_group, jnp.zeros(out_ref.shape, jnp.float32)
    )


def table_grads(digits, score_grad):
    length = score_grad.shape[2]
    padded = score_grad.shape[0] * LANES
    shape = (3 * HIGH_PARTS * H, 3 * LOW_PARTS)
    products = pl.pallas_call(
        table_grad_kernel,
        grid=(length // GRAD_TILE,),
        in_specs=[
            pl.BlockSpec((GRAD_TILE, 6, padded), lambda i: (i, 0, 0)),
            pl.BlockSpec((padded // LANES, H, GRAD_TILE, LANES), lambda i: (0, 0, i, 0)),
        ],
        out_specs=pl.BlockSpec(shape, lambda i: (0, 0)),
        out_shape=jax.ShapeDtypeStruct(shape, jnp.float32),
        compiler_params=pltpu.CompilerParams(vmem_limit_bytes=VMEM_BYTES),
    )(digits, score_grad)
    split = products.reshape(3, HIGH_PARTS, H, 3, LOW_PARTS)
    return jnp.stack(
        [jnp.transpose(split[t, :, :, t, :], (0, 2, 1)).reshape(NB, H) for t in range(3)]
    )


def norm_backward(inputs, gain_row, upstream):
    average = jnp.mean(inputs, axis=-1, keepdims=True)
    centered = inputs - average
    spread = lax.rsqrt(jnp.mean(centered * centered, axis=-1, keepdims=True) + EPSILON)
    normed = centered * spread
    scaled = upstream * gain_row
    grad = spread * (
        scaled
        - jnp.mean(scaled, axis=-1, keepdims=True)
        - normed * jnp.mean(scaled * normed, axis=-1, keepdims=True)
    )
    return grad, jnp.sum(upstream * normed, axis=0), jnp.sum(upstream, axis=0)


def small_piece(vec_bias, norm_gain, bias_hidden, rel_tables):
    return jnp.concatenate(
        [vec_bias.reshape(-1), norm_gain.reshape(-1), bias_hidden, rel_tables]
    )


def spread_small(everything, vec_rows, gain_rows, vec_size, gain_size, hidden_size):
    devices = everything.shape[0]
    vectors, gains, hidden, tables = jnp.split(
        everything, [vec_size, vec_size + gain_size, vec_size + gain_size + hidden_size], axis=1
    )
    vectors = jnp.transpose(vectors.reshape(devices, vec_rows, -1), (1, 0, 2))
    gains = jnp.transpose(gains.reshape(devices, gain_rows, -1), (1, 0, 2))
    return (
        vectors.reshape(vec_rows, -1).astype(jnp.float32),
        gains.reshape(gain_rows, -1).astype(jnp.float32),
        hidden.reshape(-1).astype(jnp.float32),
        tables.reshape(3, NB, H),
    )


def body(
    own_kernels, block_input, cotangent, seg_ids, slot_valid, rel_buckets, w_qkv, w_out, w_in,
    w_down, vec_bias, norm_gain, bias_hidden, rel_tables,
):
    row_in = block_input[0]
    row_cot = cotangent[0].astype(jnp.float32)
    segments = seg_ids[0]
    validity = slot_valid[0]
    buckets = rel_buckets[0]
    length, width = row_in.shape
    padded = -(-length // LANES) * LANES
    scale = (width // H) ** (-0.5)
    devices = lax.axis_size(BOTH)
    weights = [w_qkv, w_out, w_in, w_down]

    small = small_piece(vec_bias, norm_gain, bias_hidden, rel_tables)
    small_size = small.shape[0]
    weight_plan = [
        weight_waves(0, w_qkv.shape[0], w_qkv.shape[1], w_qkv.shape[0], 8),
        weight_waves(1, w_out.shape[0], w_out.shape[1], w_out.shape[0], 8),
        weight_waves(2, w_in.shape[0], w_in.shape[1], w_in.shape[0], 8),
        weight_waves(3, w_down.shape[0], w_down.shape[1], 32, 8),
    ]
    if own_kernels:
        pad_to = SMALL_ROWS * LANES
        small_block = jnp.pad(small, (0, pad_to - small_size)).reshape(SMALL_ROWS, LANES)
        plan = [wave_of(4, 0, SMALL_ROWS, 0, 1, 0, 0)] + sum(weight_plan, [])
        gathered = gather_all(weights + [small_block], plan, 1)
        full_qkv, full_out, full_in, full_down = [
            whole.reshape(-1, whole.shape[-1]) for whole in gathered[:4]
        ]
        everything = gathered[4].reshape(devices, pad_to)[:, :small_size]
    else:
        full_qkv, full_out, full_in, full_down = [
            lax.all_gather(weight, BOTH, axis=0, tiled=True) for weight in weights
        ]
        everything = lax.all_gather(small, BOTH, axis=0, tiled=False)
    vectors, gains, hidden_bias, tables = spread_small(
        everything, vec_bias.shape[0], norm_gain.shape[0], vec_bias.size, norm_gain.size,
        bias_hidden.size,
    )

    wide = ((0, 0), (0, padded - length))
    buckets = jnp.swapaxes(buckets, 1, 2)
    packed = jnp.pad(buckets[0] | (buckets[1] << 7) | (buckets[2] << 14), wide)
    digits = jnp.concatenate([buckets // LOW_PARTS, buckets % LOW_PARTS], axis=0)
    digits = jnp.pad(
        jnp.transpose(digits.astype(jnp.bfloat16), (1, 0, 2)), ((0, 0),) + wide
    )
    position = jnp.arange(length)
    allowed = (segments[:, None] == segments[None, :]) & (
        (validity[:, None] > 0) | (position[:, None] == position[None, :])
    )
    mask = jnp.pad(jnp.where(allowed, 0.0, MASK_FILL), wide)
    steps = jnp.round(tables.astype(jnp.float32) * TABLE_STEP).astype(jnp.int32)
    pair_tables = (steps[:, :, 0::2] << 16) | (steps[:, :, 1::2] & 0xFFFF)
    pair_tables = jnp.transpose(pair_tables, (0, 2, 1))[:, :, None, :]

    mixed = dot_plain(row_in, full_qkv)
    queries = (mixed[:, :width] + vectors[0]).astype(jnp.bfloat16) * jnp.bfloat16(scale)
    keys = mixed[:, width : 2 * width].astype(jnp.bfloat16)
    values = (mixed[:, 2 * width :] + vectors[1]).astype(jnp.bfloat16)
    taller = ((0, padded - length), (0, 0))
    queries = jnp.pad(queries, taller)
    probs, context_t = attention_forward(keys, queries.T, values.T, packed, pair_tables, mask)
    context_t = context_t[:, :length]
    first_sum = row_in.astype(jnp.float32) + dot_first(context_t, full_out) + vectors[2]
    normed_first = layer_norm(first_sum, gains[0], vectors[4])
    first_low = normed_first.astype(jnp.bfloat16)
    hidden = dot_plain(first_low, full_in) + hidden_bias
    active = gelu_exact(hidden).astype(jnp.bfloat16)
    second_sum = normed_first + dot_plain(active, full_down) + vectors[3]
    output = layer_norm(second_sum, gains[1], vectors[5]).astype(jnp.bfloat16)

    grad_second, grad_gain_two, grad_shift_two = norm_backward(second_sum, gains[1], row_cot)
    down_grad = grad_second.astype(jnp.bfloat16)
    grad_w_down = dot_first(active, down_grad).astype(jnp.bfloat16)
    unused, gelu_back = jax.vjp(gelu_exact, hidden)
    hidden_grad = gelu_back(dot_last(down_grad, full_down))[0].astype(jnp.bfloat16)
    grad_w_in = dot_first(first_low, hidden_grad).astype(jnp.bfloat16)
    grad_first = dot_last(hidden_grad, full_in) + grad_second
    grad_first_sum, grad_gain_one, grad_shift_one = norm_backward(first_sum, gains[0], grad_first)
    branch_grad = grad_first_sum.astype(jnp.bfloat16)
    grad_w_out = dot_plain(context_t, branch_grad).astype(jnp.bfloat16)
    context_grad = jnp.pad(dot_last(branch_grad, full_out).astype(jnp.bfloat16), taller)
    grad_queries_t, grad_keys, grad_values, score_grad = attention_backward(
        values, context_grad.T, context_grad, queries, keys.T, probs
    )
    grad_queries = grad_queries_t[:, :length].T
    grad_mixed = jnp.concatenate([grad_queries, grad_keys, grad_values], axis=1)
    grad_w_qkv = dot_first(row_in, grad_mixed).astype(jnp.bfloat16)
    grad_input = grad_first_sum + dot_last(grad_mixed, full_qkv)
    grad_tables = table_grads(digits, score_grad)

    grad_vectors = jnp.stack(
        [
            jnp.sum(grad_queries.astype(jnp.float32), axis=0),
            jnp.sum(grad_values.astype(jnp.float32), axis=0),
            jnp.sum(branch_grad.astype(jnp.float32), axis=0),
            jnp.sum(down_grad.astype(jnp.float32), axis=0),
            grad_shift_one,
            grad_shift_two,
        ]
    )
    grad_gains = jnp.stack([grad_gain_one, grad_gain_two])
    grad_hidden_bias = jnp.sum(hidden_grad.astype(jnp.float32), axis=0)

    def by_device(matrix):
        return jnp.transpose(matrix.reshape(matrix.shape[0], devices, -1), (1, 0, 2)).reshape(
            devices, -1
        )

    small_grads = jnp.concatenate(
        [
            by_device(grad_vectors),
            by_device(grad_gains),
            grad_hidden_bias.reshape(devices, -1),
            grad_tables.reshape(devices, -1),
        ],
        axis=1,
    )
    weight_grads = [grad_w_qkv, grad_w_out, grad_w_in, grad_w_down]
    if own_kernels:
        pad_to = SMALL_GRAD_ROWS * LANES
        small_block = jnp.pad(small_grads, ((0, 0), (0, pad_to - small_size)))
        blocks = [
            grad.reshape(DIMS + (2,) + weight.shape) for grad, weight in zip(weight_grads, weights)
        ] + [small_block.reshape(DIMS + (2, SMALL_GRAD_ROWS, LANES))]
        plan = (
            weight_plan[3] + weight_plan[2] + weight_plan[1] + weight_plan[0]
            + [wave_of(4, 0, SMALL_GRAD_ROWS, 0, 1, 0, 0)]
        )
        shards = scatter_all(blocks, plan, 2)
        small_shard = shards[4].reshape(-1)[:small_size]
    else:
        shards = [
            lax.psum_scatter(
                grad.astype(jnp.float32), BOTH, scatter_dimension=0, tiled=True
            )
            for grad in weight_grads
        ]
        small_shard = lax.psum_scatter(small_grads, BOTH, scatter_dimension=0, tiled=True)[0]
    shard_vectors, shard_gains, shard_hidden, shard_tables = jnp.split(
        small_shard,
        [
            vec_bias.size,
            vec_bias.size + norm_gain.size,
            vec_bias.size + norm_gain.size + bias_hidden.size,
        ],
    )
    return (
        output[None],
        grad_input[None],
        shards[0],
        shards[1],
        shards[2],
        shards[3],
        shard_vectors.reshape(vec_bias.shape),
        shard_gains.reshape(norm_gain.shape),
        shard_hidden,
        shard_tables,
    )


def solution(mesh):
    rows = P(BOTH)
    columns = P(None, BOTH)
    in_specs = (rows,) * 9 + (columns, columns, rows, rows)
    out_specs = (rows,) * 6 + (columns, columns, rows, rows)
    chips = DIMS[0] * DIMS[1] * DIMS[2]
    own_kernels = mesh.shape["dp"] == chips and mesh.shape["fsdp"] == 2
    return jax.shard_map(
        functools.partial(body, own_kernels),
        mesh=mesh,
        in_specs=in_specs,
        out_specs=out_specs,
        check_vma=False,
    )
```

time: 1570 us -> 596 us (0.38)
  matrix products: 750 us -> 123 us
  waiting for transfers between devices: 449 us -> 0 us
  Pallas kernels: 0 us -> 361 us
  blocking collectives: 197 us -> 0 us
  local copies, waits for them, and re-layouts: 103 us -> 59.5 us
    dot_general x28 -> x4, matrix products: 667 us -> 48.4 us  [dot_plain(): return jnp.dot(left, right, preferred_element_type=jnp.float32)]
    reduce_scatter x3 -> x0, waiting for transfers between devices: 372 us -> none  [the longest x1 187 us: body(): lax.psum_scatter(grad_w_down, ('dp', 'fsdp'), scatter_dimension=0, tiled=...]
    pallas_call x0 -> x5, Pallas kernels: none -> 361 us  [the longest x1 121 us: gather_all(): pl.pallas_call(functools.partial(gather_kernel, waves, arrays), in_specs=...]
    all_gather x3 -> x0, blocking collectives: 122 us -> none  [the longest x1 44 us: body(): lax.all_gather(vec_bias, ('dp', 'fsdp'), axis=1, tiled=True)]
    unnamed x13 -> x0, waiting for transfers between devices: 77.1 us -> none
    unnamed x2 -> x0, blocking collectives: 75.2 us -> none
    convert_element_type x3 -> x5, other arithmetic: 22.6 us -> 1.38 us  [the longest x1 1.29 us: body(): values = (mixed[:, 2 * width:] + vectors[1]).astype(jnp.bfloat16)]
    transpose x1 -> x6, local copies, waits for them, and re-layouts: 20.2 us -> 2.79 us  [the longest x1 1.48 us: body(): grad_queries_t, grad_keys, grad_values, score_grad = attention_backward(v...]
  transfers between devices with their start and end apart: 10 -> 0, of which waited for: 3 -> 0; matrix products, arithmetic and copies ran while one was open for 52% -> 0% of each run, Pallas kernels for 0% -> 0%
where the time goes in v1:
time: 596 us; the launch traced here: 589 us
  Pallas kernels  361 us (61%)
  matrix products  123 us (21%)
  local copies, waits for them, and re-layouts  59.5 us (10%)
  other arithmetic  43.3 us (7%)
    pallas_call x1, Pallas kernels, gather_all(): pl.pallas_call(functools.partial(gather_kernel, waves, arrays), in_specs=...  121 us
    pallas_call x1, Pallas kernels, scatter_all(): pl.pallas_call(functools.partial(scatter_kernel, waves, arrays), in_specs...  116 us
    pallas_call x1, Pallas kernels, table_grads(): pl.pallas_call(table_grad_kernel, grid=(length // GRAD_TILE,), in_specs=[...  65.3 us
    dot_general x4, matrix products, dot_plain(): return jnp.dot(left, right, preferred_element_type=jnp.float32)  48.4 us
    dot_general x4, matrix products, dot_last(): lax.dot_general(left, right, (((1,), (1,)), ((), ())), preferred_element_...  38.7 us
    dot_general x4, matrix products, dot_first(): lax.dot_general(left, right, (((0,), (0,)), ((), ())), preferred_element_...  36.3 us
    pallas_call x1, Pallas kernels, attention_forward(): pl.pallas_call(attention_forward_kernel, grid=(pairs,), in_specs=[pl.Bloc...  35.6 us
    unnamed x93, local copies, waits for them, and re-layouts  23.5 us

profile of v1, /device:TPU:0, one launch (start us, length us, event | category | flops | bytes accessed | tf_op | source)
XLA Modules:
  0.0 588.9 jit_solution(9332746652558314778)
XLA Ops:
  8.6 8.5 %copy.31 = s32[1,3,576,576]{2,1,3,0:T(4,128)} copy(s32[1,3,576,576]{3,2,1,0:T(8,128)} %param.17) | data formatting | bytes 7962624 | tf_op args[4]
  17.1 10.0 %fusion.21 = s32[1,576,576]{2,0,1:T(1,128)S(1)} fusion(s32[3,576,576]{2,0,1:T(4,128)} %bitcast.119), kind=kLoop, calls=%fused_computation.72 | loop fusion | flops 1327104 | bytes 5308416 | tf_op jit(solution)/shard_map/or | solution.py:715
  28.5 1.9 copy-done
  30.4 11.8 %fusion.6 = (bf16[3,576,576]{2,0,1:T(4,128)(2,1)S(1)}, bf16[3,576,576]{2,0,1:T(4,128)(2,1)S(1)}) fusion(s32[1,3,576,576]{2,1,3,0:T(4,128)S(1)} %copy-done), kind=kLoop, calls=%fused_computation.25 | loop fusion | flops 20901888 | bytes 7962624 | tf_op jit(solution)/shard_map/convert.5
  42.2 3.2 maximum_bitcast_fusion
  45.4 3.8 pad.32.digit_ref
  49.2 120.9 %shard_map.204 = (bf16[4,2,2,2,32,3072]{5,4,3,2,1,0:T(8,128)(2,1)}, bf16[4,2,2,2,32,1024]{5,4,3,2,1,0:T(8,128)(2,1)}, bf16[4,2,2,2,32,4096]{5,4,3,2,1,0:T(8,128)...) custom-call(bf16[32,3072]{1,0:T(8,128)(2,1)} %refs_0_.1, bf16[32,1024]{1,0:T(8,128)(2,1)} %refs_1_.1, ...), custom_call_target="tpu_custom_call" | custom-call | tf_op jit(solution)/shard_map/pallas_call | solution.py:228
  175.7 7.4 %convolution_bitcast_fusion = f32[576,3072]{0,1:T(8,128)S(1)} fusion(bf16[1024,3072]{1,0:T(8,128)(2,1)} %bitcast.149, bf16[1,576,1024]{2,1,0:T(8,128)(2,1)S(1)} %copy-done.35), kind=kOutput, calls=%fused_computation.31 | convolution fusion | flops 3623878656 | bytes 14548992 | tf_op jit(solution)/shard_map/dot_general | solution.py:32
  186.2 2.9 copy.35.value_ref
  194.9 35.6 %shard_map.205 = (bf16[16,576,640]{2,1,0:T(8,128)(2,1)}, bf16[1024,640]{1,0:T(8,128)(2,1)}) custom-call(bf16[576,1024]{1,0:T(8,128)(2,1)} %copy.34.key_ref, bf16[1024,640]{1,0:T(8,128)(2,1)} %pad_bitcast_fusion.1.query_ref, bf16[1024,576]{1,0:T(8,128)(2,1)} %fusion.72.value_ref, s32[576,640]{1,0:T(8,128)} %pad.29.packed_ref, s32[3,8,1,128]{3,2,1,0:T(1,128)} %bitcast.138, ...), custom_call_target="tpu_custom_call" | custom-call | tf_op jit(solution)/shard_map/pallas_call | solution.py:479
  230.5 3.4 fusion.58
  234.6 30.4 %multiply_convert_fusion = (bf16[576,4096]{1,0:T(8,128)(2,1)S(1)}, f32[576,4096]{1,0:T(8,128)}, f32[576,4096]{1,0:T(8,128)}) fusion(f32[4096]{0:T(1024)S(1)} %fusion.33, bf16[1024,4096]{1,0:T(8,128)(2,1)S(1)} %bitcast.144, f32[576,1024]{1,0:T(8,128)S(1)} %get-tuple-element.74, f32[1024]{0:T(1024)S(1)} %add.130, f32[1024]{0:T(1024)S(1)} %mul.156, ...), kind=kOutput, calls=%fused_computation.4 | convolution fusion | flops 4990500864 | bytes 34370048 | tf_op jit(solution)/shard_map/dot_general | solution.py:32
  265.1 5.3 fusion.59
  275.8 3.3 convert_reduce_fusion.2
  279.1 18.1 %convert_reduce_fusion = (f32[4096]{0:T(1024)}, bf16[576,4096]{1,0:T(8,128)(2,1)}) fusion(f32[576,4096]{1,0:T(8,128)} %get-tuple-element.62, bf16[4096,1024]{1,0:T(8,128)(2,1)} %bitcast.145, f32[576,1024]{1,0:T(8,128)S(1)} %get-tuple-element.58, f32[576,4096]{1,0:T(8,128)} %get-tuple-element.75, f32[4096]{0:T(1024)S(1)} %copy-done.30), kind=kOutput, calls=%fused_computation.2 | convolution fusion | flops 4872531968 | bytes 34373632 | tf_op jit(solution)/shard_map/dot_general | solution.py:42
  297.2 10.3 %multiply_reduce_fusion = (f32[1024]{0:T(1024)}, f32[576]{0:T(1024)S(1)}, f32[576]{0:T(1024)S(1)}, f32[1024]{0:T(1024)}, f32[576,1024]{1,0:T(8,128)S(1)}) fusion(f32[576,1024]{1,0:T(8,128)S(1)} %copy-done.4, f32[576]{0:T(1024)S(1)} %copy-done.26, f32[576]{0:T(1024)S(1)} %broadcast_multiply_fusion.5, f32[1024]{0:T(1024)S(1)} %copy-done.23, ...), kind=kOutput, calls=%fused_computation.50 | convolution fusion | flops 4837733376 | bytes 20206592 | tf_op jit(solution)/shard_map/dot_general | solution.py:42
  318.3 5.2 convolution_convert_fusion.3
  323.5 11.8 %convolution_convert_fusion = bf16[1024,4096]{1,0:T(8,128)(2,1)} fusion(bf16[576,4096]{1,0:T(8,128)(2,1)} %get-tuple-element.80, f32[576,1024]{1,0:T(8,128)S(1)} %copy-done.4, f32[1024]{0:T(1024)S(1)} %copy-done.32, f32[1024]{0:T(1024)S(1)} %copy-done.24, f32[576]{0:T(1024)S(1)} %copy-done.27, f32[576]{0:T(1024)S(1)} %copy-done.21), kind=kOutput, calls=%fused_computation.23 | convolution fusion | flops 4838981632 | bytes 15479296 | tf_op jit(solution)/shard_map/dot_general | solution.py:36
  338.1 11.7 %convolution_convert_fusion.1 = bf16[4096,1024]{1,0:T(8,128)(2,1)} fusion(bf16[576,4096]{1,0:T(8,128)(2,1)} %copy-done.36, f32[576,1024]{1,0:T(8,128)} %copy-done.6), kind=kOutput, calls=%fused_computation.24 | convolution fusion | flops 4836622336 | bytes 15466496 | tf_op jit(solution)/shard_map/dot_general | solution.py:36
  349.8 23.2 %shard_map.206 = (bf16[1024,640]{1,0:T(8,128)(2,1)}, bf16[576,1024]{1,0:T(8,128)(2,1)}, bf16[576,1024]{1,0:T(8,128)(2,1)}, f32[5,16,576,128]{3,2,1,0:T(8,128)}) custom-call(bf16[576,1024]{1,0:T(8,128)(2,1)} %copy.35.value_ref, bf16[1024,640]{1,0:T(8,128)(2,1)} %copy.36.context_grad_t_ref, bf16[640,1024]{1,0:T(8,128)(2,1)} %get-tuple-element.68.context_grad_ref, ...), custom_call_target="tpu_custom_call" | custom-call | tf_op jit(solution)/shard_map/pallas_call | solution.py:545
  373.0 65.3 %shard_map.207 = f32[192,96]{1,0:T(8,128)} custom-call(bf16[576,6,640]{2,1,0:T(8,128)(2,1)} %pad.32.digit_ref, f32[5,16,576,128]{3,2,1,0:T(8,128)} %get-tuple-element.36.score_grad_ref), custom_call_target="tpu_custom_call" | custom-call | tf_op jit(solution)/shard_map/pallas_call | solution.py:619
  441.3 8.9 %add_bitcast_fusion = f32[1,576,1024]{2,1,0:T(8,128)} fusion(f32[576,1024]{1,0:T(8,128)S(1)} %copy-done.8, bf16[1024,3072]{1,0:T(8,128)(2,1)} %bitcast.150, bf16[576,1024]{1,0:T(8,128)(2,1)S(1)} %copy-done.10, bf16[576,1024]{1,0:T(8,128)(2,1)} %get-tuple-element.34, bf16[576,1024]{1,0:T(8,128)(2,1)S(1)} %slice_bitcast_fusion), kind=kOutput, calls=%fused_computation.55 | convolution fusion | flops 3635085312 | bytes 14548992 | tf_op jit(solution)/shard_map/dot_general | solution.py:42
  452.5 9.4 %convolution_convert_fusion.2 = bf16[3072,1024]{0,1:T(8,128)(2,1)} fusion(bf16[576,1024]{1,0:T(8,128)(2,1)S(1)} %copy-done.10, bf16[576,1024]{1,0:T(8,128)(2,1)} %get-tuple-element.34, bf16[576,1024]{1,0:T(8,128)(2,1)S(1)} %copy-done.12, bf16[1,576,1024]{2,1,0:T(8,128)(2,1)} %param.13), kind=kOutput, calls=%fused_computation.30 | convolution fusion | flops 3637641216 | bytes 11010048 | tf_op jit(solution)/shard_map/dot_general | solution.py:36
  461.9 116.1 %shard_map.208 = (f32[32,3072]{1,0:T(8,128)}, f32[32,1024]{1,0:T(8,128)}, f32[32,4096]{1,0:T(8,128)}, f32[128,1024]{1,0:T(8,128)}, f32[8,128]{1,0:T(8,128)}) custom-call(bf16[4,2,2,2,32,3072]{5,4,3,2,1,0:T(8,128)(2,1)} %bitcast.123, bf16[4,2,2,2,32,1024]{5,4,3,2,1,0:T(8,128)(2,1)} %bitcast.125, bf16[4,2,2,2,32,4096]{5,4,3,2,1,0:T(8,128)(2,1)} %bitcast.121, ...), custom_call_target="tpu_custom_call" | custom-call | tf_op jit(solution)/shard_map/pallas_call | solution.py:395
  (175 shorter events, 58.8 us)
Async XLA Ops:
  49.2 126.5 %copy-start.35 = (bf16[1,576,1024]{2,1,0:T(8,128)(2,1)S(1)}, bf16[1,576,1024]{2,1,0:T(8,128)(2,1)}, u32[]{:S(2)}) copy-start(bf16[1,576,1024]{2,1,0:T(8,128)(2,1)} %param.13) | copy-start | bytes 3538948
  171.1 63.2 %copy-start.29 = (f32[4096]{0:T(1024)}, f32[4096]{0:T(1024)S(1)}, u32[]{:S(2)}) copy-start(f32[4096]{0:T(1024)S(1)} %fusion.33) | copy-start | bytes 49156
  172.5 92.6 %copy-start.22 = (f32[1024]{0:T(1024)}, f32[1024]{0:T(1024)S(1)}, u32[]{:S(2)}) copy-start(f32[1024]{0:T(1024)S(1)} %mul.156) | copy-start | bytes 12292
  172.6 92.5 %copy-start.31 = (f32[1024]{0:T(1024)}, f32[1024]{0:T(1024)S(1)}, u32[]{:S(2)}) copy-start(f32[1024]{0:T(1024)S(1)} %add.130) | copy-start | bytes 12292
  186.1 7.3 %copy-start.1 = (bf16[576,1024]{0,1:T(8,128)(2,1)}, bf16[576,1024]{0,1:T(8,128)(2,1)S(1)}, u32[]{:S(2)}) copy-start(bf16[576,1024]{0,1:T(8,128)(2,1)S(1)} %get-tuple-element.64) | copy-start | bytes 3538948
  194.9 35.6 %copy-start.33 = (bf16[4,2,2,2,32,1024]{5,4,3,2,1,0:T(8,128)(2,1)S(1)}, bf16[4,2,2,2,32,1024]{5,4,3,2,1,0:T(8,128)(2,1)}, u32[]{:S(2)}) copy-start(bf16[4,2,2,2,32,1024]{5,4,3,2,1,0:T(8,128)(2,1)} %get-tuple-element.29) | copy-start | bytes 6291460
  230.4 34.6 %slice-start.2 = ((s8[8388608]{0:T(1024)(128)(4,1)}), s8[4194304]{0:T(1024)(128)(4,1)S(1)}, s32[]{:S(2)}) async-start(s8[8388608]{0:T(1024)(128)(4,1)} %bitcast.146), calls=%async_computation.2 | async-start | bytes 8388608
  233.9 31.2 %copy-start.3 = (f32[576,1024]{1,0:T(8,128)}, f32[576,1024]{1,0:T(8,128)S(1)}, u32[]{:S(2)}) copy-start(f32[576,1024]{1,0:T(8,128)S(1)} %get-tuple-element.74) | copy-start | bytes 7077892
  233.9 73.6 %copy-start.20 = (f32[576]{0:T(1024)}, f32[576]{0:T(1024)S(1)}, u32[]{:S(2)}) copy-start(f32[576]{0:T(1024)S(1)} %broadcast_multiply_fusion.5) | copy-start | bytes 6916
  234.6 30.4 %copy-start.25 = (f32[576]{0:T(1024)}, f32[576]{0:T(1024)S(1)}, u32[]{:S(2)}) copy-start(f32[576]{0:T(1024)S(1)} %add_rsqrt_fusion.1) | copy-start | bytes 6916
  234.6 30.5 %slice-start.3 = ((s8[8388608]{0:T(1024)(128)(4,1)}), s8[4194304]{0:T(1024)(128)(4,1)S(1)}, s32[]{:S(2)}) async-start(s8[8388608]{0:T(1024)(128)(4,1)} %bitcast.146), calls=%async_computation.3 | async-start | bytes 8388608
  279.1 18.1 %copy-start.6 = (f32[576,1024]{1,0:T(8,128)}, f32[576,1024]{1,0:T(8,128)S(1)}, u32[]{:S(2)}) copy-start(f32[576,1024]{1,0:T(8,128)S(1)} %get-tuple-element.58) | copy-start | bytes 7077892
  279.1 18.1 %copy-start.4 = (f32[576,1024]{1,0:T(8,128)S(1)}, f32[576,1024]{1,0:T(8,128)}, u32[]{:S(2)}) copy-start(f32[576,1024]{1,0:T(8,128)} %copy-done.3) | copy-start | bytes 7077892
  279.1 18.1 %copy-start.23 = (f32[1024]{0:T(1024)S(1)}, f32[1024]{0:T(1024)}, u32[]{:S(2)}) copy-start(f32[1024]{0:T(1024)} %copy-done.22) | copy-start | bytes 12292
  279.1 18.1 %copy-start.26 = (f32[576]{0:T(1024)S(1)}, f32[576]{0:T(1024)}, u32[]{:S(2)}) copy-start(f32[576]{0:T(1024)} %copy-done.25) | copy-start | bytes 6916
  309.1 5.6 copy-start.19
  373.0 65.3 %copy-start.9 = (bf16[1024,640]{1,0:T(8,128)(2,1)S(1)}, bf16[1024,640]{1,0:T(8,128)(2,1)}, u32[]{:S(2)}) copy-start(bf16[1024,640]{1,0:T(8,128)(2,1)} %get-tuple-element.33) | copy-start | bytes 3932164
  441.3 8.9 %copy-start.11 = (bf16[576,1024]{1,0:T(8,128)(2,1)}, bf16[576,1024]{1,0:T(8,128)(2,1)S(1)}, u32[]{:S(2)}) copy-start(bf16[576,1024]{1,0:T(8,128)(2,1)S(1)} %slice_bitcast_fusion) | copy-start | bytes 3538948
  441.3 9.3 %copy-start.15 = (f32[1,32,32]{2,0,1:T(1,128)S(1)}, f32[1,32,32]{2,0,1:T(1,128)}, u32[]{:S(2)}) copy-start(f32[1,32,32]{2,0,1:T(1,128)} %stack.38) | copy-start | bytes 12292
  441.3 9.3 %copy-start.16 = (f32[1,32,32]{2,0,1:T(1,128)S(1)}, f32[1,32,32]{2,0,1:T(1,128)}, u32[]{:S(2)}) copy-start(f32[1,32,32]{2,0,1:T(1,128)} %stack.35) | copy-start | bytes 12292
  441.3 9.3 %copy-start.17 = (f32[1,32,32]{2,0,1:T(1,128)S(1)}, f32[1,32,32]{2,0,1:T(1,128)}, u32[]{:S(2)}) copy-start(f32[1,32,32]{2,0,1:T(1,128)} %stack.36) | copy-start | bytes 12292
  441.3 9.3 %copy-start.18 = (f32[1,32,32]{2,0,1:T(1,128)S(1)}, f32[1,32,32]{2,0,1:T(1,128)}, u32[]{:S(2)}) copy-start(f32[1,32,32]{2,0,1:T(1,128)} %stack.37) | copy-start | bytes 12292
  441.3 9.6 %copy-start.14 = (f32[192,96]{1,0:T(8,128)S(1)}, f32[192,96]{1,0:T(8,128)}, u32[]{:S(2)}) copy-start(f32[192,96]{1,0:T(8,128)} %shard_map.207) | copy-start | bytes 221188
  578.0 9.6 %copy-start.13 = (f32[128,1024]{1,0:T(8,128)S(1)}, f32[128,1024]{1,0:T(8,128)}, u32[]{:S(2)}) copy-start(f32[128,1024]{1,0:T(8,128)} %get-tuple-element.98) | copy-start | bytes 1572868
  (17 other events, 54.5 us)

commit v2 on v1

--- a/solution.py
+++ b/solution.py
@@ -1,5 +1,6 @@
 import functools
 import itertools
+import typing
 
 import jax
 import jax.numpy as jnp
@@ -21,9 +22,9 @@
 GATHER_ORDERS = ((0, 2, 1), (0, 1, 2), (2, 1, 0))
 STEPS = 5
 LAG = 2
-SMALL_ROWS = 16
-SMALL_GRAD_ROWS = 8
 GRAD_TILE = 64
+ROWS_AT_ONCE = 16
+WINDOW_TILES = 3
 HIGH_PARTS = 4
 LOW_PARTS = NB // HIGH_PARTS
 
@@ -109,58 +110,71 @@
     return sum(DIMS[axis] - 1 for axis in order[:phase])
 
 
-def gather_steps(wave, number, full, send, recv, place, core):
+def gather_steps(wave, number, full, outs, send, recv, out_sem, place, core):
     array, row, rows, bounds = wave
     whole = full[array]
     routes = [r for r in range(len(GATHER_ORDERS)) if bounds[r + 1] > bounds[r]]
     total_hops = hops_before(GATHER_ORDERS[0], 3)
-    started = []
-    arriving = {}
-    from_core = []
 
     def copy(route, slot, index, target):
         part = whole.at[
             index[0], index[1], index[2], core,
             pl.ds(row, rows), pl.ds(bounds[route], bounds[route + 1] - bounds[route]),
         ]
-        made = pltpu.make_async_remote_copy(
+        return pltpu.make_async_remote_copy(
             part, part, send.at[number, route, slot], recv.at[number, route, slot],
             device_id=target, device_id_type=MESH,
         )
-        made.start()
-        started.append(made)
-        return made
-
-    def to_core(route, slot, index):
-        from_core.append(copy(route, total_hops + slot, index, device_at(place, 1 - core)))
+
+    def to_core(route, phase, distance):
+        if phase is None:
+            return copy(route, total_hops, list(place), device_at(place, 1 - core))
+        order = GATHER_ORDERS[route]
+        axis = order[phase]
+        index = list(place)
+        for done in order[:phase]:
+            index[done] = slice(None)
+        index[axis] = lax.rem(place[axis] + DIMS[axis] - distance, DIMS[axis])
+        slot = total_hops + hops_before(order, phase) + distance
+        return copy(route, slot, index, device_at(place, 1 - core))
+
+    def hop(route, phase, distance):
+        order = GATHER_ORDERS[route]
+        index = list(place)
+        for axis in order[:phase]:
+            index[axis] = slice(None)
+        return copy(
+            route, hops_before(order, phase) + distance - 1, index,
+            device_at(shifted(place, order[phase], distance), core),
+        )
+
+    def hops(phase):
+        return [
+            (route, phase, distance)
+            for route in routes
+            for distance in range(1, DIMS[GATHER_ORDERS[route][phase]])
+        ]
 
     def launch(phase):
-        for route in routes:
-            order = GATHER_ORDERS[route]
-            index = list(place)
-            for axis in order[:phase]:
-                index[axis] = slice(None)
-            for distance in range(1, DIMS[order[phase]]):
-                arriving[route, phase, distance] = copy(
-                    route, hops_before(order, phase) + distance - 1, index,
-                    device_at(shifted(place, order[phase], distance), core),
-                )
+        for which in hops(phase):
+            hop(*which).start()
 
     def land(phase):
-        for route in routes:
-            order = GATHER_ORDERS[route]
-            axis = order[phase]
-            for distance in range(1, DIMS[axis]):
-                arriving[route, phase, distance].wait_recv()
-                index = list(place)
-                for done in order[:phase]:
-                    index[done] = slice(None)
-                index[axis] = lax.rem(place[axis] + DIMS[axis] - distance, DIMS[axis])
-                to_core(route, 1 + hops_before(order, phase) + distance - 1, index)
+        for which in hops(phase):
+            hop(*which).wait_recv()
+            to_core(*which).start()
+
+    def out_copy():
+        part = (slice(None),) * 4 + (
+            pl.ds(row, rows), pl.ds(bounds[0], bounds[-1] - bounds[0]),
+        )
+        return pltpu.make_async_copy(
+            full[array].at[part], outs[array].at[part], out_sem.at[number]
+        )
 
     def first():
         for route in routes:
-            to_core(route, 0, list(place))
+            to_core(route, None, 0).start()
         launch(0)
 
     def second():
@@ -175,74 +189,499 @@
         land(2)
 
     def fifth():
-        for made in from_core:
-            made.wait_recv()
-        for made in started:
-            made.wait_send()
-
-    return [first, second, third, fourth, fifth]
-
-
-def gather_kernel(waves, arrays, *refs):
-    shards = refs[:arrays]
-    outs = refs[arrays : 2 * arrays]
-    local_sem, send, recv, out_sem = refs[2 * arrays : 2 * arrays + 4]
-    full = refs[2 * arrays + 4 :]
+        for route in routes:
+            to_core(route, None, 0).wait_recv()
+        for phase in range(3):
+            for which in hops(phase):
+                to_core(*which).wait_recv()
+        if array < len(outs):
+            out_copy().start()
+
+    def finish():
+        for route in routes:
+            to_core(route, None, 0).wait_send()
+        for phase in range(3):
+            for which in hops(phase):
+                hop(*which).wait_send()
+                to_core(*which).wait_send()
+        if array < len(outs):
+            out_copy().wait()
+
+    return [first, second, third, fourth, fifth, finish]
+
+
+def erf(values):
+    clipped = jnp.clip(values, -3.832506856900711, 3.832506856900711)
+    square = clipped * clipped
+    top = jnp.full_like(square, 0.00022905065861350646)
+    for term in (
+        0.0034082910107109506, 0.050955695062380861, 0.18520832239976145, 1.128379143519084,
+    ):
+        top = top * square + term
+    bottom = jnp.full_like(square, -1.1791602954361697e-7)
+    for term in (
+        0.000023547966471313185, 0.0010179625278914885, 0.014070470171167667,
+        0.11098505178285362, 0.49746925110067538, 1.0,
+    ):
+        bottom = bottom * square + term
+    return clipped * top / bottom
+
+
+def gelu_and_slope(hidden):
+    chance = 0.5 + 0.5 * erf(hidden * (0.5**0.5))
+    density = jnp.exp(-0.5 * hidden * hidden) * 0.3989422804014327
+    return hidden * chance, chance + hidden * density
+
+
+def norm_rows(inputs, gain_row, shift_row):
+    average = jnp.mean(inputs, axis=-1, keepdims=True)
+    centered = inputs - average
+    variance = jnp.mean(centered * centered, axis=-1, keepdims=True)
+    return centered * lax.rsqrt(variance + EPSILON) * gain_row + shift_row
+
+
+def attention_pair(pair_number, refs):
+    (
+        row_ref, qkv_ref, vector_ref, table_ref, packed_ref, mask_ref, score_ref, probs_ref,
+        query_ref, key_t_ref, value_ref, context_ref, context_t_ref,
+    ) = refs
+    length, width = row_ref.shape
+    padded = packed_ref.shape[1]
+    pair = 2 * width // H
+    half = pair // 2
+    scale = half ** (-0.5)
+    at = pl.multiple_of(pair_number * pair, pair)
+    mine = pl.ds(at, pair)
+    row_in = row_ref[...]
+
+    def project(part):
+        columns = pl.ds(pl.multiple_of(part * width + at, pair), pair)
+        return dot_plain(row_in, qkv_ref[:, columns])
+
+    queries = ((project(0) + vector_ref[0:1, mine]).astype(jnp.bfloat16)) * jnp.bfloat16(scale)
+    keys = project(1).astype(jnp.bfloat16)
+    values = (project(2) + vector_ref[1:2, mine]).astype(jnp.bfloat16)
+    query_ref[0:length, mine] = queries
+    query_ref[length:, mine] = jnp.zeros((padded - length, pair), jnp.bfloat16)
+    value_ref[:, mine] = values
+    queries_t = jnp.concatenate(
+        [queries.T, jnp.zeros((pair, padded - length), jnp.bfloat16)], axis=1
+    )
+    key_t_ref[mine, :] = keys.T
+    values_t = values.T
+    feature = lax.broadcasted_iota(jnp.int32, (pair, padded), 0)
+    zero = jnp.zeros_like(queries_t)
+    score_ref[0] = dot_plain(keys, jnp.where(feature < half, queries_t, zero))
+    score_ref[1] = dot_plain(keys, jnp.where(feature < half, zero, queries_t))
+    for column in range(0, padded, LANES):
+        lanes = slice(column, column + LANES)
+        rows = [table_ref[t, pair_number] for t in range(3)]
+        tops = [jnp.full((8, LANES), 3.0 * MASK_FILL, jnp.float32) for side in range(2)]
+        for start in range(0, length, 8):
+            here = slice(start, start + 8)
+            packed = packed_ref[here, lanes]
+            sums = [None, None]
+            for table in range(3):
+                index = (packed >> (7 * table)) & (NB - 1)
+                word = jnp.take_along_axis(rows[table], index, axis=1)
+                for side, term in ((0, word >> 16), (1, (word << 16) >> 16)):
+                    sums[side] = term if table == 0 else sums[side] + term
+            mask = mask_ref[here, lanes]
+            for side in range(2):
+                scores = score_ref[side, here, lanes] + (
+                    sums[side].astype(jnp.float32) * (1.0 / TABLE_STEP) + mask
+                )
+                score_ref[side, here, lanes] = scores
+                tops[side] = jnp.maximum(tops[side], scores)
+        for side in range(2):
+            top = jnp.max(tops[side], axis=0, keepdims=True)
+            exponent = jnp.exp(score_ref[side, :, lanes] - top)
+            total = jnp.sum(exponent, axis=0, keepdims=True)
+            probs_ref[side, :, lanes] = (exponent * (1.0 / total)).astype(jnp.bfloat16)
+    context_t = jnp.concatenate(
+        [
+            dot_plain(values_t[side * half : (side + 1) * half], probs_ref[side])
+            for side in range(2)
+        ],
+        axis=0,
+    ).astype(jnp.bfloat16)
+    context_t_ref[mine, :] = context_t
+    context_ref[:, mine] = context_t.T[0:length]
+
+
+class ForwardRefs(typing.NamedTuple):
+    w_qkv: typing.Any
+    w_out: typing.Any
+    w_in: typing.Any
+    w_down: typing.Any
+    small: typing.Any
+    row: typing.Any
+    buckets: typing.Any
+    segments_down: typing.Any
+    valid_down: typing.Any
+    segments_across: typing.Any
+    full_qkv: typing.Any
+    full_out: typing.Any
+    full_in: typing.Any
+    full_down: typing.Any
+    probs: typing.Any
+    context_t: typing.Any
+    queries: typing.Any
+    keys_t: typing.Any
+    values: typing.Any
+    first_sum: typing.Any
+    first_low: typing.Any
+    active_t: typing.Any
+    slope: typing.Any
+    second_sum: typing.Any
+    vectors: typing.Any
+    packed_t: typing.Any
+    h_qkv: typing.Any
+    h_out: typing.Any
+    h_in: typing.Any
+    h_down: typing.Any
+    h_small: typing.Any
+    s_row: typing.Any
+    s_buckets: typing.Any
+    s_packed: typing.Any
+    s_mask: typing.Any
+    s_score: typing.Any
+    s_probs: typing.Any
+    s_context: typing.Any
+    s_context_t: typing.Any
+    s_query: typing.Any
+    s_key_t: typing.Any
+    s_value: typing.Any
+    s_first: typing.Any
+    s_low: typing.Any
+    s_active: typing.Any
+    s_slope: typing.Any
+    s_active_t: typing.Any
+    s_second: typing.Any
+    s_vectors: typing.Any
+    s_hidden: typing.Any
+    s_tables: typing.Any
+    local_sem: typing.Any
+    send: typing.Any
+    recv: typing.Any
+    out_sem: typing.Any
+    probs_sem: typing.Any
+    slope_sem: typing.Any
+    active_sem: typing.Any
+    store_sem: typing.Any
+
+
+def forward_kernel(waves, starts, *refs):
+    r = ForwardRefs(*refs)
     place, core = coordinates()
+    shards = [r.w_qkv, r.w_out, r.w_in, r.w_down, r.small]
+    full = [r.h_qkv, r.h_out, r.h_in, r.h_down, r.h_small]
+    outs = [r.full_qkv, r.full_out, r.full_in, r.full_down]
+    length, width = r.s_row.shape
+    padded = r.s_packed.shape[1]
     own = [
         pltpu.make_async_copy(
-            shards[i], full[i].at[place[0], place[1], place[2], core], local_sem.at[i]
-        )
-        for i in range(arrays)
+            shards[i], full[i].at[place[0], place[1], place[2], core], r.local_sem.at[i]
+        )
+        for i in range(len(shards))
     ]
+    own.append(pltpu.make_async_copy(r.row, r.s_row, r.local_sem.at[5]))
+    own.append(pltpu.make_async_copy(r.buckets, r.s_buckets, r.local_sem.at[6]))
     for copy in own:
         copy.start()
     greet(place, core)
     steps = [
-        gather_steps(wave, number, full, send, recv, place, core)
+        gather_steps(wave, number, full, outs, r.send, r.recv, r.out_sem, place, core)
         for number, wave in enumerate(waves)
     ]
-    for copy in own:
+    for copy in own[:5]:
         copy.wait()
-    leaving = []
-    for number, step in schedule(len(waves), LAG):
-        steps[number][step]()
-        if step == STEPS - 1:
-            array, row, rows, bounds = waves[number]
-            part = (slice(None),) * 4 + (
-                pl.ds(row, rows), pl.ds(bounds[0], bounds[-1] - bounds[0]),
+    events = []
+    for number, (start, lag) in enumerate(starts):
+        for step in range(STEPS):
+            events.append((start + lag * step, number, step))
+    events.sort()
+    ready = max(e[0] for e in events if waves[e[1]][0] in (0, 4))
+    first_in = max(e[0] for e in events if waves[e[1]][0] in (0, 4, 1))
+
+    def communicate(low, high):
+        for slot, number, step in events:
+            if low <= slot < high:
+                steps[number][step]()
+
+    def prepare():
+        own[6].wait()
+        for table in range(3):
+            part = r.s_buckets[table] << (7 * table)
+            packed = part if table == 0 else packed | part
+        flipped = packed.T
+        r.s_packed[...] = jnp.concatenate(
+            [flipped, jnp.zeros((length, padded - length), jnp.int32)], axis=1
+        )
+        down = lax.broadcasted_iota(jnp.int32, (length, padded), 0)
+        across = lax.broadcasted_iota(jnp.int32, (length, padded), 1)
+        same = r.segments_down[...] == r.segments_across[...]
+        usable = (r.valid_down[...] > 0) | (down == across)
+        allowed = (same & usable) | (across >= length)
+        r.s_mask[...] = jnp.where(allowed, 0.0, MASK_FILL)
+
+    def spread():
+        devices = DIMS[0] * DIMS[1] * DIMS[2] * 2
+        piece = width // devices
+        group = LANES // piece
+        buckets_each = 3 * NB // devices
+        tables = [jnp.zeros((H, LANES), jnp.float32) for t in range(3)]
+        lane = lax.broadcasted_iota(jnp.int32, (H, LANES), 1)
+        for device in range(devices):
+            spot = (device // 8, (device // 4) % 2, (device // 2) % 2, device % 2)
+            block = r.h_small[spot].astype(jnp.float32)
+            mine = slice(device // group * LANES, (device // group + 1) * LANES)
+            if device % group == 0:
+                r.s_vectors[:, mine] = block[0:8]
+            else:
+                r.s_vectors[:, mine] = r.s_vectors[:, mine] + block[0:8]
+            r.s_hidden[:, device * LANES : (device + 1) * LANES] = block[8:9]
+            low, high = device * buckets_each, (device + 1) * buckets_each
+            for table in range(low // NB, (high - 1) // NB + 1):
+                inside = (lane >= low - table * NB) & (lane < high - table * NB)
+                tables[table] = tables[table] + jnp.where(inside, block[16:32], 0.0)
+        for table in range(3):
+            fixed = jnp.round(tables[table] * TABLE_STEP).astype(jnp.int32)
+            words = (fixed[0:8] << 16) | (fixed[8:16] & 0xFFFF)
+            for pair in range(H // 2):
+                r.s_tables[table, pair] = jnp.broadcast_to(words[pair : pair + 1], (8, LANES))
+
+    communicate(0, 1)
+    prepare()
+    communicate(1, ready + 1)
+    spread()
+    own[5].wait()
+    vectors = pltpu.make_async_copy(r.s_vectors, r.vectors, r.store_sem.at[0])
+    vectors.start()
+    qkv_view = r.h_qkv.reshape(width, 3 * width)
+
+    def probs_copy(pair_number, slot):
+        return pltpu.make_async_copy(
+            r.s_probs.at[slot], r.probs.at[pl.ds(2 * pair_number, 2)],
+            r.probs_sem.at[slot],
+        )
+
+    def one_pair(pair_number, carry):
+        for number in range(H // 2):
+            slot = ready + 1 + number
+            if any(e[0] == slot for e in events):
+                @pl.when(pair_number == number)
+                def talk(slot=slot):
+                    communicate(slot, slot + 1)
+
+        slot = lax.rem(pair_number, 2)
+
+        @pl.when(pair_number >= 2)
+        def free():
+            probs_copy(pair_number - 2, slot).wait()
+
+        attention_pair(
+            pair_number,
+            (
+                r.s_row, qkv_view, r.s_vectors, r.s_tables, r.s_packed,
+                r.s_mask, r.s_score, r.s_probs.at[slot], r.s_query, r.s_key_t,
+                r.s_value, r.s_context, r.s_context_t,
+            ),
+        )
+        probs_copy(pair_number, slot).start()
+        return carry
+
+    pairs = H // 2
+    lax.fori_loop(0, pairs, one_pair, 0)
+    now = ready + 1 + pairs
+    stores = [vectors]
+
+    def store(scratch, out, number):
+        made = pltpu.make_async_copy(scratch, out, r.store_sem.at[number])
+        made.start()
+        stores.append(made)
+
+    store(r.s_context_t, r.context_t, 1)
+    store(r.s_query, r.queries, 2)
+    for part in range(padded // LANES):
+        store(r.s_packed.at[:, part * LANES : (part + 1) * LANES], r.packed_t.at[part], 9 + part)
+    store(r.s_key_t, r.keys_t, 3)
+    store(r.s_value, r.values, 4)
+    if first_in >= now:
+        communicate(now, first_in + 1)
+        now = first_in + 1
+    out_view = r.h_out.reshape(width, width)
+    tile = length // 3
+
+    def one_out(number, carry):
+        rows = pl.ds(pl.multiple_of(number * tile, tile), tile)
+        first = (
+            r.s_row[rows, :].astype(jnp.float32)
+            + dot_plain(r.s_context[rows, :], out_view[...])
+            + r.s_vectors[2:3, :]
+        )
+        r.s_first[rows, :] = first
+        normed = norm_rows(first, r.s_vectors[6:7, :], r.s_vectors[4:5, :])
+        r.s_low[rows, :] = normed.astype(jnp.bfloat16)
+        r.s_second[rows, :] = normed + r.s_vectors[3:4, :]
+        return carry
+
+    lax.fori_loop(0, 3, one_out, 0)
+    store(r.s_first, r.first_sum, 5)
+    store(r.s_low, r.first_low, 6)
+    hidden_units = r.s_active.shape[1]
+    in_view = r.h_in.reshape(width, hidden_units)
+    chunk = r.s_slope.shape[2]
+
+    def slope_copy(number, slot):
+        return pltpu.make_async_copy(
+            r.s_slope.at[slot],
+            r.slope.at[:, pl.ds(pl.multiple_of(number * chunk, chunk), chunk)],
+            r.slope_sem.at[slot],
+        )
+
+    def active_copy(number, slot):
+        return pltpu.make_async_copy(
+            r.s_active_t.at[slot],
+            r.active_t.at[pl.ds(pl.multiple_of(number * chunk, chunk), chunk)],
+            r.active_sem.at[slot],
+        )
+
+    def one_in(number, carry):
+        columns = pl.ds(pl.multiple_of(number * chunk, chunk), chunk)
+        slot = lax.rem(number, 2)
+
+        @pl.when(number >= 2)
+        def free():
+            slope_copy(number - 2, slot).wait()
+            active_copy(number - 2, slot).wait()
+
+        hidden = dot_plain(r.s_low[...], in_view[:, columns]) + r.s_hidden[:, columns]
+        active, slope = gelu_and_slope(hidden)
+        active_low = active.astype(jnp.bfloat16)
+        r.s_active[:, columns] = active_low
+        r.s_active_t[slot] = active_low.T
+        active_copy(number, slot).start()
+        r.s_slope[slot] = slope.astype(jnp.bfloat16)
+        slope_copy(number, slot).start()
+        return carry
+
+    in_waves = [(w[3][-1], number) for number, w in enumerate(waves) if w[0] == 2]
+    done = 0
+    for edge, number in in_waves:
+        arrived = starts[number][0] + starts[number][1] * (STEPS - 1)
+        if arrived >= now:
+            communicate(now, arrived + 1)
+            now = arrived + 1
+        lax.fori_loop(done, edge // chunk, one_in, 0)
+        done = edge // chunk
+    last = events[-1][0]
+    down_view = r.h_down.reshape(hidden_units, width)
+    for number, wave in enumerate(waves):
+        if wave[0] == 3:
+            arrived = starts[number][0] + starts[number][1] * (STEPS - 1)
+            if arrived >= now:
+                communicate(now, arrived + 1)
+                now = arrived + 1
+            columns = slice(wave[3][0], wave[3][-1])
+            r.s_second[:, columns] = r.s_second[:, columns] + dot_plain(
+                r.s_active[...], down_view[:, columns]
             )
-            out = pltpu.make_async_copy(
-                full[array].at[part], outs[array].at[part], out_sem.at[number]
-            )
-            out.start()
-            leaving.append(out)
-    for out in leaving:
-        out.wait()
-
-
-def gather_all(shards, waves, collective):
-    arrays = len(shards)
+    store(r.s_second, r.second_sum, 8)
+    for pair_number in (pairs - 2, pairs - 1):
+        probs_copy(pair_number, pair_number % 2).wait()
+    chunks = hidden_units // chunk
+    for number in (chunks - 2, chunks - 1):
+        slope_copy(number, number % 2).wait()
+        active_copy(number, number % 2).wait()
+    for wave_steps in steps:
+        wave_steps[STEPS]()
+    for made in stores:
+        made.wait()
+
+
+def forward_all(shards, small, row_in, buckets, segments, validity, waves, starts, collective):
+    length, width = row_in.shape
+    padded = -(-length // LANES) * LANES
+    hidden_units = shards[2].shape[1]
+    chunk = 256
     routes = len(GATHER_ORDERS)
     hops = 2 * hops_before(GATHER_ORDERS[0], 3) + 1
+    low = jnp.bfloat16
+    shape = jax.ShapeDtypeStruct
+    anywhere = pl.BlockSpec(memory_space=pl.ANY)
+    in_vmem = pl.BlockSpec(memory_space=pltpu.VMEM)
+    whole = [shape(DIMS + (2,) + shard.shape, shard.dtype) for shard in shards + [small]]
+    outs = whole[:4] + [
+        shape((H, length, padded), low),
+        shape((width, padded), low),
+        shape((padded, width), low),
+        shape((width, length), low),
+        shape((length, width), low),
+        shape((length, width), jnp.float32),
+        shape((length, width), low),
+        shape((hidden_units, length), low),
+        shape((length, hidden_units), low),
+        shape((length, width), jnp.float32),
+        shape((8, width), jnp.float32),
+        shape((padded // LANES, length, LANES), jnp.int32),
+    ]
+    scratch = [pltpu.VMEM(one.shape, one.dtype) for one in whole] + [
+        pltpu.VMEM((length, width), low),
+        pltpu.VMEM((3, length, length), jnp.int32),
+        pltpu.VMEM((length, padded), jnp.int32),
+        pltpu.VMEM((length, padded), jnp.float32),
+        pltpu.VMEM((2, length, padded), jnp.float32),
+        pltpu.VMEM((2, 2, length, padded), low),
+        pltpu.VMEM((length, width), low),
+        pltpu.VMEM((width, padded), low),
+        pltpu.VMEM((padded, width), low),
+        pltpu.VMEM((width, length), low),
+        pltpu.VMEM((length, width), low),
+        pltpu.VMEM((length, width), jnp.float32),
+        pltpu.VMEM((length, width), low),
+        pltpu.VMEM((length, hidden_units), low),
+        pltpu.VMEM((2, length, chunk), low),
+        pltpu.VMEM((2, chunk, length), low),
+        pltpu.VMEM((length, width), jnp.float32),
+        pltpu.VMEM((8, width), jnp.float32),
+        pltpu.VMEM((1, hidden_units), jnp.float32),
+        pltpu.VMEM((3, H // 2, 8, LANES), jnp.int32),
+        pltpu.SemaphoreType.DMA((7,)),
+        pltpu.SemaphoreType.DMA((len(waves), routes, hops)),
+        pltpu.SemaphoreType.DMA((len(waves), routes, hops)),
+        pltpu.SemaphoreType.DMA((len(waves),)),
+        pltpu.SemaphoreType.DMA((2,)),
+        pltpu.SemaphoreType.DMA((2,)),
+        pltpu.SemaphoreType.DMA((2,)),
+        pltpu.SemaphoreType.DMA((9 + padded // LANES,)),
+    ]
+    across = jnp.pad(segments, (0, padded - length))[None, :]
     return pl.pallas_call(
-        functools.partial(gather_kernel, waves, arrays),
-        in_specs=[pl.BlockSpec(memory_space=pl.ANY)] * arrays,
-        out_specs=[pl.BlockSpec(memory_space=pl.ANY)] * arrays,
-        out_shape=[
-            jax.ShapeDtypeStruct(DIMS + (2,) + shard.shape, shard.dtype) for shard in shards
-        ],
-        scratch_shapes=[
-            pltpu.SemaphoreType.DMA((arrays,)),
-            pltpu.SemaphoreType.DMA((len(waves), routes, hops)),
-            pltpu.SemaphoreType.DMA((len(waves), routes, hops)),
-            pltpu.SemaphoreType.DMA((len(waves),)),
-        ]
-        + [pltpu.VMEM(DIMS + (2,) + shard.shape, shard.dtype) for shard in shards],
+        functools.partial(forward_kernel, waves, starts),
+        in_specs=[anywhere] * 7 + [in_vmem] * 3,
+        out_specs=[anywhere] * len(outs),
+        out_shape=outs,
+        scratch_shapes=scratch,
         compiler_params=pltpu.CompilerParams(
             collective_id=collective, has_side_effects=True, vmem_limit_bytes=VMEM_BYTES
         ),
-    )(*shards)
+    )(*shards, small, row_in, buckets, segments[:, None], validity[:, None], across)
+
+
+def small_block(device, vec_bias, norm_gain, bias_hidden, rel_tables):
+    piece = vec_bias.shape[1]
+    group = LANES // piece
+    lane = jnp.arange(LANES)
+    tiled = jnp.tile(jnp.concatenate([vec_bias, norm_gain], axis=0), (1, group))
+    placed = jnp.where(lane // piece == device % group, tiled, jnp.zeros_like(tiled))
+    hidden = jnp.pad(bias_hidden[None, :], ((0, 7), (0, 0)))
+    heads_first = rel_tables.reshape(-1, H).T
+    buckets_each = heads_first.shape[1]
+    wanted = (lane - device * buckets_each) % NB
+    choose = (wanted[None, :] == jnp.arange(buckets_each)[:, None]).astype(jnp.bfloat16)
+    tables = dot_plain(jnp.concatenate([heads_first[0::2], heads_first[1::2]], axis=0), choose)
+    return jnp.concatenate([placed, hidden, tables.astype(jnp.bfloat16)], axis=0)
 
 
 def reduce_orders():
@@ -269,11 +708,9 @@
     return shapes
 
 
-def scatter_steps(wave, number, grads, outs, scratch, local_sem, send, recv, place, core):
+def scatter_steps(wave, number, source, out, scratch, own_sem, send, recv, place, core):
     array, row, rows, bounds = wave
-    grad = grads[array]
     base = bounds[0]
-    width = bounds[-1] - base
     total = next(scratch)
     other = next(scratch)
     orders = reduce_orders()
@@ -283,54 +720,47 @@
         for phase in range(3):
             landing[route, phase] = next(scratch)
     core_slot = hops_before(orders[0], 3)
-    started = []
-    arriving = {}
     every = slice(None)
 
-    def half(which):
-        return grad.at[:, :, :, which, pl.ds(row, rows), pl.ds(base, width)]
-
-    def first():
-        arriving["own"] = pltpu.make_async_copy(half(core), total, local_sem.at[number])
-        arriving["own"].start()
-        made = pltpu.make_async_remote_copy(
-            half(1 - core), other, send.at[number, 0, core_slot], recv.at[number, 0, core_slot],
+    def own_copy():
+        return pltpu.make_async_copy(source.at[:, :, :, core], total, own_sem.at[number])
+
+    def core_copy():
+        return pltpu.make_async_remote_copy(
+            source.at[:, :, :, 1 - core], other,
+            send.at[number, 0, core_slot], recv.at[number, 0, core_slot],
             device_id=device_at(place, 1 - core), device_id_type=MESH,
         )
-        made.start()
-        started.append(made)
-        arriving["core"] = made
+
+    def hop(route, phase, distance):
+        order = orders[route]
+        axis = order[phase]
+        index = [every] * 3
+        for done in order[:phase]:
+            index[done] = place[done]
+        index[axis] = lax.rem(place[axis] + distance, DIMS[axis])
+        slot = hops_before(order, phase) + distance - 1
+        return pltpu.make_async_remote_copy(
+            total.at[
+                index[0], index[1], index[2], :,
+                pl.ds(bounds[route] - base, bounds[route + 1] - bounds[route]),
+            ],
+            landing[route, phase].at[distance - 1],
+            send.at[number, route, slot], recv.at[number, route, slot],
+            device_id=device_at(shifted(place, axis, distance), core), device_id_type=MESH,
+        )
 
     def launch(phase):
         for route in routes:
-            order = orders[route]
-            axis = order[phase]
-            for distance in range(1, DIMS[axis]):
-                index = [every] * 3
-                for done in order[:phase]:
-                    index[done] = place[done]
-                index[axis] = lax.rem(place[axis] + distance, DIMS[axis])
-                slot = hops_before(order, phase) + distance - 1
-                made = pltpu.make_async_remote_copy(
-                    total.at[
-                        index[0], index[1], index[2], :,
-                        pl.ds(bounds[route] - base, bounds[route + 1] - bounds[route]),
-                    ],
-                    landing[route, phase].at[distance - 1],
-                    send.at[number, route, slot], recv.at[number, route, slot],
-                    device_id=device_at(shifted(place, axis, distance), core),
-                    device_id_type=MESH,
-                )
-                made.start()
-                started.append(made)
-                arriving[route, phase, distance] = made
+            for distance in range(1, DIMS[orders[route][phase]]):
+                hop(route, phase, distance).start()
 
     def land(phase):
         for route in routes:
             order = orders[route]
             axis = order[phase]
             for distance in range(1, DIMS[axis]):
-                arriving[route, phase, distance].wait_recv()
+                hop(route, phase, distance).wait_recv()
             left = axes_left(order, phase)
             columns = slice(bounds[route] - base, bounds[route + 1] - base)
             for spot in itertools.product(*[range(DIMS[a]) for a in left]):
@@ -342,13 +772,17 @@
                 for distance in range(1, DIMS[axis]):
                     added += landing[route, phase][(distance - 1,) + spot].astype(jnp.float32)
                 if phase == 2:
-                    outs[array][pl.ds(row, rows), bounds[route] : bounds[route + 1]] = added
+                    out[pl.ds(row, rows), bounds[route] : bounds[route + 1]] = added
                 else:
                     total[at] = added.astype(total.dtype)
 
+    def first():
+        own_copy().start()
+        core_copy().start()
+
     def second():
-        arriving["own"].wait()
-        arriving["core"].wait_recv()
+        own_copy().wait()
+        core_copy().wait()
 
         def one_plane(plane, carry):
             for y, x in itertools.product(range(DIMS[1]), range(DIMS[2])):
@@ -368,51 +802,869 @@
 
     def fifth():
         land(2)
-        for made in started:
-            made.wait_send()
+        for route in routes:
+            for phase in range(3):
+                for distance in range(1, DIMS[orders[route][phase]]):
+                    hop(route, phase, distance).wait_send()
 
     return [first, second, third, fourth, fifth]
 
 
-def scatter_kernel(waves, arrays, *refs):
-    grads = refs[:arrays]
-    outs = refs[arrays : 2 * arrays]
-    local_sem, send, recv = refs[2 * arrays : 2 * arrays + 3]
-    scratch = iter(refs[2 * arrays + 3 :])
+SCATTER_AFTER = (0, 1, 3, 5, 7)
+
+
+def step_runner(steps, starts):
+    events = sorted(
+        (start + SCATTER_AFTER[step], number, step)
+        for number, start in enumerate(starts)
+        for step in range(STEPS)
+    )
+
+    def communicate(slot):
+        for when, number, step in events:
+            if when == slot:
+                steps[number][step]()
+
+    return communicate, events[-1][0]
+
+
+def store_blocks(target, product, rows):
+    planes = product.shape[0] // rows
+    for block in range(planes):
+        spot = (block // 8, (block // 4) % 2, (block // 2) % 2, block % 2)
+        target[spot] = product[block * rows : (block + 1) * rows].astype(target.dtype)
+
+
+def fold_rows(values):
+    total = values[0:8]
+    for start in range(8, values.shape[0], 8):
+        total = total + values[start : start + 8]
+    return total
+
+
+def norm_rows_backward(inputs, gain_row, upstream):
+    average = jnp.mean(inputs, axis=-1, keepdims=True)
+    centered = inputs - average
+    spread = lax.rsqrt(jnp.mean(centered * centered, axis=-1, keepdims=True) + EPSILON)
+    normed = centered * spread
+    scaled = upstream * gain_row
+    grad = spread * (
+        scaled
+        - jnp.mean(scaled, axis=-1, keepdims=True)
+        - normed * jnp.mean(scaled * normed, axis=-1, keepdims=True)
+    )
+    return grad, normed
+
+
+def attention_pair_backward(refs):
+    (
+        value_ref, context_grad_t_ref, context_grad_ref, query_ref, key_t_ref, probs_ref,
+        grads_ref, score_grad_ref, prob_grad_ref, low_ref,
+    ) = refs
+    length, pair = value_ref.shape
+    padded = context_grad_t_ref.shape[1]
+    half = pair // 2
+    scale = half ** (-0.5)
+    feature = lax.broadcasted_iota(jnp.int32, (pair, padded), 0)
+    upstream = context_grad_t_ref[...]
+    zero = jnp.zeros_like(upstream)
+    prob_grad_ref[0] = dot_plain(value_ref[...], jnp.where(feature < half, upstream, zero))
+    prob_grad_ref[1] = dot_plain(value_ref[...], jnp.where(feature < half, zero, upstream))
+    for part in range(padded // LANES):
+        lanes = slice(part * LANES, (part + 1) * LANES)
+        for side in range(2):
+            probs = probs_ref[side, :, lanes].astype(jnp.float32)
+            prob_grad = prob_grad_ref[side, :, lanes]
+            inner = jnp.sum(probs * prob_grad, axis=0, keepdims=True)
+            score_grad = probs * (prob_grad - inner)
+            score_grad_ref[part, side] = score_grad
+            low_ref[side, :, lanes] = score_grad.astype(jnp.bfloat16)
+    grad_query_t = jnp.concatenate(
+        [
+            dot_plain(key_t_ref[side * half : (side + 1) * half, :], low_ref[side])
+            for side in range(2)
+        ],
+        axis=0,
+    )
+    grads_ref[0] = (grad_query_t * scale).astype(jnp.bfloat16).T[0:length]
+    first_half = lax.broadcasted_iota(jnp.int32, (length, pair), 1) < half
+    grad_key = [dot_plain(low_ref[side], query_ref[...]) for side in range(2)]
+    grads_ref[1] = jnp.where(first_half, grad_key[0], grad_key[1]).astype(jnp.bfloat16)
+    grad_value = [dot_plain(probs_ref[side], context_grad_ref[...]) for side in range(2)]
+    grads_ref[2] = jnp.where(first_half, grad_value[0], grad_value[1]).astype(jnp.bfloat16)
+
+
+class FeedInputs(typing.NamedTuple):
+    full_in: typing.Any
+    full_down: typing.Any
+    full_out: typing.Any
+    second_sum: typing.Any
+    cotangent: typing.Any
+    first_sum: typing.Any
+    first_low: typing.Any
+    active_t: typing.Any
+    slope: typing.Any
+    probs: typing.Any
+    queries: typing.Any
+    keys_t: typing.Any
+    values: typing.Any
+    vectors: typing.Any
+
+
+class FeedOutputs(typing.NamedTuple):
+    shard_in: typing.Any
+    shard_down: typing.Any
+    output: typing.Any
+    grad_first_sum: typing.Any
+    branch_grad: typing.Any
+    grad_mixed: typing.Any
+    score_grad: typing.Any
+    sums: typing.Any
+    hidden_sums: typing.Any
+
+
+class FeedRefs(typing.NamedTuple):
+    full_in: typing.Any
+    full_down: typing.Any
+    full_out: typing.Any
+    second_sum: typing.Any
+    cotangent: typing.Any
+    first_sum: typing.Any
+    first_low: typing.Any
+    active_t: typing.Any
+    slope: typing.Any
+    probs: typing.Any
+    queries: typing.Any
+    keys_t: typing.Any
+    values: typing.Any
+    vectors: typing.Any
+    shard_in: typing.Any
+    shard_down: typing.Any
+    output: typing.Any
+    grad_first_sum: typing.Any
+    branch_grad: typing.Any
+    grad_mixed: typing.Any
+    score_grad: typing.Any
+    sums: typing.Any
+    hidden_sums: typing.Any
+    own_sem: typing.Any
+    send: typing.Any
+    recv: typing.Any
+    load_sem: typing.Any
+    store_sem: typing.Any
+    chunk_sem: typing.Any
+    probs_sem: typing.Any
+    grads_sem: typing.Any
+    score_sem: typing.Any
+    s_stage: typing.Any
+    s_in: typing.Any
+    s_down: typing.Any
+    s_grad: typing.Any
+    s_low: typing.Any
+    s_vectors: typing.Any
+    s_sums: typing.Any
+    s_hidden: typing.Any
+    s_branch: typing.Any
+
+
+def feed_backward_kernel(waves, *refs):
+    r = FeedRefs(*refs[: len(FeedRefs._fields)])
+    buffers = refs[len(FeedRefs._fields) :]
     place, core = coordinates()
+    length, width = r.s_low.shape
+    hidden_units = r.s_hidden.shape[1]
+    padded = r.probs.shape[2]
+    chunk = 512
+    down_waves = sum(wave[0] == 1 for wave in waves)
+    loads = {}
+
+    def load(source, target, number):
+        made = pltpu.make_async_copy(source, target, r.load_sem.at[number])
+        made.start()
+        loads[number] = made
+
+    load(r.vectors, r.s_vectors, 0)
     greet(place, core)
-    steps = [
-        scatter_steps(wave, number, grads, outs, scratch, local_sem, send, recv, place, core)
-        for number, wave in enumerate(waves)
+    counts = [len(scatter_scratch([wave], [jnp.bfloat16] * 2)) for wave in waves]
+    offsets = [sum(counts[:number]) for number in range(len(waves))]
+
+    def steps_of(number, stage):
+        mine = iter(buffers[offsets[number] : offsets[number] + counts[number]])
+        return scatter_steps(
+            waves[number], number, stage,
+            r.s_down if waves[number][0] == 1 else r.s_in, mine,
+            r.own_sem, r.send, r.recv, place, core,
+        )
+
+    steps = [None] * len(waves)
+    for number in range(down_waves, len(waves)):
+        steps[number] = steps_of(number, r.s_stage.at[number % 2])
+    communicate, last = step_runner(steps, list(range(len(waves))))
+    stores = []
+
+    def store(scratch, out, number):
+        made = pltpu.make_async_copy(scratch, out, r.store_sem.at[number])
+        made.start()
+        stores.append(made)
+        return made
+
+    loads[0].wait()
+    gains = [r.s_vectors[6:7, :], r.s_vectors[7:8, :]]
+    tile = 32
+    nothing = jnp.zeros((8, width), jnp.float32)
+
+    def feed_phase(
+        s_second, s_cot, s_out, s_active, s_low_rows, s_low_t, s_wd, s_wi, s_slope, s_stage_down
+    ):
+        for number in range(down_waves):
+            steps[number] = steps_of(number, s_stage_down.at[number % 2])
+        load(r.second_sum, s_second, 2)
+        load(r.cotangent, s_cot, 3)
+        load(r.active_t, s_active, 4)
+        load(r.first_low, s_low_rows, 5)
+
+        def chunk_copies(number, slot):
+            columns = pl.ds(pl.multiple_of(number * chunk, chunk), chunk)
+            return [
+                pltpu.make_async_copy(
+                    r.full_down.at[columns], s_wd.at[slot], r.chunk_sem.at[slot, 0]
+                ),
+                pltpu.make_async_copy(
+                    r.full_in.at[:, columns], s_wi.at[slot], r.chunk_sem.at[slot, 1]
+                ),
+                pltpu.make_async_copy(
+                    r.slope.at[:, columns], s_slope.at[slot], r.chunk_sem.at[slot, 2]
+                ),
+            ]
+
+        for copy in chunk_copies(0, 0):
+            copy.start()
+        loads[2].wait()
+        loads[3].wait()
+
+        def one_norm(number, carry):
+            rows = pl.ds(pl.multiple_of(number * tile, tile), tile)
+            upstream = s_cot[rows, :].astype(jnp.float32)
+            grad, normed = norm_rows_backward(s_second[rows, :], gains[1], upstream)
+            s_out[rows, :] = (normed * gains[1] + r.s_vectors[5:6, :]).astype(jnp.bfloat16)
+            r.s_grad[rows, :] = grad
+            low = grad.astype(jnp.bfloat16)
+            r.s_low[rows, :] = low
+            return (
+                carry[0] + fold_rows(low.astype(jnp.float32)),
+                carry[1] + fold_rows(upstream),
+                carry[2] + fold_rows(upstream * normed),
+            )
+
+        sums = lax.fori_loop(0, length // tile, one_norm, (nothing, nothing, nothing))
+        for row, total in zip((3, 5, 7), sums):
+            r.s_sums[row : row + 1, :] = jnp.sum(total, axis=0, keepdims=True)
+        store(s_out, r.output, 0)
+        loads[4].wait()
+        rows_each = waves[0][2]
+        spots = list(itertools.product(range(DIMS[1]), range(DIMS[2]), range(2)))
+
+        def to_stage(stage, plane, product, rows, columns):
+            for block, spot in enumerate(spots):
+                stage[(plane,) + spot + (slice(None), columns)] = product[
+                    block * rows : (block + 1) * rows
+                ].astype(jnp.bfloat16)
+
+        for number in range(down_waves):
+            columns = slice(waves[number][3][0], waves[number][3][-1])
+
+            def one_down(plane, carry, number=number, columns=columns):
+                size = len(spots) * rows_each
+                units = pl.ds(pl.multiple_of(plane * size, size), size)
+                product = dot_plain(s_active[units, :], r.s_low[:, columns])
+                to_stage(
+                    s_stage_down.at[number % 2], plane, product, rows_each, slice(None)
+                )
+                return carry
+
+            lax.fori_loop(0, DIMS[0], one_down, 0)
+            communicate(number)
+        loads[5].wait()
+        s_low_t[...] = s_low_rows[...].T
+        in_rows = waves[down_waves][2]
+        per_wave = (waves[down_waves][3][-1] - waves[down_waves][3][0]) // chunk
+        for number in range(down_waves, len(waves)):
+
+            def one_piece(piece, carry, number=number):
+                index = (number - down_waves) * per_wave + piece
+                slot = lax.rem(index, 2)
+
+                @pl.when(index + 1 < hidden_units // chunk)
+                def fetch():
+                    for copy in chunk_copies(index + 1, 1 - slot):
+                        copy.start()
+
+                for copy in chunk_copies(index, slot):
+                    copy.wait()
+                hidden_grad = dot_last(r.s_low[...], s_wd[slot]) * s_slope[slot].astype(
+                    jnp.float32
+                )
+                low = hidden_grad.astype(jnp.bfloat16)
+                here = pl.ds(pl.multiple_of(index * chunk, chunk), chunk)
+                r.s_hidden[:, here] = jnp.sum(
+                    low.astype(jnp.float32), axis=0, keepdims=True
+                )
+                there = pl.ds(pl.multiple_of(piece * chunk, chunk), chunk)
+                size = len(spots) * in_rows
+                for plane in range(DIMS[0]):
+                    product = dot_plain(s_low_t[plane * size : (plane + 1) * size, :], low)
+                    to_stage(r.s_stage.at[number % 2], plane, product, in_rows, there)
+                r.s_grad[...] = r.s_grad[...] + dot_last(low, s_wi[slot])
+                return carry
+
+            lax.fori_loop(0, per_wave, one_piece, 0)
+            communicate(number)
+        stores[0].wait()
+
+    bf, full32 = jnp.bfloat16, jnp.float32
+    pl.run_scoped(
+        feed_phase,
+        pltpu.VMEM((length, width), full32),
+        pltpu.VMEM((length, width), bf),
+        pltpu.VMEM((length, width), bf),
+        pltpu.VMEM((hidden_units, length), bf),
+        pltpu.VMEM((length, width), bf),
+        pltpu.VMEM((width, length), bf),
+        pltpu.VMEM((2, chunk, width), bf),
+        pltpu.VMEM((2, width, chunk), bf),
+        pltpu.VMEM((2, length, chunk), bf),
+        pltpu.VMEM((2,) + DIMS + (2, waves[0][2], waves[0][3][-1] - waves[0][3][0]), bf),
+    )
+    now = len(waves)
+    pairs = H // 2
+    pair = width // pairs
+
+    def norm_phase(s_first):
+        load(r.first_sum, s_first, 1)
+        loads[1].wait()
+
+        def one_norm(number, carry):
+            rows = pl.ds(pl.multiple_of(number * tile, tile), tile)
+            upstream = r.s_grad[rows, :]
+            grad, normed = norm_rows_backward(s_first[rows, :], gains[0], upstream)
+            r.s_grad[rows, :] = grad
+            low = grad.astype(jnp.bfloat16)
+            r.s_branch[rows, :] = low
+            return (
+                carry[0] + fold_rows(low.astype(jnp.float32)),
+                carry[1] + fold_rows(upstream),
+                carry[2] + fold_rows(upstream * normed),
+            )
+
+        sums = lax.fori_loop(0, length // tile, one_norm, (nothing, nothing, nothing))
+        for row, total in zip((2, 4, 6), sums):
+            r.s_sums[row : row + 1, :] = jnp.sum(total, axis=0, keepdims=True)
+
+    pl.run_scoped(norm_phase, pltpu.VMEM((length, width), full32))
+    store(r.s_grad, r.grad_first_sum, 1)
+    store(r.s_branch, r.branch_grad, 2)
+    communicate(now)
+
+    def attention_phase(
+        s_wout, s_context_grad, s_context_grad_t, s_query, s_key_t, s_value, s_probs, s_prob_grad,
+        s_low, s_score, s_grads,
+    ):
+        load(r.full_out, s_wout, 6)
+        load(r.queries, s_query, 7)
+        load(r.keys_t, s_key_t, 8)
+        load(r.values, s_value, 9)
+
+        def probs_copy(number, slot):
+            return pltpu.make_async_copy(
+                r.probs.at[pl.ds(2 * number, 2)], s_probs.at[slot], r.probs_sem.at[slot]
+            )
+
+        def score_copy(number, slot):
+            return pltpu.make_async_copy(
+                s_score.at[slot], r.score_grad.at[:, pl.ds(2 * number, 2)],
+                r.score_sem.at[slot],
+            )
+
+        def grads_copy(number, slot, part):
+            columns = pl.ds(pl.multiple_of(part * width + number * pair, pair), pair)
+            return pltpu.make_async_copy(
+                s_grads.at[slot, part], r.grad_mixed.at[:, columns],
+                r.grads_sem.at[slot, part],
+            )
+
+        probs_copy(0, 0).start()
+        loads[6].wait()
+        s_context_grad[length:, :] = jnp.zeros((padded - length, width), bf)
+        s_context_grad[0:length, :] = dot_last(r.s_branch[...], s_wout[...]).astype(bf)
+        s_context_grad_t[...] = s_context_grad[...].T
+        communicate(now + 1)
+        for number in (7, 8, 9):
+            loads[number].wait()
+
+        def one_pair(number, carry):
+            slot = lax.rem(number, 2)
+            probs_copy(number, slot).wait()
+
+            @pl.when(number + 1 < pairs)
+            def fetch():
+                probs_copy(number + 1, 1 - slot).start()
+
+            @pl.when(number >= 2)
+            def free():
+                score_copy(number - 2, slot).wait()
+                for part in range(3):
+                    grads_copy(number - 2, slot, part).wait()
+
+            mine = pl.ds(pl.multiple_of(number * pair, pair), pair)
+            attention_pair_backward(
+                (
+                    s_value.at[:, mine], s_context_grad_t.at[mine], s_context_grad.at[:, mine],
+                    s_query.at[:, mine], s_key_t.at[mine], s_probs.at[slot], s_grads.at[slot],
+                    s_score.at[slot], s_prob_grad, s_low,
+                )
+            )
+            for row, part in ((0, 0), (1, 2)):
+                r.s_sums[row : row + 1, mine] = jnp.sum(
+                    s_grads[slot, part].astype(full32), axis=0, keepdims=True
+                )
+            score_copy(number, slot).start()
+            for part in range(3):
+                grads_copy(number, slot, part).start()
+            for turn in range(pairs):
+                if now + 2 + turn <= last:
+                    @pl.when(number == turn)
+                    def talk(turn=turn):
+                        communicate(now + 2 + turn)
+
+            return carry
+
+        lax.fori_loop(0, pairs, one_pair, 0)
+        for number in (pairs - 2, pairs - 1):
+            score_copy(number, number % 2).wait()
+            for part in range(3):
+                grads_copy(number, number % 2, part).wait()
+
+    pl.run_scoped(
+        attention_phase,
+        pltpu.VMEM((width, width), bf),
+        pltpu.VMEM((padded, width), bf),
+        pltpu.VMEM((width, padded), bf),
+        pltpu.VMEM((padded, width), bf),
+        pltpu.VMEM((width, length), bf),
+        pltpu.VMEM((length, width), bf),
+        pltpu.VMEM((2, 2, length, padded), bf),
+        pltpu.VMEM((2, length, padded), full32),
+        pltpu.VMEM((2, length, padded), bf),
+        pltpu.VMEM((2, padded // LANES, 2, length, LANES), full32),
+        pltpu.VMEM((2, 3, length, pair), bf),
+    )
+    for slot in range(now + 2 + pairs, last + 1):
+        communicate(slot)
+    store(r.s_sums, r.sums, 3)
+    store(r.s_hidden, r.hidden_sums, 4)
+    store(r.s_in, r.shard_in, 5)
+    store(r.s_down, r.shard_down, 6)
+    for made in stores[1:]:
+        made.wait()
+
+
+def feed_backward(inputs, in_shape, down_shape, collective):
+    length, width = inputs.first_sum.shape
+    hidden_units = inputs.slope.shape[1]
+    padded = inputs.probs.shape[2]
+    bf, full32 = jnp.bfloat16, jnp.float32
+    shape = jax.ShapeDtypeStruct
+    anywhere = pl.BlockSpec(memory_space=pl.ANY)
+    waves = even_waves(1, down_shape, 2, (1, 1, 0)) + weight_waves(0, in_shape[0], in_shape[1], in_shape[0], 8)
+    outs = [
+        shape(in_shape, full32),
+        shape(down_shape, full32),
+        shape((length, width), bf),
+        shape((length, width), full32),
+        shape((length, width), bf),
+        shape((length, 3 * width), bf),
+        shape((padded // LANES, H, length, LANES), full32),
+        shape((8, width), full32),
+        shape((1, hidden_units), full32),
     ]
-    for number, step in schedule(len(waves), LAG):
-        steps[number][step]()
-
-
-def scatter_all(grads, waves, collective):
-    arrays = len(grads)
     sems = (len(waves), len(GATHER_ORDERS), hops_before(GATHER_ORDERS[0], 3) + 1)
-    return pl.pallas_call(
-        functools.partial(scatter_kernel, waves, arrays),
-        in_specs=[pl.BlockSpec(memory_space=pl.ANY)] * arrays,
-        out_specs=[pl.BlockSpec(memory_space=pltpu.VMEM)] * arrays,
-        out_shape=[jax.ShapeDtypeStruct(grad.shape[4:], jnp.float32) for grad in grads],
-        scratch_shapes=[
-            pltpu.SemaphoreType.DMA((len(waves),)),
-            pltpu.SemaphoreType.DMA(sems),
-            pltpu.SemaphoreType.DMA(sems),
-        ]
-        + scatter_scratch(waves, [grad.dtype for grad in grads]),
+    dma = pltpu.SemaphoreType.DMA
+    scratch = [
+        dma((len(waves),)), dma(sems), dma(sems), dma((10,)), dma((7,)), dma((2, 3)), dma((2,)),
+        dma((2, 3)), dma((2,)),
+        pltpu.VMEM((2,) + DIMS + (2, in_shape[0], waves[-1][3][-1] - waves[-1][3][0]), bf),
+        pltpu.VMEM(in_shape, full32),
+        pltpu.VMEM(down_shape, full32),
+        pltpu.VMEM((length, width), full32),
+        pltpu.VMEM((length, width), bf),
+        pltpu.VMEM((8, width), full32),
+        pltpu.VMEM((8, width), full32),
+        pltpu.VMEM((1, hidden_units), full32),
+        pltpu.VMEM((length, width), bf),
+    ] + scatter_scratch(waves, [bf, bf])
+    results = pl.pallas_call(
+        functools.partial(feed_backward_kernel, waves),
+        in_specs=[anywhere] * len(inputs),
+        out_specs=[anywhere] * len(outs),
+        out_shape=outs,
+        scratch_shapes=scratch,
         compiler_params=pltpu.CompilerParams(
             collective_id=collective, has_side_effects=True, vmem_limit_bytes=VMEM_BYTES
         ),
-    )(*grads)
+    )(*inputs)
+    return FeedOutputs(*results)
+
+
+class LastInputs(typing.NamedTuple):
+    row_in: typing.Any
+    grad_mixed: typing.Any
+    full_qkv: typing.Any
+    context_t: typing.Any
+    branch_grad: typing.Any
+    score_grad: typing.Any
+    packed_t: typing.Any
+    grad_first_sum: typing.Any
+    sums: typing.Any
+    hidden_sums: typing.Any
+    starts: typing.Any
+
+
+class LastOutputs(typing.NamedTuple):
+    shard_qkv: typing.Any
+    shard_out: typing.Any
+    shard_small: typing.Any
+    grad_input: typing.Any
+
+
+class LastRefs(typing.NamedTuple):
+    row_in: typing.Any
+    grad_mixed: typing.Any
+    full_qkv: typing.Any
+    context_t: typing.Any
+    branch_grad: typing.Any
+    score_grad: typing.Any
+    packed_t: typing.Any
+    grad_first_sum: typing.Any
+    sums: typing.Any
+    hidden_sums: typing.Any
+    starts: typing.Any
+    shard_qkv: typing.Any
+    shard_out: typing.Any
+    shard_small: typing.Any
+    grad_input: typing.Any
+    own_sem: typing.Any
+    send: typing.Any
+    recv: typing.Any
+    load_sem: typing.Any
+    store_sem: typing.Any
+    score_sem: typing.Any
+    s_stage: typing.Any
+    s_small: typing.Any
+    s_out_qkv: typing.Any
+    s_out_out: typing.Any
+    s_out_small: typing.Any
+    s_row: typing.Any
+    s_row_t: typing.Any
+    s_mixed: typing.Any
+    s_qkv: typing.Any
+    s_context_t: typing.Any
+    s_branch: typing.Any
+    s_packed: typing.Any
+    s_input: typing.Any
+    s_sums: typing.Any
+    s_hidden: typing.Any
+    s_score: typing.Any
+    s_work: typing.Any
+    s_product: typing.Any
+
+
+def last_backward_kernel(waves, *refs):
+    r = LastRefs(*refs[: len(LastRefs._fields)])
+    buffers = iter(refs[len(LastRefs._fields) :])
+    place, core = coordinates()
+    length, width = r.s_row.shape
+    padded = r.s_packed.shape[0] * LANES
+    rows_each = waves[0][2]
+    loads = {}
+    for number, (source, target) in enumerate(
+        (
+            (r.row_in, r.s_row), (r.grad_mixed, r.s_mixed), (r.context_t, r.s_context_t),
+            (r.branch_grad, r.s_branch), (r.packed_t, r.s_packed), (r.full_qkv, r.s_qkv),
+            (r.grad_first_sum, r.s_input), (r.sums, r.s_sums), (r.hidden_sums, r.s_hidden),
+        )
+    ):
+        loads[number] = pltpu.make_async_copy(source, target, r.load_sem.at[number])
+        loads[number].start()
+
+    def score_copy(block, slot):
+        rows = pl.ds(pl.multiple_of(block * GRAD_TILE, GRAD_TILE), GRAD_TILE)
+        return pltpu.make_async_copy(
+            r.score_grad.at[:, :, rows], r.s_score.at[slot], r.score_sem.at[slot]
+        )
+
+    score_copy(0, 0).start()
+    greet(place, core)
+    results = [r.s_out_qkv, r.s_out_out, r.s_out_small]
+    main = len(waves) - 1
+    steps = [
+        scatter_steps(
+            wave, number, r.s_small if number == main else r.s_stage.at[number % 2],
+            results[wave[0]], buffers, r.own_sem, r.send, r.recv, place, core,
+        )
+        for number, wave in enumerate(waves)
+    ]
+    communicate, last = step_runner(steps, list(range(main)))
+    spots = list(itertools.product(range(DIMS[1]), range(DIMS[2]), range(2)))
+    size = len(spots) * rows_each
+    loads[0].wait()
+    r.s_row_t[...] = r.s_row[...].T
+    loads[1].wait()
+    for number in range(main):
+        array, row, rows, bounds = waves[number]
+        columns = slice(bounds[0], bounds[-1])
+        if array == 1:
+            loads[2].wait()
+            loads[3].wait()
+
+        def one_plane(plane, carry, array=array, number=number, columns=columns):
+            units = pl.ds(pl.multiple_of(plane * size, size), size)
+            if array == 0:
+                product = dot_plain(r.s_row_t[units, :], r.s_mixed[:, columns])
+            else:
+                product = dot_plain(
+                    r.s_context_t[units, 0:length], r.s_branch[:, columns]
+                )
+            for block, spot in enumerate(spots):
+                r.s_stage[(number % 2, plane) + spot] = product[
+                    block * rows_each : (block + 1) * rows_each
+                ].astype(jnp.bfloat16)
+            return carry
+
+        lax.fori_loop(0, DIMS[0], one_plane, 0)
+        communicate(number)
+    loads[5].wait()
+    loads[6].wait()
+    strip = 256
+    for start in range(0, width, strip):
+        r.s_input[:, start : start + strip] = r.s_input[:, start : start + strip] + dot_last(
+            r.s_mixed[...], r.s_qkv[start : start + strip, :]
+        )
+    stored = pltpu.make_async_copy(r.s_input, r.grad_input, r.store_sem.at[0])
+    stored.start()
+    communicate(main)
+    loads[4].wait()
+    parts = padded // LANES
+    span = WINDOW_TILES * LANES
+    levels = lax.broadcasted_iota(jnp.int32, (LOW_PARTS, span), 0).astype(jnp.bfloat16)
+    one = jnp.ones((LOW_PARTS, span), jnp.bfloat16)
+    no_one = jnp.zeros((LOW_PARTS, span), jnp.bfloat16)
+    nothing = jnp.zeros((H, span), jnp.bfloat16)
+
+    def window(tiles, turn):
+        rolled = [pltpu.roll(one_tile, (LANES - turn) & (LANES - 1), 1) for one_tile in tiles]
+        kept = lax.broadcasted_iota(jnp.int32, tiles[0].shape, 1) < LANES - turn
+        return jnp.concatenate(
+            [jnp.where(kept, here, after) for here, after in zip(rolled[:-1], rolled[1:])],
+            axis=1,
+        )
+
+    def spread_digit(digit, rows):
+        as_float = digit.astype(jnp.float32)
+        low = jnp.concatenate([as_float, as_float], axis=0).astype(jnp.bfloat16)
+        return jnp.concatenate([low] * (rows // 16), axis=0)
+
+    r.s_product[...] = jnp.zeros(r.s_product.shape, jnp.float32)
+    blocks = length // GRAD_TILE
+
+    def one_block(block, carry):
+        slot = lax.rem(block, 2)
+
+        @pl.when(block + 1 < blocks)
+        def fetch():
+            score_copy(block + 1, 1 - slot).start()
+
+        score_copy(block, slot).wait()
+        r.s_work[...] = r.s_score[slot]
+        flat = r.s_work.reshape(parts * H * GRAD_TILE, LANES)
+
+        def one_group(group, total):
+            lefts = []
+            rights = []
+            for offset in range(ROWS_AT_ONCE):
+                row = group * ROWS_AT_ONCE + offset
+                begin = r.starts[block * GRAD_TILE + row]
+                tile = begin // LANES
+                turn = lax.rem(begin, LANES)
+                grads_parts = []
+                packed_parts = []
+                for part in range(WINDOW_TILES + 1):
+                    which = lax.rem(tile + part, parts)
+                    grads_parts.append(
+                        flat[pl.ds(which * H * GRAD_TILE + row, H, stride=GRAD_TILE), :]
+                    )
+                    packed_parts.append(
+                        jnp.broadcast_to(
+                            r.s_packed[which, pl.ds(block * GRAD_TILE + row, 1), :], (8, LANES)
+                        )
+                    )
+                grads = window(grads_parts, turn).astype(jnp.bfloat16)
+                packed = window(packed_parts, turn)
+                masked = []
+                onehot = []
+                for table in range(3):
+                    high = spread_digit((packed >> (7 * table + 5)) & (HIGH_PARTS - 1), H)
+                    for part in range(HIGH_PARTS):
+                        masked.append(jnp.where(high == jnp.bfloat16(part), grads, nothing))
+                    low = spread_digit((packed >> (7 * table)) & (LOW_PARTS - 1), LOW_PARTS)
+                    onehot.append(jnp.where(low == levels, one, no_one))
+                lefts.append(jnp.concatenate(masked, axis=0))
+                rights.append(jnp.concatenate(onehot, axis=0))
+            return total + dot_last(
+                jnp.concatenate(lefts, axis=1), jnp.concatenate(rights, axis=1)
+            )
+
+        total = lax.fori_loop(
+            0, GRAD_TILE // ROWS_AT_ONCE, one_group, jnp.zeros(r.s_product.shape, jnp.float32)
+        )
+        r.s_product[...] = r.s_product[...] + total
+        for turn in range(blocks):
+            if main + 1 + turn <= last:
+                @pl.when(block == turn)
+                def talk(turn=turn):
+                    communicate(main + 1 + turn)
+
+        return carry
+
+    lax.fori_loop(0, blocks, one_block, 0)
+    for slot in range(main + 1 + blocks, last + 1):
+        communicate(slot)
+    loads[7].wait()
+    loads[8].wait()
+    lane = lax.broadcasted_iota(jnp.int32, (H, LANES), 1)
+    product = jnp.concatenate(
+        [
+            r.s_product[...],
+            jnp.zeros((3 * HIGH_PARTS * H, LANES - 3 * LOW_PARTS), jnp.float32),
+        ],
+        axis=1,
+    )
+    tables = []
+    for table in range(3):
+        whole = jnp.zeros((H, LANES), jnp.float32)
+        for part in range(HIGH_PARTS):
+            start = (table * HIGH_PARTS + part) * H
+            turned = pltpu.roll(
+                product[start : start + H], ((part - table) * LOW_PARTS) % LANES, 1
+            )
+            inside = (lane >= part * LOW_PARTS) & (lane < (part + 1) * LOW_PARTS)
+            whole = jnp.where(inside, turned, whole)
+        tables.append(whole)
+    devices = DIMS[0] * DIMS[1] * DIMS[2] * 2
+    group = LANES // (width // devices)
+    buckets_each = 3 * NB // devices
+    empty = jnp.zeros((7, LANES), jnp.float32)
+    for device in range(devices):
+        spot = (device // 8, (device // 4) % 2, (device // 2) % 2, device % 2)
+        columns = slice(device // group * LANES, (device // group + 1) * LANES)
+        low = device * buckets_each
+        table = low // NB
+        mine = tables[table]
+        if (low + buckets_each - 1) // NB > table:
+            mine = jnp.where(lane >= low - table * NB, mine, tables[table + 1])
+        hidden = r.s_hidden[:, device * LANES : (device + 1) * LANES]
+        r.s_small[spot] = jnp.concatenate(
+            [r.s_sums[:, columns], hidden, empty, mine], axis=0
+        )
+    for step in steps[main]:
+        step()
+    stores = [stored]
+    for number, (source, target) in enumerate(
+        ((r.s_out_qkv, r.shard_qkv), (r.s_out_out, r.shard_out), (r.s_out_small, r.shard_small))
+    ):
+        stores.append(
+            pltpu.make_async_copy(source, target, r.store_sem.at[number + 1])
+        )
+        stores[-1].start()
+    for made in stores:
+        made.wait()
+
+
+def last_backward(inputs, qkv_shape, out_shape, collective):
+    length, width = inputs.row_in.shape
+    hidden_units = inputs.hidden_sums.shape[1]
+    padded = inputs.packed_t.shape[0] * LANES
+    bf, full32 = jnp.bfloat16, jnp.float32
+    shape = jax.ShapeDtypeStruct
+    anywhere = pl.BlockSpec(memory_space=pl.ANY)
+    small_rows = 16 + H
+    waves = weight_waves(0, qkv_shape[0], qkv_shape[1], qkv_shape[0], 8)
+    waves += weight_waves(1, out_shape[0], out_shape[1], out_shape[0], 8)
+    waves.append(wave_of(2, 0, small_rows, 0, 1, 0, 0))
+    outs = [
+        shape(qkv_shape, full32),
+        shape(out_shape, full32),
+        shape((small_rows, LANES), full32),
+        shape((length, width), full32),
+    ]
+    sems = (len(waves), len(GATHER_ORDERS), hops_before(GATHER_ORDERS[0], 3) + 1)
+    dma = pltpu.SemaphoreType.DMA
+    scratch = [
+        dma((len(waves),)), dma(sems), dma(sems), dma((9,)), dma((4,)), dma((2,)),
+        pltpu.VMEM((2,) + DIMS + (2, qkv_shape[0], waves[0][3][-1] - waves[0][3][0]), bf),
+        pltpu.VMEM(DIMS + (2, small_rows, LANES), full32),
+        pltpu.VMEM(qkv_shape, full32),
+        pltpu.VMEM(out_shape, full32),
+        pltpu.VMEM((small_rows, LANES), full32),
+        pltpu.VMEM((length, width), bf),
+        pltpu.VMEM((width, length), bf),
+        pltpu.VMEM((length, 3 * width), bf),
+        pltpu.VMEM((width, 3 * width), bf),
+        pltpu.VMEM((width, padded), bf),
+        pltpu.VMEM((length, width), bf),
+        pltpu.VMEM((padded // LANES, length, LANES), jnp.int32),
+        pltpu.VMEM((length, width), full32),
+        pltpu.VMEM((8, width), full32),
+        pltpu.VMEM((1, hidden_units), full32),
+        pltpu.VMEM((2, padded // LANES, H, GRAD_TILE, LANES), full32),
+        pltpu.VMEM((padded // LANES, H, GRAD_TILE, LANES), full32),
+        pltpu.VMEM((3 * HIGH_PARTS * H, 3 * LOW_PARTS), full32),
+    ] + scatter_scratch(waves, [bf, bf, full32])
+    results = pl.pallas_call(
+        functools.partial(last_backward_kernel, waves),
+        in_specs=[anywhere] * (len(inputs) - 1) + [pl.BlockSpec(memory_space=pltpu.SMEM)],
+        out_specs=[anywhere] * len(outs),
+        out_shape=outs,
+        scratch_shapes=scratch,
+        compiler_params=pltpu.CompilerParams(
+            collective_id=collective, has_side_effects=True, vmem_limit_bytes=VMEM_BYTES
+        ),
+    )(*inputs)
+    return LastOutputs(*results)
+
+
+def even_waves(array, shape, tiles, parts):
+    return [
+        wave_of(array, 0, shape[0], tile * LANES, *parts)
+        for tile in range(0, shape[1] // LANES, tiles)
+    ]
 
 
 def split_wave(array, row, rows, column, tiles, turn):
     edge = tiles // 8
     one = (tiles - edge + turn) // 2
     return wave_of(array, row, rows, column, one, tiles - edge - one, edge)
+
+
+def forward_plan(weights, small):
+    w_qkv, w_out, w_in, w_down = weights
+    waves = [wave_of(4, 0, small.shape[0], 0, 1, 0, 0)]
+    waves += weight_waves(0, w_qkv.shape[0], w_qkv.shape[1], w_qkv.shape[0], 8)
+    early = len(waves)
+    waves += weight_waves(1, w_out.shape[0], w_out.shape[1], w_out.shape[0], 8)
+    waves += weight_waves(2, w_in.shape[0], w_in.shape[1], w_in.shape[0], 8)
+    waves += even_waves(3, w_down.shape, 2, (1, 1, 0))
+    starts = [(number, 1) if number < early else (number, LAG) for number in range(len(waves))]
+    return waves, starts
 
 
 def weight_waves(array, rows, columns, row_step, tile_step):
@@ -647,25 +1899,80 @@
     return grad, jnp.sum(upstream * normed, axis=0), jnp.sum(upstream, axis=0)
 
 
-def small_piece(vec_bias, norm_gain, bias_hidden, rel_tables):
-    return jnp.concatenate(
+def spread_small(everything, vec_bias, norm_gain, bias_hidden):
+    devices = everything.shape[0]
+    vec_size, gain_size = vec_bias.size, norm_gain.size
+    vectors, gains, hidden, tables = jnp.split(
+        everything, [vec_size, vec_size + gain_size, vec_size + gain_size + bias_hidden.size], axis=1
+    )
+    vectors = jnp.transpose(vectors.reshape(devices, vec_bias.shape[0], -1), (1, 0, 2))
+    gains = jnp.transpose(gains.reshape(devices, norm_gain.shape[0], -1), (1, 0, 2))
+    rows = jnp.concatenate(
+        [vectors.reshape(vec_bias.shape[0], -1), gains.reshape(norm_gain.shape[0], -1)], axis=0
+    )
+    return rows.astype(jnp.float32), hidden.reshape(-1).astype(jnp.float32), tables.reshape(3, NB, H)
+
+
+def forward_by_ops(
+    weights, row_in, buckets, segments, validity, vec_bias, norm_gain, bias_hidden, rel_tables
+):
+    length, width = row_in.shape
+    padded = -(-length // LANES) * LANES
+    scale = (width // H) ** (-0.5)
+    full = [lax.all_gather(weight, BOTH, axis=0, tiled=True) for weight in weights]
+    small = jnp.concatenate(
         [vec_bias.reshape(-1), norm_gain.reshape(-1), bias_hidden, rel_tables]
     )
-
-
-def spread_small(everything, vec_rows, gain_rows, vec_size, gain_size, hidden_size):
-    devices = everything.shape[0]
-    vectors, gains, hidden, tables = jnp.split(
-        everything, [vec_size, vec_size + gain_size, vec_size + gain_size + hidden_size], axis=1
-    )
-    vectors = jnp.transpose(vectors.reshape(devices, vec_rows, -1), (1, 0, 2))
-    gains = jnp.transpose(gains.reshape(devices, gain_rows, -1), (1, 0, 2))
-    return (
-        vectors.reshape(vec_rows, -1).astype(jnp.float32),
-        gains.reshape(gain_rows, -1).astype(jnp.float32),
-        hidden.reshape(-1).astype(jnp.float32),
-        tables.reshape(3, NB, H),
-    )
+    everything = lax.all_gather(small, BOTH, axis=0, tiled=False)
+    vectors, hidden_bias, tables = spread_small(everything, vec_bias, norm_gain, bias_hidden)
+    wide = ((0, 0), (0, padded - length))
+    flipped = jnp.swapaxes(buckets, 1, 2)
+    packed = jnp.pad(flipped[0] | (flipped[1] << 7) | (flipped[2] << 14), wide)
+    position = jnp.arange(length)
+    allowed = (segments[:, None] == segments[None, :]) & (
+        (validity[:, None] > 0) | (position[:, None] == position[None, :])
+    )
+    mask = jnp.pad(jnp.where(allowed, 0.0, MASK_FILL), wide)
+    fixed = jnp.round(tables.astype(jnp.float32) * TABLE_STEP).astype(jnp.int32)
+    pair_tables = (fixed[:, :, 0::2] << 16) | (fixed[:, :, 1::2] & 0xFFFF)
+    pair_tables = jnp.transpose(pair_tables, (0, 2, 1))[:, :, None, :]
+    mixed = dot_plain(row_in, full[0])
+    queries = (mixed[:, :width] + vectors[0]).astype(jnp.bfloat16) * jnp.bfloat16(scale)
+    keys = mixed[:, width : 2 * width].astype(jnp.bfloat16)
+    values = (mixed[:, 2 * width :] + vectors[1]).astype(jnp.bfloat16)
+    queries = jnp.pad(queries, ((0, padded - length), (0, 0)))
+    probs, context_t = attention_forward(keys, queries.T, values.T, packed, pair_tables, mask)
+    branch = dot_first(context_t[:, :length], full[1])
+    first_sum = row_in.astype(jnp.float32) + branch + vectors[2]
+    normed_first = layer_norm(first_sum, vectors[6], vectors[4])
+    first_low = normed_first.astype(jnp.bfloat16)
+    hidden = dot_plain(first_low, full[2]) + hidden_bias
+    active, slope = gelu_and_slope(hidden)
+    active = active.astype(jnp.bfloat16)
+    second_sum = normed_first + dot_plain(active, full[3]) + vectors[3]
+    return full + [
+        probs, context_t, queries, keys.T, values, first_sum, first_low, active, slope,
+        second_sum, vectors, packed,
+    ]
+
+
+class Kept(typing.NamedTuple):
+    full_qkv: typing.Any
+    full_out: typing.Any
+    full_in: typing.Any
+    full_down: typing.Any
+    probs: typing.Any
+    context_t: typing.Any
+    queries: typing.Any
+    keys_t: typing.Any
+    values: typing.Any
+    first_sum: typing.Any
+    first_low: typing.Any
+    active_t: typing.Any
+    slope: typing.Any
+    second_sum: typing.Any
+    vectors: typing.Any
+    packed_t: typing.Any
 
 
 def body(
@@ -674,79 +1981,85 @@
 ):
     row_in = block_input[0]
     row_cot = cotangent[0].astype(jnp.float32)
-    segments = seg_ids[0]
-    validity = slot_valid[0]
-    buckets = rel_buckets[0]
     length, width = row_in.shape
-    padded = -(-length // LANES) * LANES
-    scale = (width // H) ** (-0.5)
     devices = lax.axis_size(BOTH)
     weights = [w_qkv, w_out, w_in, w_down]
-
-    small = small_piece(vec_bias, norm_gain, bias_hidden, rel_tables)
-    small_size = small.shape[0]
-    weight_plan = [
-        weight_waves(0, w_qkv.shape[0], w_qkv.shape[1], w_qkv.shape[0], 8),
-        weight_waves(1, w_out.shape[0], w_out.shape[1], w_out.shape[0], 8),
-        weight_waves(2, w_in.shape[0], w_in.shape[1], w_in.shape[0], 8),
-        weight_waves(3, w_down.shape[0], w_down.shape[1], 32, 8),
-    ]
     if own_kernels:
-        pad_to = SMALL_ROWS * LANES
-        small_block = jnp.pad(small, (0, pad_to - small_size)).reshape(SMALL_ROWS, LANES)
-        plan = [wave_of(4, 0, SMALL_ROWS, 0, 1, 0, 0)] + sum(weight_plan, [])
-        gathered = gather_all(weights + [small_block], plan, 1)
-        full_qkv, full_out, full_in, full_down = [
-            whole.reshape(-1, whole.shape[-1]) for whole in gathered[:4]
-        ]
-        everything = gathered[4].reshape(devices, pad_to)[:, :small_size]
+        device = lax.axis_index("dp") * 2 + lax.axis_index("fsdp")
+        small = small_block(device, vec_bias, norm_gain, bias_hidden, rel_tables)
+        waves, starts = forward_plan(weights, small)
+        forward = forward_all(
+            weights, small, row_in, rel_buckets[0], seg_ids[0], slot_valid[0], waves, starts, 1
+        )
+        forward = [whole.reshape(-1, whole.shape[-1]) for whole in forward[:4]] + list(forward[4:])
     else:
-        full_qkv, full_out, full_in, full_down = [
-            lax.all_gather(weight, BOTH, axis=0, tiled=True) for weight in weights
-        ]
-        everything = lax.all_gather(small, BOTH, axis=0, tiled=False)
-    vectors, gains, hidden_bias, tables = spread_small(
-        everything, vec_bias.shape[0], norm_gain.shape[0], vec_bias.size, norm_gain.size,
-        bias_hidden.size,
-    )
-
-    wide = ((0, 0), (0, padded - length))
-    buckets = jnp.swapaxes(buckets, 1, 2)
-    packed = jnp.pad(buckets[0] | (buckets[1] << 7) | (buckets[2] << 14), wide)
-    digits = jnp.concatenate([buckets // LOW_PARTS, buckets % LOW_PARTS], axis=0)
-    digits = jnp.pad(
-        jnp.transpose(digits.astype(jnp.bfloat16), (1, 0, 2)), ((0, 0),) + wide
-    )
-    position = jnp.arange(length)
-    allowed = (segments[:, None] == segments[None, :]) & (
-        (validity[:, None] > 0) | (position[:, None] == position[None, :])
-    )
-    mask = jnp.pad(jnp.where(allowed, 0.0, MASK_FILL), wide)
-    steps = jnp.round(tables.astype(jnp.float32) * TABLE_STEP).astype(jnp.int32)
-    pair_tables = (steps[:, :, 0::2] << 16) | (steps[:, :, 1::2] & 0xFFFF)
-    pair_tables = jnp.transpose(pair_tables, (0, 2, 1))[:, :, None, :]
-
-    mixed = dot_plain(row_in, full_qkv)
-    queries = (mixed[:, :width] + vectors[0]).astype(jnp.bfloat16) * jnp.bfloat16(scale)
-    keys = mixed[:, width : 2 * width].astype(jnp.bfloat16)
-    values = (mixed[:, 2 * width :] + vectors[1]).astype(jnp.bfloat16)
+        forward = forward_by_ops(
+            weights, row_in, rel_buckets[0], seg_ids[0], slot_valid[0], vec_bias, norm_gain,
+            bias_hidden, rel_tables,
+        )
+    if own_kernels:
+        kept = Kept(*forward)
+        fed = feed_backward(
+            FeedInputs(
+                kept.full_in, kept.full_down, kept.full_out, kept.second_sum, cotangent[0],
+                kept.first_sum, kept.first_low, kept.active_t, kept.slope, kept.probs,
+                kept.queries, kept.keys_t, kept.values, kept.vectors,
+            ),
+            w_in.shape, w_down.shape, 2,
+        )
+        segments = seg_ids[0]
+        starts = jnp.sum(segments[None, :] < segments[:, None], axis=1, dtype=jnp.int32)
+        done = last_backward(
+            LastInputs(
+                row_in, fed.grad_mixed, kept.full_qkv, kept.context_t, fed.branch_grad,
+                fed.score_grad, kept.packed_t, fed.grad_first_sum, fed.sums, fed.hidden_sums,
+                starts,
+            ),
+            w_qkv.shape, w_out.shape, 3,
+        )
+        small = done.shard_small
+        piece = vec_bias.shape[1]
+        vec_rows = vec_bias.shape[0]
+        sums = lax.dynamic_slice(
+            small, (0, device % (LANES // piece) * piece), (8, piece)
+        )
+        buckets_each = rel_tables.shape[0] // H
+        twice = jnp.concatenate([small[16:], small[16:]], axis=1)
+        tables = lax.dynamic_slice(twice, (0, device * buckets_each % NB), (H, buckets_each))
+        return (
+            fed.output[None],
+            done.grad_input[None],
+            done.shard_qkv,
+            done.shard_out,
+            fed.shard_in,
+            fed.shard_down,
+            sums[:vec_rows],
+            sums[vec_rows:],
+            small[8],
+            tables.T.reshape(-1),
+        )
+    (
+        full_qkv, full_out, full_in, full_down, probs, context_t, queries, keys_t, values,
+        first_sum, first_low, active, slope, second_sum, vectors, packed,
+    ) = forward
+    padded = packed.shape[1]
+    gains = vectors[6:8]
     taller = ((0, padded - length), (0, 0))
-    queries = jnp.pad(queries, taller)
-    probs, context_t = attention_forward(keys, queries.T, values.T, packed, pair_tables, mask)
     context_t = context_t[:, :length]
-    first_sum = row_in.astype(jnp.float32) + dot_first(context_t, full_out) + vectors[2]
-    normed_first = layer_norm(first_sum, gains[0], vectors[4])
-    first_low = normed_first.astype(jnp.bfloat16)
-    hidden = dot_plain(first_low, full_in) + hidden_bias
-    active = gelu_exact(hidden).astype(jnp.bfloat16)
-    second_sum = normed_first + dot_plain(active, full_down) + vectors[3]
+    digits = jnp.stack(
+        [
+            (packed >> (7 * t + shift)) & mask
+            for shift, mask in ((5, HIGH_PARTS - 1), (0, LOW_PARTS - 1))
+            for t in range(3)
+        ],
+        axis=1,
+    ).astype(jnp.bfloat16)
     output = layer_norm(second_sum, gains[1], vectors[5]).astype(jnp.bfloat16)
 
     grad_second, grad_gain_two, grad_shift_two = norm_backward(second_sum, gains[1], row_cot)
     down_grad = grad_second.astype(jnp.bfloat16)
     grad_w_down = dot_first(active, down_grad).astype(jnp.bfloat16)
-    unused, gelu_back = jax.vjp(gelu_exact, hidden)
-    hidden_grad = gelu_back(dot_last(down_grad, full_down))[0].astype(jnp.bfloat16)
+    hidden_grad = (dot_last(down_grad, full_down) * slope.astype(jnp.float32)).astype(jnp.bfloat16)
     grad_w_in = dot_first(first_low, hidden_grad).astype(jnp.bfloat16)
     grad_first = dot_last(hidden_grad, full_in) + grad_second
     grad_first_sum, grad_gain_one, grad_shift_one = norm_backward(first_sum, gains[0], grad_first)
@@ -754,7 +2067,7 @@
     grad_w_out = dot_plain(context_t, branch_grad).astype(jnp.bfloat16)
     context_grad = jnp.pad(dot_last(branch_grad, full_out).astype(jnp.bfloat16), taller)
     grad_queries_t, grad_keys, grad_values, score_grad = attention_backward(
-        values, context_grad.T, context_grad, queries, keys.T, probs
+        values, context_grad.T, context_grad, queries, keys_t, probs
     )
     grad_queries = grad_queries_t[:, :length].T
     grad_mixed = jnp.concatenate([grad_queries, grad_keys, grad_values], axis=1)
@@ -790,26 +2103,13 @@
         axis=1,
     )
     weight_grads = [grad_w_qkv, grad_w_out, grad_w_in, grad_w_down]
-    if own_kernels:
-        pad_to = SMALL_GRAD_ROWS * LANES
-        small_block = jnp.pad(small_grads, ((0, 0), (0, pad_to - small_size)))
-        blocks = [
-            grad.reshape(DIMS + (2,) + weight.shape) for grad, weight in zip(weight_grads, weights)
-        ] + [small_block.reshape(DIMS + (2, SMALL_GRAD_ROWS, LANES))]
-        plan = (
-            weight_plan[3] + weight_plan[2] + weight_plan[1] + weight_plan[0]
-            + [wave_of(4, 0, SMALL_GRAD_ROWS, 0, 1, 0, 0)]
-        )
-        shards = scatter_all(blocks, plan, 2)
-        small_shard = shards[4].reshape(-1)[:small_size]
-    else:
-        shards = [
-            lax.psum_scatter(
-                grad.astype(jnp.float32), BOTH, scatter_dimension=0, tiled=True
-            )
-            for grad in weight_grads
-        ]
-        small_shard = lax.psum_scatter(small_grads, BOTH, scatter_dimension=0, tiled=True)[0]
+    shards = [
+        lax.psum_scatter(
+            grad.astype(jnp.float32), BOTH, scatter_dimension=0, tiled=True
+        )
+        for grad in weight_grads
+    ]
+    small_shard = lax.psum_scatter(small_grads, BOTH, scatter_dimension=0, tiled=True)[0]
     shard_vectors, shard_gains, shard_hidden, shard_tables = jnp.split(
         small_shard,
         [

time: 596 us -> 365 us (0.61)
  matrix products: 123 us -> 0.25 us
  local copies, waits for them, and re-layouts: 59.5 us -> 15.5 us
  other arithmetic: 43.3 us -> 3.7 us
  Pallas kernels: 361 us -> 341 us
    dot_general x8 -> x0, matrix products: 75 us -> none  [the longest x4 38.7 us: dot_last(): lax.dot_general(left, right, (((1,), (1,)), ((), ())), preferred_element_...]
    dot_general x4 -> x1, matrix products: 48.4 us -> 0.25 us  [dot_plain(): return jnp.dot(left, right, preferred_element_type=jnp.float32)]
    pallas_call x5 -> x3, Pallas kernels: 361 us -> 341 us  [the longest x1 148 us: forward_all(): pl.pallas_call(functools.partial(forward_kernel, waves, starts), in_specs...]
    unnamed x93 -> x18, local copies, waits for them, and re-layouts: 23.5 us -> 5.43 us
    another operation x2 -> x0, other arithmetic: 11.8 us -> none
    or x2 -> x0, other arithmetic: 10.7 us -> none  [the longest x1 10 us: body(): packed = jnp.pad(buckets[0] | buckets[1] << 7 | buckets[2] << 14, wide)]
    pad x5 -> x1, local copies, waits for them, and re-layouts: 8.85 us -> 0.01 us  [forward_all(): across = jnp.pad(segments, (0, padded - length))[None, :]]
    reduce_sum x8 -> x1, other arithmetic: 8.83 us -> 0.92 us  [body(): jnp.sum(segments[None, :] < segments[:, None], axis=1, dtype=jnp.int32)]
where the time goes in v2:
time: 365 us; the launch traced here: 362 us
  Pallas kernels  341 us (93%)
  local copies, waits for them, and re-layouts  15.5 us (4%)
  other arithmetic  3.7 us (1%)
    pallas_call x1, Pallas kernels, forward_all(): pl.pallas_call(functools.partial(forward_kernel, waves, starts), in_specs...  148 us
    pallas_call x1, Pallas kernels, feed_backward(): pl.pallas_call(functools.partial(feed_backward_kernel, waves), in_specs=[...  110 us
    pallas_call x1, Pallas kernels, last_backward(): pl.pallas_call(functools.partial(last_backward_kernel, waves), in_specs=[...  83.3 us

profile of v2, /device:TPU:0, one launch (start us, length us, event | category | flops | bytes accessed | tf_op | source)
XLA Modules:
  0.0 361.6 jit_solution(11247015903728009436)
XLA Ops:
  0.7 0.7 pad_maximum_fusion
  1.4 0.7 reduce
  2.1 0.9 convert_reduce_fusion.refs_10_
  3.0 0.6 broadcast_in_dim.24.refs_9_
  3.6 0.7 reshape.58
  4.4 0.1 slice.20
  4.6 0.2 convolution_convert_fusion
  4.9 1.3 fusion.3.refs_4_
  6.2 1.6 copy.27.refs_8_
  7.7 1.6 copy.26.refs_7_
  9.3 148.1 %shard_map.204 = (bf16[4,2,2,2,32,3072]{5,4,3,2,1,0:T(8,128)(2,1)}, bf16[4,2,2,2,32,1024]{5,4,3,2,1,0:T(8,128)(2,1)}, bf16[4,2,2,2,32,4096]{5,4,3,2,1,0:T(8,128)...) custom-call(bf16[32,3072]{1,0:T(8,128)(2,1)} %refs_0_.1, ...), custom_call_target="tpu_custom_call" | custom-call | tf_op jit(solution)/shard_map/pallas_call | solution.py:660
  157.4 109.7 %shard_map.205 = (f32[32,4096]{1,0:T(8,128)}, f32[128,1024]{1,0:T(8,128)}, bf16[576,1024]{1,0:T(8,128)(2,1)}, f32[576,1024]{1,0:T(8,128)}, bf16[576,1024]{1,0:T(...) custom-call(bf16[1024,4096]{1,0:T(8,128)(2,1)} %bitcast.18, ...), custom_call_target="tpu_custom_call" | custom-call | tf_op jit(solution)/shard_map/pallas_call | solution.py:1305
  267.1 83.3 %shard_map.206 = (f32[32,3072]{1,0:T(8,128)}, f32[32,1024]{1,0:T(8,128)}, f32[32,128]{1,0:T(8,128)}, f32[576,1024]{1,0:T(8,128)}) custom-call(bf16[576,1024]{1,0:T(8,128)(2,1)} %bitcast.22, bf16[576,3072]{1,0:T(8,128)(2,1)} %get-tuple-element.53.refs_1_, bf16[1024,3072]{1,0:T(8,128)(2,1)} %bitcast.20, bf16[1024,640]{1,0:T(8,128)(2,1)} %get-tuple-element.55.refs_3_, ...), custom_call_target="tpu_custom_call" | custom-call | tf_op jit(solution)/shard_map/pallas_call | solution.py:1632
  350.5 1.3 slice_bitcast_fusion
  351.8 1.3 constant_dynamic-slice_fusion
  353.1 0.7 slice.24
  354.0 0.6 reshape.63
  354.6 1.2 slice.22
  355.9 1.0 copy.35
  356.9 1.4 copy.36
  358.3 0.7 copy.37
  359.1 0.7 copy.38
  359.7 0.8 copy.39
  360.5 0.8 copy.40
  (21 shorter events, 0.4 us)
Async XLA Ops:
  267.1 88.8 %copy-start.1 = (bf16[576,1024]{1,0:T(8,128)(2,1)S(1)}, bf16[576,1024]{1,0:T(8,128)(2,1)}, u32[]{:S(2)}) copy-start(bf16[576,1024]{1,0:T(8,128)(2,1)} %get-tuple-element.52) | copy-start | bytes 3538948
  350.4 6.5 %copy-start = (f32[576,1024]{1,0:T(8,128)S(1)}, f32[576,1024]{1,0:T(8,128)}, u32[]{:S(2)}) copy-start(f32[576,1024]{1,0:T(8,128)} %get-tuple-element.62) | copy-start | bytes 7077892
  356.9 1.4 copy-start.4
  356.9 2.2 copy-start.5
  356.9 2.8 copy-start.3
  358.3 2.2 copy-start.2

commit v3 on v2

--- a/solution.py
+++ b/solution.py
@@ -21,7 +21,7 @@
 DIMS = (4, 2, 2)
 GATHER_ORDERS = ((0, 2, 1), (0, 1, 2), (2, 1, 0))
 STEPS = 5
-LAG = 2
+LAG = 3
 GRAD_TILE = 64
 ROWS_AT_ONCE = 16
 WINDOW_TILES = 3
@@ -318,7 +318,6 @@
     row: typing.Any
     buckets: typing.Any
     segments_down: typing.Any
-    valid_down: typing.Any
     segments_across: typing.Any
     full_qkv: typing.Any
     full_out: typing.Any
@@ -420,8 +419,8 @@
         )
         down = lax.broadcasted_iota(jnp.int32, (length, padded), 0)
         across = lax.broadcasted_iota(jnp.int32, (length, padded), 1)
-        same = r.segments_down[...] == r.segments_across[...]
-        usable = (r.valid_down[...] > 0) | (down == across)
+        same = (r.segments_down[...] >> 1) == r.segments_across[...]
+        usable = ((r.segments_down[...] & 1) > 0) | (down == across)
         allowed = (same & usable) | (across >= length)
         r.s_mask[...] = jnp.where(allowed, 0.0, MASK_FILL)
 
@@ -532,6 +531,7 @@
     hidden_units = r.s_active.shape[1]
     in_view = r.h_in.reshape(width, hidden_units)
     chunk = r.s_slope.shape[2]
+    unit = r.active_t.shape[1]
 
     def slope_copy(number, slot):
         return pltpu.make_async_copy(
@@ -543,7 +543,7 @@
     def active_copy(number, slot):
         return pltpu.make_async_copy(
             r.s_active_t.at[slot],
-            r.active_t.at[pl.ds(pl.multiple_of(number * chunk, chunk), chunk)],
+            r.active_t.at[pl.ds(number * (chunk // unit), chunk // unit)],
             r.active_sem.at[slot],
         )
 
@@ -560,7 +560,7 @@
         active, slope = gelu_and_slope(hidden)
         active_low = active.astype(jnp.bfloat16)
         r.s_active[:, columns] = active_low
-        r.s_active_t[slot] = active_low.T
+        r.s_active_t[slot] = active_low.T.reshape(chunk // unit, unit, length)
         active_copy(number, slot).start()
         r.s_slope[slot] = slope.astype(jnp.bfloat16)
         slope_copy(number, slot).start()
@@ -604,6 +604,7 @@
     length, width = row_in.shape
     padded = -(-length // LANES) * LANES
     hidden_units = shards[2].shape[1]
+    unit = shards[3].shape[0]
     chunk = 256
     routes = len(GATHER_ORDERS)
     hops = 2 * hops_before(GATHER_ORDERS[0], 3) + 1
@@ -620,7 +621,7 @@
         shape((length, width), low),
         shape((length, width), jnp.float32),
         shape((length, width), low),
-        shape((hidden_units, length), low),
+        shape((hidden_units // unit, unit, length), low),
         shape((length, hidden_units), low),
         shape((length, width), jnp.float32),
         shape((8, width), jnp.float32),
@@ -642,7 +643,7 @@
         pltpu.VMEM((length, width), low),
         pltpu.VMEM((length, hidden_units), low),
         pltpu.VMEM((2, length, chunk), low),
-        pltpu.VMEM((2, chunk, length), low),
+        pltpu.VMEM((2, chunk // unit, unit, length), low),
         pltpu.VMEM((length, width), jnp.float32),
         pltpu.VMEM((8, width), jnp.float32),
         pltpu.VMEM((1, hidden_units), jnp.float32),
@@ -657,16 +658,17 @@
         pltpu.SemaphoreType.DMA((9 + padded // LANES,)),
     ]
     across = jnp.pad(segments, (0, padded - length))[None, :]
+    marks = segments * 2 + (validity > 0).astype(jnp.int32)
     return pl.pallas_call(
         functools.partial(forward_kernel, waves, starts),
-        in_specs=[anywhere] * 7 + [in_vmem] * 3,
+        in_specs=[anywhere] * 7 + [in_vmem] * 2,
         out_specs=[anywhere] * len(outs),
         out_shape=outs,
         scratch_shapes=scratch,
         compiler_params=pltpu.CompilerParams(
             collective_id=collective, has_side_effects=True, vmem_limit_bytes=VMEM_BYTES
         ),
-    )(*shards, small, row_in, buckets, segments[:, None], validity[:, None], across)
+    )(*shards, small, row_in, buckets, marks[:, None], across)
 
 
 def small_block(device, vec_bias, norm_gain, bias_hidden, rel_tables):
@@ -810,7 +812,7 @@
     return [first, second, third, fourth, fifth]
 
 
-SCATTER_AFTER = (0, 1, 3, 5, 7)
+SCATTER_AFTER = (0, 1, 4, 7, 10)
 
 
 def step_runner(steps, starts):
@@ -997,7 +999,7 @@
         )
 
     steps = [None] * len(waves)
-    for number in range(down_waves, len(waves)):
+    for number in range(len(waves)):
         steps[number] = steps_of(number, r.s_stage.at[number % 2])
     communicate, last = step_runner(steps, list(range(len(waves))))
     stores = []
@@ -1014,10 +1016,8 @@
     nothing = jnp.zeros((8, width), jnp.float32)
 
     def feed_phase(
-        s_second, s_cot, s_out, s_active, s_low_rows, s_low_t, s_wd, s_wi, s_slope, s_stage_down
+        s_second, s_cot, s_out, s_active, s_low_rows, s_low_t, s_wd, s_wi, s_slope
     ):
-        for number in range(down_waves):
-            steps[number] = steps_of(number, s_stage_down.at[number % 2])
         load(r.second_sum, s_second, 2)
         load(r.cotangent, s_cot, 3)
         load(r.active_t, s_active, 4)
@@ -1071,15 +1071,15 @@
                 ].astype(jnp.bfloat16)
 
         for number in range(down_waves):
-            columns = slice(waves[number][3][0], waves[number][3][-1])
-
-            def one_down(plane, carry, number=number, columns=columns):
-                size = len(spots) * rows_each
-                units = pl.ds(pl.multiple_of(plane * size, size), size)
-                product = dot_plain(s_active[units, :], r.s_low[:, columns])
-                to_stage(
-                    s_stage_down.at[number % 2], plane, product, rows_each, slice(None)
+            first_row = waves[number][1]
+
+            def one_down(plane, carry, number=number, first_row=first_row):
+                group = pl.ds(plane * len(spots), len(spots))
+                units = s_active[group, first_row : first_row + rows_each, :]
+                product = dot_plain(
+                    units.reshape(len(spots) * rows_each, length), r.s_low[...]
                 )
+                to_stage(r.s_stage.at[number % 2], plane, product, rows_each, slice(None))
                 return carry
 
             lax.fori_loop(0, DIMS[0], one_down, 0)
@@ -1127,13 +1127,12 @@
         pltpu.VMEM((length, width), full32),
         pltpu.VMEM((length, width), bf),
         pltpu.VMEM((length, width), bf),
-        pltpu.VMEM((hidden_units, length), bf),
+        pltpu.VMEM(r.active_t.shape, bf),
         pltpu.VMEM((length, width), bf),
         pltpu.VMEM((width, length), bf),
         pltpu.VMEM((2, chunk, width), bf),
         pltpu.VMEM((2, width, chunk), bf),
         pltpu.VMEM((2, length, chunk), bf),
-        pltpu.VMEM((2,) + DIMS + (2, waves[0][2], waves[0][3][-1] - waves[0][3][0]), bf),
     )
     now = len(waves)
     pairs = H // 2
@@ -1275,7 +1274,8 @@
     bf, full32 = jnp.bfloat16, jnp.float32
     shape = jax.ShapeDtypeStruct
     anywhere = pl.BlockSpec(memory_space=pl.ANY)
-    waves = even_waves(1, down_shape, 2, (1, 1, 0)) + weight_waves(0, in_shape[0], in_shape[1], in_shape[0], 8)
+    waves = weight_waves(1, down_shape[0], down_shape[1], in_shape[0], 8)
+    waves += weight_waves(0, in_shape[0], in_shape[1], in_shape[0], 8)
     outs = [
         shape(in_shape, full32),
         shape(down_shape, full32),
@@ -1663,7 +1663,7 @@
     waves += weight_waves(1, w_out.shape[0], w_out.shape[1], w_out.shape[0], 8)
     waves += weight_waves(2, w_in.shape[0], w_in.shape[1], w_in.shape[0], 8)
     waves += even_waves(3, w_down.shape, 2, (1, 1, 0))
-    starts = [(number, 1) if number < early else (number, LAG) for number in range(len(waves))]
+    starts = [(number, 1) if number < early else (number - 1, LAG) for number in range(len(waves))]
     return waves, starts
 
 

time: 365 us -> 338 us (0.926)
  Pallas kernels: 341 us -> 317 us
    pallas_call x1, Pallas kernels: 110 us -> 97 us  [feed_backward(): pl.pallas_call(functools.partial(feed_backward_kernel, waves), in_specs=[...]
    pallas_call x1, Pallas kernels: 83.3 us -> 76.7 us  [last_backward(): pl.pallas_call(functools.partial(last_backward_kernel, waves), in_specs=[...]
    pallas_call x1, Pallas kernels: 148 us -> 143 us  [forward_all(): pl.pallas_call(functools.partial(forward_kernel, waves, starts), in_specs...]
where the time goes in v3:
time: 338 us; the launch traced here: 335 us
  Pallas kernels  317 us (94%)
  local copies, waits for them, and re-layouts  13.3 us (4%)
  other arithmetic  3.71 us (1%)
    pallas_call x1, Pallas kernels, forward_all(): pl.pallas_call(functools.partial(forward_kernel, waves, starts), in_specs...  143 us
    pallas_call x1, Pallas kernels, feed_backward(): pl.pallas_call(functools.partial(feed_backward_kernel, waves), in_specs=[...  97 us
    pallas_call x1, Pallas kernels, last_backward(): pl.pallas_call(functools.partial(last_backward_kernel, waves), in_specs=[...  76.7 us

profile of v3, /device:TPU:0, one launch (start us, length us, event | category | flops | bytes accessed | tf_op | source)
XLA Modules:
  0.0 334.8 jit_solution(9300373647110137864)
XLA Ops:
  0.7 0.7 pad_maximum_fusion
  1.4 0.7 reshape.90
  2.2 0.1 slice.20
  2.3 0.1 slice.19
  2.4 0.2 convolution_convert_fusion
  2.7 1.3 fusion.3.refs_4_
  4.0 0.7 fusion.15
  4.7 0.9 convert_reduce_fusion.refs_10_
  5.6 0.6 broadcast_in_dim.25.refs_8_
  6.2 0.9 copy.25.refs_7_
  7.1 142.9 %shard_map.204 = (bf16[4,2,2,2,32,3072]{5,4,3,2,1,0:T(8,128)(2,1)}, bf16[4,2,2,2,32,1024]{5,4,3,2,1,0:T(8,128)(2,1)}, bf16[4,2,2,2,32,4096]{5,4,3,2,1,0:T(8,128)...) custom-call(bf16[32,3072]{1,0:T(8,128)(2,1)} %refs_0_.1, ...), custom_call_target="tpu_custom_call" | custom-call | tf_op jit(solution)/shard_map/pallas_call | solution.py:662
  150.0 97.0 %shard_map.205 = (f32[32,4096]{1,0:T(8,128)}, f32[128,1024]{1,0:T(8,128)}, bf16[576,1024]{1,0:T(8,128)(2,1)}, f32[576,1024]{1,0:T(8,128)}, bf16[576,1024]{1,0:T(...) custom-call(bf16[1024,4096]{1,0:T(8,128)(2,1)} %bitcast.18, ...), custom_call_target="tpu_custom_call" | custom-call | tf_op jit(solution)/shard_map/pallas_call | solution.py:1305
  247.0 76.7 %shard_map.206 = (f32[32,3072]{1,0:T(8,128)}, f32[32,1024]{1,0:T(8,128)}, f32[32,128]{1,0:T(8,128)}, f32[576,1024]{1,0:T(8,128)}) custom-call(bf16[576,1024]{1,0:T(8,128)(2,1)} %bitcast.22, bf16[576,3072]{1,0:T(8,128)(2,1)} %get-tuple-element.53.refs_1_, bf16[1024,3072]{1,0:T(8,128)(2,1)} %bitcast.20, bf16[1024,640]{1,0:T(8,128)(2,1)} %get-tuple-element.55.refs_3_, ...), custom_call_target="tpu_custom_call" | custom-call | tf_op jit(solution)/shard_map/pallas_call | solution.py:1632
  323.7 1.3 slice_bitcast_fusion
  325.0 1.3 constant_dynamic-slice_fusion
  326.4 0.7 slice.24
  327.2 0.6 reshape.95
  327.9 1.2 slice.22
  329.1 1.0 copy.33
  330.2 1.4 copy.34
  331.6 0.7 copy.35
  332.3 0.7 copy.36
  333.0 0.8 copy.37
  333.8 0.8 copy.38
  (20 shorter events, 0.3 us)
Async XLA Ops:
  246.9 82.2 %copy-start.1 = (bf16[576,1024]{1,0:T(8,128)(2,1)S(1)}, bf16[576,1024]{1,0:T(8,128)(2,1)}, u32[]{:S(2)}) copy-start(bf16[576,1024]{1,0:T(8,128)(2,1)} %get-tuple-element.52) | copy-start | bytes 3538948
  323.7 6.5 %copy-start = (f32[576,1024]{1,0:T(8,128)S(1)}, f32[576,1024]{1,0:T(8,128)}, u32[]{:S(2)}) copy-start(f32[576,1024]{1,0:T(8,128)} %get-tuple-element.62) | copy-start | bytes 7077892
  330.2 1.4 copy-start.4
  330.2 2.2 copy-start.5
  330.2 2.8 copy-start.3
  331.6 2.2 copy-start.2

commit v4 on v3

--- a/solution.py
+++ b/solution.py
@@ -1663,7 +1663,7 @@
     waves += weight_waves(1, w_out.shape[0], w_out.shape[1], w_out.shape[0], 8)
     waves += weight_waves(2, w_in.shape[0], w_in.shape[1], w_in.shape[0], 8)
     waves += even_waves(3, w_down.shape, 2, (1, 1, 0))
-    starts = [(number, 1) if number < early else (number - 1, LAG) for number in range(len(waves))]
+    starts = [(number, 1) if number < early else (number - 2, LAG) for number in range(len(waves))]
     return waves, starts
 
 

time: 338 us -> 342 us (1.012)
  Pallas kernels: 317 us -> 321 us
    pallas_call x1, Pallas kernels: 143 us -> 146 us  [forward_all(): pl.pallas_call(functools.partial(forward_kernel, waves, starts), in_specs...]
where the time goes in v4:
time: 342 us; the launch traced here: 339 us
  Pallas kernels  321 us (94%)
  local copies, waits for them, and re-layouts  13.3 us (4%)
  other arithmetic  3.71 us (1%)
    pallas_call x1, Pallas kernels, forward_all(): pl.pallas_call(functools.partial(forward_kernel, waves, starts), in_specs...  146 us
    pallas_call x1, Pallas kernels, feed_backward(): pl.pallas_call(functools.partial(feed_backward_kernel, waves), in_specs=[...  96.6 us
    pallas_call x1, Pallas kernels, last_backward(): pl.pallas_call(functools.partial(last_backward_kernel, waves), in_specs=[...  77.7 us

profile of v4, /device:TPU:0, one launch (start us, length us, event | category | flops | bytes accessed | tf_op | source)
XLA Modules:
  0.0 338.8 jit_solution(9545929078302379841)
XLA Ops:
  0.7 0.7 pad_maximum_fusion
  1.4 0.7 reshape.90
  2.2 0.1 slice.20
  2.3 0.1 slice.19
  2.4 0.2 convolution_convert_fusion
  2.7 1.3 fusion.3.refs_4_
  4.0 0.7 fusion.15
  4.7 0.9 convert_reduce_fusion.refs_10_
  5.6 0.6 broadcast_in_dim.25.refs_8_
  6.2 0.9 copy.25.refs_7_
  7.1 146.3 %shard_map.204 = (bf16[4,2,2,2,32,3072]{5,4,3,2,1,0:T(8,128)(2,1)}, bf16[4,2,2,2,32,1024]{5,4,3,2,1,0:T(8,128)(2,1)}, bf16[4,2,2,2,32,4096]{5,4,3,2,1,0:T(8,128)...) custom-call(bf16[32,3072]{1,0:T(8,128)(2,1)} %refs_0_.1, ...), custom_call_target="tpu_custom_call" | custom-call | tf_op jit(solution)/shard_map/pallas_call | solution.py:662
  153.4 96.6 %shard_map.205 = (f32[32,4096]{1,0:T(8,128)}, f32[128,1024]{1,0:T(8,128)}, bf16[576,1024]{1,0:T(8,128)(2,1)}, f32[576,1024]{1,0:T(8,128)}, bf16[576,1024]{1,0:T(...) custom-call(bf16[1024,4096]{1,0:T(8,128)(2,1)} %bitcast.18, ...), custom_call_target="tpu_custom_call" | custom-call | tf_op jit(solution)/shard_map/pallas_call | solution.py:1305
  250.0 77.7 %shard_map.206 = (f32[32,3072]{1,0:T(8,128)}, f32[32,1024]{1,0:T(8,128)}, f32[32,128]{1,0:T(8,128)}, f32[576,1024]{1,0:T(8,128)}) custom-call(bf16[576,1024]{1,0:T(8,128)(2,1)} %bitcast.22, bf16[576,3072]{1,0:T(8,128)(2,1)} %get-tuple-element.53.refs_1_, bf16[1024,3072]{1,0:T(8,128)(2,1)} %bitcast.20, bf16[1024,640]{1,0:T(8,128)(2,1)} %get-tuple-element.55.refs_3_, ...), custom_call_target="tpu_custom_call" | custom-call | tf_op jit(solution)/shard_map/pallas_call | solution.py:1632
  327.7 1.3 slice_bitcast_fusion
  329.0 1.3 constant_dynamic-slice_fusion
  330.4 0.7 slice.24
  331.2 0.6 reshape.95
  331.9 1.2 slice.22
  333.1 1.0 copy.33
  334.2 1.4 copy.34
  335.6 0.7 copy.35
  336.3 0.7 copy.36
  337.0 0.8 copy.37
  337.8 0.8 copy.38
  (20 shorter events, 0.3 us)
Async XLA Ops:
  250.0 83.1 %copy-start.1 = (bf16[576,1024]{1,0:T(8,128)(2,1)S(1)}, bf16[576,1024]{1,0:T(8,128)(2,1)}, u32[]{:S(2)}) copy-start(bf16[576,1024]{1,0:T(8,128)(2,1)} %get-tuple-element.52) | copy-start | bytes 3538948
  327.7 6.5 %copy-start = (f32[576,1024]{1,0:T(8,128)S(1)}, f32[576,1024]{1,0:T(8,128)}, u32[]{:S(2)}) copy-start(f32[576,1024]{1,0:T(8,128)} %get-tuple-element.62) | copy-start | bytes 7077892
  334.2 1.4 copy-start.4
  334.2 2.2 copy-start.5
  334.2 2.8 copy-start.3
  335.6 2.2 copy-start.2
